TPU v7x, 32 devices: a whole 2x2x4 slice. The times are simulated.
32 devices in a mesh: dp: 16 (over z, y, core), mp: 2 (over x).
Axes of the slice: x: 2, y: 2, z: 4, core: 2. Of those that a mesh axis runs over, the one named last changes fastest.
Arguments:
- tokens_in: bfloat16 [16384, 768], P('dp'), may hold values from -6 to 6
- segments: int32 [16384], P('dp'), may hold values from 0 to 1, as said below
- gains_first: float32 [2, 768], replicated, may hold values from 0.1 to 1.9
- qkv_first: bfloat16 [768, 3, 768], P(None, None, 'mp'), may hold values from -0.21875 to 0.21875
- proj_first: bfloat16 [768, 768], P('mp'), may hold values from -2.5 to 2.5
- up_first: bfloat16 [768, 3072], P(None, 'mp'), may hold values from -0.21875 to 0.21875
- down_first: bfloat16 [3072, 768], P('mp'), may hold values from -0.109375 to 0.109375
- pass_embed: bfloat16 [2, 768], replicated, may hold values from -3 to 3
- gains_second: float32 [2, 768], replicated, may hold values from 0.1 to 1.9
- qkv_second: bfloat16 [768, 3, 768], P(None, None, 'mp'), may hold values from -0.21875 to 0.21875
- proj_second: bfloat16 [768, 768], P('mp'), may hold values from -2.5 to 2.5
- up_second: bfloat16 [768, 3072], P(None, 'mp'), may hold values from -0.21875 to 0.21875
- down_second: bfloat16 [3072, 768], P('mp'), may hold values from -0.109375 to 0.109375
- cotangent: bfloat16 [16384, 768], P('dp')
Outputs:
- output: bfloat16 [16384, 768], P('dp')
- grad_input: float32 [16384, 768], P('dp')
- grad_gains_first: float32 [2, 768], P(None, 'dp')
- grad_qkv_first: float32 [768, 3, 768], P('dp', None, 'mp')
- grad_proj_first: float32 [768, 768], P('mp', 'dp')
- grad_up_first: float32 [768, 3072], P('dp', 'mp')
- grad_down_first: float32 [3072, 768], P('mp', 'dp')
- grad_pass_embed: float32 [2, 768], P(None, 'dp')
- grad_gains_second: float32 [2, 768], P(None, 'dp')
- grad_qkv_second: float32 [768, 3, 768], P('dp', None, 'mp')
- grad_proj_second: float32 [768, 768], P('mp', 'dp')
- grad_up_second: float32 [768, 3072], P('dp', 'mp')
- grad_down_second: float32 [3072, 768], P('mp', 'dp')
Inputs may be any that keep to these rules, and one draw needn't show every extreme that they name: `segments`: each run of 1024 rows consists of aligned blocks of 1024 rows; half of all blocks hold one item of 1024 rows and the others hold items of 512 rows each; some run holds short items only. Numbers count the items of one run from 0 in the order of rows.
All inputs are finite; a program needn't handle non-finite values.
Results may differ from a plain program's by a relative error of at most 0.03.
Values may be sent and summed in bfloat16 or wider, within the bound.
No kernel may reach another device: no remote copies, remote signals or barrier semaphores. Data moves between devices by JAX's collectives and lax.ppermute only.
A program may use at most 256 MiB of HBM per device.

v0:
```python
import jax
import jax.numpy as jnp
from jax import lax
from jax.sharding import PartitionSpec as P

HEAD_DIM = 64
PASSES = 2


EPSILON = 1e-05
NEG_FILL = -1e30


def layer_norm(values, gain_row):
    centered = values - jnp.mean(values, axis=-1, keepdims=True)
    variance = jnp.mean(centered * centered, axis=-1, keepdims=True)
    return centered * lax.rsqrt(variance + EPSILON) * gain_row


def exact_gelu(values):
    return jax.nn.gelu(values, approximate=False)


def block_mask(segments, row_start, count, key_limit):
    query_rows = row_start + lax.broadcasted_iota(jnp.int32, (count, key_limit), 0)
    key_rows = lax.broadcasted_iota(jnp.int32, (count, key_limit), 1)
    same_item = segments[row_start : row_start + count][:, None] == segments[:key_limit][None, :]
    return jnp.logical_and(same_item, key_rows <= query_rows)


def masked_scores(query_heads, key_heads, segments, row_start, block_rows):
    key_limit = row_start + block_rows
    scaling = query_heads.shape[2] ** (-0.5)
    scores = (
        jnp.einsum(
            "qhd,khd->hqk",
            query_heads[row_start:key_limit],
            key_heads[:key_limit],
            preferred_element_type=jnp.float32,
        )
        * scaling
    )
    allowed = block_mask(segments, row_start, block_rows, key_limit)
    return jnp.where(allowed[None], scores, NEG_FILL)


def attention_forward(query_heads, key_heads, value_heads, segments):
    total_rows = query_heads.shape[0]
    block_rows = min(512, total_rows)
    outputs = []
    log_sums = []
    for row_start in range(0, total_rows, block_rows):
        key_limit = row_start + block_rows
        scores = masked_scores(query_heads, key_heads, segments, row_start, block_rows)
        largest = jnp.max(scores, axis=-1, keepdims=True)
        weights = jnp.exp(scores - largest)
        totals = jnp.sum(weights, axis=-1, keepdims=True)
        probs_low = (weights / totals).astype(jnp.bfloat16)
        outputs.append(
            jnp.einsum(
                "hqk,khd->qhd",
                probs_low,
                value_heads[:key_limit],
                preferred_element_type=jnp.float32,
            )
        )
        log_sums.append(largest + jnp.log(totals))
    return (jnp.concatenate(outputs, axis=0), jnp.concatenate(log_sums, axis=1))


def attention_backward(query_heads, key_heads, value_heads, segments, log_sums, grad_att):
    total_rows = query_heads.shape[0]
    block_rows = min(512, total_rows)
    scaling = query_heads.shape[2] ** (-0.5)
    query_parts = []
    grad_key = jnp.zeros(key_heads.shape, jnp.float32)
    grad_value = jnp.zeros(value_heads.shape, jnp.float32)
    for row_start in range(0, total_rows, block_rows):
        key_limit = row_start + block_rows
        scores = masked_scores(query_heads, key_heads, segments, row_start, block_rows)
        probs = jnp.exp(scores - log_sums[:, row_start:key_limit])
        probs_low = probs.astype(jnp.bfloat16)
        grad_block = grad_att[row_start:key_limit]
        grad_probs = jnp.einsum(
            "qhd,khd->hqk", grad_block, value_heads[:key_limit], preferred_element_type=jnp.float32
        )
        row_delta = jnp.sum(probs * grad_probs, axis=-1, keepdims=True)
        grad_scores = (probs * (grad_probs - row_delta)).astype(jnp.bfloat16)
        query_parts.append(
            jnp.einsum(
                "hqk,khd->qhd",
                grad_scores,
                key_heads[:key_limit],
                preferred_element_type=jnp.float32,
            )
            * scaling
        )
        grad_key = grad_key.at[:key_limit].add(
            jnp.einsum(
                "hqk,qhd->khd",
                grad_scores,
                query_heads[row_start:key_limit],
                preferred_element_type=jnp.float32,
            )
            * scaling
        )
        grad_value = grad_value.at[:key_limit].add(
            jnp.einsum("hqk,qhd->khd", probs_low, grad_block, preferred_element_type=jnp.float32)
        )
    return (jnp.concatenate(query_parts, axis=0), grad_key, grad_value)


def layer_forward(residual, segments, gain_pair, qkv_weight, proj_weight, up_weight, down_weight):
    total_rows = residual.shape[0]
    local_width = qkv_weight.shape[2]
    head_count = local_width // HEAD_DIM
    normed_first = layer_norm(residual, gain_pair[0]).astype(jnp.bfloat16)
    projected = jnp.einsum(
        "rd,dcn->rcn", normed_first, qkv_weight, preferred_element_type=jnp.float32
    ).astype(jnp.bfloat16)
    head_split = projected.reshape(total_rows, 3, head_count, HEAD_DIM)
    attended, log_sums = attention_forward(
        head_split[:, 0], head_split[:, 1], head_split[:, 2], segments
    )
    attended_low = attended.reshape(total_rows, local_width).astype(jnp.bfloat16)
    partial_attn = jnp.dot(attended_low, proj_weight, preferred_element_type=jnp.float32)
    middle = residual + lax.psum(partial_attn.astype(jnp.bfloat16), "mp").astype(jnp.float32)
    normed_second = layer_norm(middle, gain_pair[1]).astype(jnp.bfloat16)
    pre_act = jnp.dot(normed_second, up_weight, preferred_element_type=jnp.float32)
    hidden_low = exact_gelu(pre_act).astype(jnp.bfloat16)
    partial_mlp = jnp.dot(hidden_low, down_weight, preferred_element_type=jnp.float32)
    output = middle + lax.psum(partial_mlp.astype(jnp.bfloat16), "mp").astype(jnp.float32)
    stored = (
        residual,
        normed_first,
        projected,
        log_sums,
        attended_low,
        middle,
        normed_second,
        pre_act,
        hidden_low,
    )
    return (output, stored)


def layer_backward(
    grad_out, segments, gain_pair, qkv_weight, proj_weight, up_weight, down_weight, stored
):
    (
        residual,
        normed_first,
        projected,
        log_sums,
        attended_low,
        middle,
        normed_second,
        stored_pre,
        hidden_low,
    ) = stored
    total_rows, local_width = attended_low.shape
    head_count = local_width // HEAD_DIM
    grad_low = grad_out.astype(jnp.bfloat16)
    grad_down = jnp.einsum("rf,rd->fd", hidden_low, grad_low, preferred_element_type=jnp.float32)
    grad_hidden = jnp.einsum("rd,fd->rf", grad_low, down_weight, preferred_element_type=jnp.float32)
    unused_value, gelu_back = jax.vjp(exact_gelu, stored_pre)
    grad_pre = gelu_back(grad_hidden)[0].astype(jnp.bfloat16)
    grad_up = jnp.einsum("rd,rf->df", normed_second, grad_pre, preferred_element_type=jnp.float32)
    partial_norm = jnp.einsum("rf,df->rd", grad_pre, up_weight, preferred_element_type=jnp.float32)
    grad_normed = lax.psum(partial_norm.astype(jnp.bfloat16), "mp").astype(jnp.float32)
    unused_norm, norm_back = jax.vjp(layer_norm, middle, gain_pair[1])
    grad_mid_part, grad_gain_second = norm_back(grad_normed)
    grad_middle = grad_out + grad_mid_part
    middle_low = grad_middle.astype(jnp.bfloat16)
    grad_proj = jnp.einsum(
        "rn,rd->nd", attended_low, middle_low, preferred_element_type=jnp.float32
    )
    grad_att = jnp.einsum("rd,nd->rn", middle_low, proj_weight, preferred_element_type=jnp.float32)
    grad_att = grad_att.astype(jnp.bfloat16).reshape(total_rows, head_count, HEAD_DIM)
    head_split = projected.reshape(total_rows, 3, head_count, HEAD_DIM)
    grad_query, grad_key, grad_value = attention_backward(
        head_split[:, 0], head_split[:, 1], head_split[:, 2], segments, log_sums, grad_att
    )
    grad_proj_in = jnp.stack([grad_query, grad_key, grad_value], axis=1)
    grad_proj_in = grad_proj_in.reshape(total_rows, 3, local_width).astype(jnp.bfloat16)
    grad_qkv = jnp.einsum(
        "rd,rcn->dcn", normed_first, grad_proj_in, preferred_element_type=jnp.float32
    )
    partial_first = jnp.einsum(
        "rcn,dcn->rd", grad_proj_in, qkv_weight, preferred_element_type=jnp.float32
    )
    grad_first = lax.psum(partial_first.astype(jnp.bfloat16), "mp").astype(jnp.float32)
    unused_first, first_back = jax.vjp(layer_norm, residual, gain_pair[0])
    grad_res_part, grad_gain_first = first_back(grad_first)
    grad_input = grad_middle + grad_res_part
    grad_gains = jnp.stack([grad_gain_first, grad_gain_second])
    return (grad_input, grad_qkv, grad_proj, grad_up, grad_down, grad_gains)


def per_device(
    tokens_in,
    segments,
    gains_first,
    qkv_first,
    proj_first,
    up_first,
    down_first,
    pass_embed,
    gains_second,
    qkv_second,
    proj_second,
    up_second,
    down_second,
    cotangent,
):
    total_rows = tokens_in.shape[0]
    residual = tokens_in.astype(jnp.float32)
    between, stored_first = layer_forward(
        residual, segments, gains_first, qkv_first, proj_first, up_first, down_first
    )
    parity = lax.broadcasted_iota(jnp.int32, (total_rows, PASSES), 0) % PASSES
    choices_row = lax.broadcasted_iota(jnp.int32, (total_rows, PASSES), 1)
    one_hot = (parity == choices_row).astype(jnp.float32)
    pass_table = pass_embed.astype(jnp.float32)
    joined = between + jnp.dot(
        one_hot, pass_table, precision=lax.Precision.HIGHEST, preferred_element_type=jnp.float32
    )
    top, stored_second = layer_forward(
        joined, segments, gains_second, qkv_second, proj_second, up_second, down_second
    )
    output = top.astype(jnp.bfloat16)
    second_grads = layer_backward(
        cotangent.astype(jnp.float32),
        segments,
        gains_second,
        qkv_second,
        proj_second,
        up_second,
        down_second,
        stored_second,
    )
    grad_joined = second_grads[0]
    grad_table = jnp.einsum(
        "rp,rd->pd",
        one_hot,
        grad_joined,
        precision=lax.Precision.HIGHEST,
        preferred_element_type=jnp.float32,
    )
    small_second = jnp.concatenate([second_grads[5], grad_table], axis=0)
    first_grads = layer_backward(
        grad_joined,
        segments,
        gains_first,
        qkv_first,
        proj_first,
        up_first,
        down_first,
        stored_first,
    )
    rows_all = (
        lax.psum_scatter(first_grads[1], "dp", scatter_dimension=0, tiled=True),
        lax.psum_scatter(first_grads[3], "dp", scatter_dimension=0, tiled=True),
        lax.psum_scatter(second_grads[1], "dp", scatter_dimension=0, tiled=True),
        lax.psum_scatter(second_grads[3], "dp", scatter_dimension=0, tiled=True),
    )
    cols_all = (
        lax.psum_scatter(first_grads[2], "dp", scatter_dimension=1, tiled=True),
        lax.psum_scatter(first_grads[4], "dp", scatter_dimension=1, tiled=True),
        lax.psum_scatter(first_grads[5], "dp", scatter_dimension=1, tiled=True),
        lax.psum_scatter(second_grads[2], "dp", scatter_dimension=1, tiled=True),
        lax.psum_scatter(second_grads[4], "dp", scatter_dimension=1, tiled=True),
        lax.psum_scatter(small_second, "dp", scatter_dimension=1, tiled=True),
    )
    summed_first = (rows_all[0], rows_all[1], cols_all[0], cols_all[1], cols_all[2])
    summed_second = (rows_all[2], rows_all[3], cols_all[3], cols_all[4], cols_all[5])
    small_summed = summed_second[4]
    return (
        output,
        first_grads[0],
        summed_first[4],
        summed_first[0],
        summed_first[2],
        summed_first[1],
        summed_first[3],
        small_summed[2:],
        small_summed[:2],
        summed_second[0],
        summed_second[2],
        summed_second[1],
        summed_second[3],
    )


def solution(mesh):
    placed = (
        P("dp", None),
        P("dp"),
        P(),
        P(None, None, "mp"),
        P("mp", None),
        P(None, "mp"),
        P("mp", None),
        P(),
        P(),
        P(None, None, "mp"),
        P("mp", None),
        P(None, "mp"),
        P("mp", None),
        P("dp", None),
    )
    return jax.shard_map(
        per_device,
        mesh=mesh,
        in_specs=placed,
        out_specs=(
            P("dp", None),
            P("dp", None),
            P(None, "dp"),
            P("dp", None, "mp"),
            P("mp", "dp"),
            P("dp", "mp"),
            P("mp", "dp"),
            P(None, "dp"),
            P(None, "dp"),
            P("dp", None, "mp"),
            P("mp", "dp"),
            P("dp", "mp"),
            P("mp", "dp"),
        ),
        check_vma=False,
    )
```

profile of v0, /device:TPU:0, one launch (start us, length us, event | category | flops | bytes accessed | tf_op | source)
XLA Modules:
  0.0 1374.3 jit_solution(5621557861621091775)
XLA Ops:
  33.7 54.3 %all-reduce.13.cloned.1.call-done = bf16[1024,768]{1,0:T(8,128)(2,1)} async-done(((bf16[1024,768]{1,0:T(8,128)(2,1)}), bf16[1024,768]{1,0:T(8,128)(2,1)}) %all-reduce.13.cloned.1.call-update) | async-done | bytes 1572880 | tf_op jit(solution)/shard_map/psum | solution.py:127
  92.2 17.6 %multiply_convert_fusion.5 = (bf16[1024,1536]{1,0:T(8,128)(2,1)S(1)}, f32[1024,1536]{1,0:T(8,128)}, f32[1024,1536]{1,0:T(8,128)}) fusion(bf16[768,1536]{1,0:T(8,128)(2,1)S(1)} %copy-done, bf16[1024,768]{1,0:T(8,128)(2,1)S(1)} %copy-done.14, bf16[1024,768]{1,0:T(8,128)(2,1)S(1)} %copy-done.4, f32[768]{0:T(1024)S(1)} %get-tuple-element.151, ...), kind=kOutput, calls=%fused_computation.48 | convolution fusion | flops 2523660288 | bytes 21244928 | tf_op jit(solution)/shard_map/dot_general | solution.py:129
  111.6 3.7 convolution_convert_fusion.7
  115.4 51.5 %all-reduce.15.cloned.1.call-done = bf16[1024,768]{1,0:T(8,128)(2,1)} async-done(((bf16[1024,768]{1,0:T(8,128)(2,1)}), bf16[1024,768]{1,0:T(8,128)(2,1)}) %all-reduce.15.cloned.1.call-update) | async-done | bytes 1572880 | tf_op jit(solution)/shard_map/psum | solution.py:132
  166.9 3.7 fusion.152
  191.0 51.4 %all-reduce.17.cloned.1.call-done = bf16[1024,768]{1,0:T(8,128)(2,1)} async-done(((bf16[1024,768]{1,0:T(8,128)(2,1)}), bf16[1024,768]{1,0:T(8,128)(2,1)}) %all-reduce.17.cloned.1.call-update) | async-done | bytes 1572880 | tf_op jit(solution)/shard_map/psum | solution.py:127
  250.8 18.1 %add_convert_fusion.1 = (bf16[1024,1536]{1,0:T(8,128)(2,1)S(1)}, f32[1024,1536]{1,0:T(8,128)}) fusion(f32[1024,1536]{1,0:T(8,128)S(1)} %fusion.139, bf16[1024,768]{1,0:T(8,128)(2,1)S(1)} %copy-done.34, bf16[1536,768]{1,0:T(8,128)(2,1)S(1)} %copy-done.116), kind=kOutput, calls=%fused_computation.31 | convolution fusion | flops 2529165312 | bytes 19660800 | tf_op jit(solution)/shard_map/rd,fd->rf/dot_general | solution.py:165
  270.5 3.7 convolution_convert_fusion.5
  274.9 51.0 %all-reduce.19.cloned.1.call-done = bf16[1024,768]{1,0:T(8,128)(2,1)} async-done(((bf16[1024,768]{1,0:T(8,128)(2,1)}), bf16[1024,768]{1,0:T(8,128)(2,1)}) %all-reduce.19.cloned.1.call-update) | async-done | bytes 1572880 | tf_op jit(solution)/shard_map/psum | solution.py:170
  325.9 4.4 fusion.44
  338.5 4.7 multiply_reduce_fusion.3
  343.2 6.4 multiply_convert_fusion.3
  353.0 3.9 fusion.80
  356.9 6.9 multiply_reduce_fusion.1
  367.4 9.9 multiply_convert_fusion.1
  385.1 5.6 bitcast_convert_fusion.1
  392.0 50.3 %all-reduce.21.cloned.1.call-done = bf16[1024,768]{1,0:T(8,128)(2,1)} async-done(((bf16[1024,768]{1,0:T(8,128)(2,1)}), bf16[1024,768]{1,0:T(8,128)(2,1)}) %all-reduce.21.cloned.1.call-update) | async-done | bytes 1572880 | tf_op jit(solution)/shard_map/psum | solution.py:192
  450.2 8.3 add_convert_fusion
  460.1 3.8 convolution_convert_fusion.4
  464.0 6.3 multiply_convert_fusion.4
  472.1 3.8 convolution_convert_fusion.6
  475.9 39.7 %all-reduce.23.cloned.1.call-done = bf16[1024,768]{1,0:T(8,128)(2,1)} async-done(((bf16[1024,768]{1,0:T(8,128)(2,1)}), bf16[1024,768]{1,0:T(8,128)(2,1)}) %all-reduce.23.cloned.1.call-update) | async-done | bytes 1572880 | tf_op jit(solution)/shard_map/psum | solution.py:170
  515.6 3.6 fusion.41
  528.3 4.6 multiply_reduce_fusion.2
  532.9 6.5 multiply_convert_fusion.2
  542.8 3.9 fusion.79
  546.7 6.8 multiply_reduce_fusion
  557.3 9.5 multiply_convert_fusion
  574.6 5.6 bitcast_convert_fusion
  585.4 81.0 %all-reduce.25.cloned.1.call-done = (bf16[1024,768]{1,0:T(8,128)(2,1)}, bf16[1024,768]{1,0:T(8,128)(2,1)}) async-done(((bf16[1024,768]{1,0:T(8,128)(2,1)}, bf16[1024,768]{1,0:T(8,128)(2,1)}), (bf16[1024,768]{1,0:T(8,128)(2,1)}, bf16[1024,768]{1,0:T(8,128)(2,1)})) %all-reduce.25.cloned.1.call-update) | async-done | bytes 3145744 | tf_op jit(solution)/shard_map/psum | solution.py:132
  672.4 3.7 fusion.155
  676.2 4.0 fusion.100
  680.6 6.8 fusion.99
  687.5 7.2 fusion.156
  695.4 7.9 fusion.138
  704.5 6.1 fusion.98
  710.8 7.9 fusion.140
  718.8 7.7 fusion.103
  728.6 4.0 add_convert_fusion.2
  735.9 48.1 %reduce-scatter.31.cloned.1.call-done = f32[48,2]{1,0:T(8,128)} async-done(((f32[768,2]{1,0:T(8,128)}), f32[48,2]{1,0:T(8,128)}) %reduce-scatter.31.cloned.1.call-update) | async-done | bytes 400
  785.4 60.3 %reduce-scatter.25.cloned.1.call-done = f32[384,48]{0,1:T(8,128)} async-done(((f32[384,768]{0,1:T(8,128)}), f32[384,48]{0,1:T(8,128)}) %reduce-scatter.25.cloned.1.call-update) | async-done | bytes 73744 | tf_op jit(solution)/shard_map/reduce_scatter | solution.py:271
  845.7 61.8 %reduce-scatter.17.cloned.1.call-done = f32[384,48]{0,1:T(8,128)} async-done(((f32[384,768]{0,1:T(8,128)}), f32[384,48]{0,1:T(8,128)}) %reduce-scatter.17.cloned.1.call-update) | async-done | bytes 73744 | tf_op jit(solution)/shard_map/reduce_scatter | solution.py:268
  907.5 71.9 %reduce-scatter.23.cloned.1.call-done = f32[48,3,384]{2,0,1:T(8,128)} async-done(((f32[768,3,384]{2,0,1:T(8,128)}), f32[48,3,384]{2,0,1:T(8,128)}) %reduce-scatter.23.cloned.1.call-update) | async-done | bytes 221200 | tf_op jit(solution)/shard_map/reduce_scatter | solution.py:264
  979.3 79.3 %reduce-scatter.29.cloned.1.call-done = f32[1536,48]{0,1:T(8,128)} async-done(((f32[1536,768]{0,1:T(8,128)}), f32[1536,48]{0,1:T(8,128)}) %reduce-scatter.29.cloned.1.call-update) | async-done | bytes 294928 | tf_op jit(solution)/shard_map/reduce_scatter | solution.py:272
  1058.6 78.9 %reduce-scatter.27.cloned.1.call-done = f32[48,1536]{1,0:T(8,128)} async-done(((f32[768,1536]{1,0:T(8,128)}), f32[48,1536]{1,0:T(8,128)}) %reduce-scatter.27.cloned.1.call-update) | async-done | bytes 294928 | tf_op jit(solution)/shard_map/reduce_scatter | solution.py:265
  1137.5 71.9 %reduce-scatter.15.cloned.1.call-done = f32[48,3,384]{2,0,1:T(8,128)} async-done(((f32[768,3,384]{2,0,1:T(8,128)}), f32[48,3,384]{2,0,1:T(8,128)}) %reduce-scatter.15.cloned.1.call-update) | async-done | bytes 221200 | tf_op jit(solution)/shard_map/reduce_scatter | solution.py:262
  1209.4 79.3 %reduce-scatter.19.cloned.1.call-done = f32[48,1536]{1,0:T(8,128)} async-done(((f32[768,1536]{1,0:T(8,128)}), f32[48,1536]{1,0:T(8,128)}) %reduce-scatter.19.cloned.1.call-update) | async-done | bytes 294928 | tf_op jit(solution)/shard_map/reduce_scatter | solution.py:263
  1288.6 78.9 %reduce-scatter.21.cloned.1.call-done = f32[1536,48]{0,1:T(8,128)} async-done(((f32[1536,768]{0,1:T(8,128)}), f32[1536,48]{0,1:T(8,128)}) %reduce-scatter.21.cloned.1.call-update) | async-done | bytes 294928 | tf_op jit(solution)/shard_map/reduce_scatter | solution.py:269
  (406 shorter events, 142.7 us)
Async XLA Ops:
  7.2 85.0 %copy-start = (bf16[768,1536]{1,0:T(8,128)(2,1)S(1)}, bf16[768,1536]{1,0:T(8,128)(2,1)}, u32[]{:S(2)}) copy-start(bf16[768,1536]{1,0:T(8,128)(2,1)} %param.43) | copy-start | bytes 7077892
  7.2 80.8 %all-reduce.13.cloned.1.call-start = ((), (), s32[]{:S(2)}) async-start(), calls=%async_computation.10 | async-start | bytes 3145728 | tf_op jit(solution)/shard_map/psum | solution.py:127
  11.9 80.3 %copy-start.56 = (f32[768]{0:T(1024)}, f32[768]{0:T(1024)S(1)}, u32[]{:S(2)}) copy-start(f32[768]{0:T(1024)S(1)} %get-tuple-element.151) | copy-start | bytes 9220
  14.5 11.3 copy-start.26
  33.7 133.2 %all-reduce.15.cloned.1.call-start = ((), (), s32[]{:S(2)}) async-start(), calls=%async_computation.11 | async-start | bytes 3145728 | tf_op jit(solution)/shard_map/psum | solution.py:132
  90.9 19.0 %copy-start.54 = (f32[1024]{0:T(1024)}, f32[1024]{0:T(1024)S(1)}, u32[]{:S(2)}) copy-start(f32[1024]{0:T(1024)S(1)} %broadcast_multiply_fusion.2) | copy-start | bytes 12292
  92.2 17.6 %copy-start.58 = (f32[1024]{0:T(1024)}, f32[1024]{0:T(1024)S(1)}, u32[]{:S(2)}) copy-start(f32[1024]{0:T(1024)S(1)} %fusion.127) | copy-start | bytes 12292
  92.2 19.3 %copy-start.114 = (bf16[1536,768]{1,0:T(8,128)(2,1)S(1)}, bf16[1536,768]{1,0:T(8,128)(2,1)}, u32[]{:S(2)}) copy-start(bf16[1536,768]{1,0:T(8,128)(2,1)} %param.44) | copy-start | bytes 7077892
  111.6 55.3 %copy-start.112 = (bf16[2,768]{1,0:T(2,128)(2,1)S(1)}, bf16[2,768]{1,0:T(2,128)(2,1)}, u32[]{:S(2)}) copy-start(bf16[2,768]{1,0:T(2,128)(2,1)} %param.45) | copy-start | bytes 9220
  115.3 127.2 %all-reduce.17.cloned.1.call-start = ((), (), s32[]{:S(2)}) async-start(), calls=%async_computation.12 | async-start | bytes 3145728 | tf_op jit(solution)/shard_map/psum | solution.py:127
  115.3 55.3 %copy-start.110 = (pred[1024]{0:T(1024)(128)(4,1)}, pred[1024]{0:T(1024)(128)(4,1)S(1)}, u32[]{:S(2)}) copy-start(pred[1024]{0:T(1024)(128)(4,1)S(1)} %fusion.125) | copy-start | bytes 3076
  115.3 55.3 %copy-start.92 = (s32[1024]{0:T(1024)}, s32[1024]{0:T(1024)S(1)}, u32[]{:S(2)}) copy-start(s32[1024]{0:T(1024)S(1)} %fusion.122) | copy-start | bytes 12292
  115.4 55.3 %copy-start.94 = (s32[1024]{0:T(1024)}, s32[1024]{0:T(1024)S(1)}, u32[]{:S(2)}) copy-start(s32[1024]{0:T(1024)S(1)} %iota_and_fusion) | copy-start | bytes 12292
  115.4 55.9 %copy-start.82 = (f32[768]{0:T(1024)}, f32[768]{0:T(1024)S(1)}, u32[]{:S(2)}) copy-start(f32[768]{0:T(1024)S(1)} %get-tuple-element.150) | copy-start | bytes 9220
  115.4 214.8 %copy-start.84 = (f32[768]{0:T(1024)}, f32[768]{0:T(1024)S(1)}, u32[]{:S(2)}) copy-start(f32[768]{0:T(1024)S(1)} %get-tuple-element.149) | copy-start | bytes 9220
  190.8 135.1 %all-reduce.19.cloned.1.call-start = ((), (), s32[]{:S(2)}) async-start(), calls=%async_computation.13 | async-start | bytes 3145728 | tf_op jit(solution)/shard_map/psum | solution.py:170
  245.2 85.1 %copy-start.70 = (f32[1024]{0:T(1024)}, f32[1024]{0:T(1024)S(1)}, u32[]{:S(2)}) copy-start(f32[1024]{0:T(1024)S(1)} %broadcast_multiply_fusion) | copy-start | bytes 12292
  245.7 84.6 %copy-start.86 = (f32[1024]{0:T(1024)}, f32[1024]{0:T(1024)S(1)}, u32[]{:S(2)}) copy-start(f32[1024]{0:T(1024)S(1)} %fusion.129) | copy-start | bytes 12292
  250.7 18.1 %copy-start.33 = (f32[1024,1536]{1,0:T(8,128)}, f32[1024,1536]{1,0:T(8,128)S(1)}, u32[]{:S(2)}) copy-start(f32[1024,1536]{1,0:T(8,128)S(1)} %fusion.139) | copy-start | bytes 18874372
  274.2 168.1 %all-reduce.21.cloned.1.call-start = ((), (), s32[]{:S(2)}) async-start(), calls=%async_computation.14 | async-start | bytes 3145728 | tf_op jit(solution)/shard_map/psum | solution.py:192
  343.2 13.7 %slice-start.3 = ((s8[12582912]{0:T(1024)(128)(4,1)}), s8[4194304]{0:T(1024)(128)(4,1)S(1)}, s32[]{:S(2)}) async-start(s8[12582912]{0:T(1024)(128)(4,1)} %bitcast.196), calls=%async_computation.30 | async-start | bytes 8388608
  343.2 13.7 %slice-start.4 = ((s8[12582912]{0:T(1024)(128)(4,1)}), s8[4194304]{0:T(1024)(128)(4,1)S(1)}, s32[]{:S(2)}) async-start(s8[12582912]{0:T(1024)(128)(4,1)} %bitcast.196), calls=%async_computation.31 | async-start | bytes 8388608
  385.0 57.3 %copy-start.69 = (f32[1024]{0:T(1024)S(1)}, f32[1024]{0:T(1024)}, u32[]{:S(2)}) copy-start(f32[1024]{0:T(1024)} %copy-done.68) | copy-start | bytes 12292
  385.0 57.3 %copy-start.83 = (f32[768]{0:T(1024)S(1)}, f32[768]{0:T(1024)}, u32[]{:S(2)}) copy-start(f32[768]{0:T(1024)} %copy-done.82) | copy-start | bytes 9220
  390.7 54.9 %copy-start.101 = (f32[1024]{0:T(1024)S(1)}, f32[1024]{0:T(1024)}, u32[]{:S(2)}) copy-start(f32[1024]{0:T(1024)} %copy-done.100) | copy-start | bytes 12292
  390.7 55.0 %copy-start.91 = (f32[1024]{0:T(1024)S(1)}, f32[1024]{0:T(1024)}, u32[]{:S(2)}) copy-start(f32[1024]{0:T(1024)} %copy-done.90) | copy-start | bytes 12292
  390.7 124.9 %all-reduce.23.cloned.1.call-start = ((), (), s32[]{:S(2)}) async-start(), calls=%async_computation.15 | async-start | bytes 3145728 | tf_op jit(solution)/shard_map/psum | solution.py:170
  463.9 202.5 %all-reduce.25.cloned.1.call-start = ((), (), s32[]{:S(2)}) async-start(), calls=%async_computation.26 | async-start | bytes 6291456 | tf_op jit(solution)/shard_map/psum | solution.py:132
  472.1 43.5 %copy-start.55 = (f32[1024]{0:T(1024)S(1)}, f32[1024]{0:T(1024)}, u32[]{:S(2)}) copy-start(f32[1024]{0:T(1024)} %copy-done.54) | copy-start | bytes 12292
  472.1 43.5 %copy-start.57 = (f32[768]{0:T(1024)S(1)}, f32[768]{0:T(1024)}, u32[]{:S(2)}) copy-start(f32[768]{0:T(1024)} %copy-done.56) | copy-start | bytes 9220
  475.9 43.2 %copy-start.99 = (f32[1024]{0:T(1024)S(1)}, f32[1024]{0:T(1024)}, u32[]{:S(2)}) copy-start(f32[1024]{0:T(1024)} %copy-done.98) | copy-start | bytes 12292
  475.9 43.3 %copy-start.59 = (f32[1024]{0:T(1024)S(1)}, f32[1024]{0:T(1024)}, u32[]{:S(2)}) copy-start(f32[1024]{0:T(1024)} %copy-done.58) | copy-start | bytes 12292
  532.9 13.8 %slice-start = ((s8[12582912]{0:T(1024)(128)(4,1)}), s8[4194304]{0:T(1024)(128)(4,1)S(1)}, s32[]{:S(2)}) async-start(s8[12582912]{0:T(1024)(128)(4,1)} %bitcast.194), calls=%async_computation.27 | async-start | bytes 8388608
  532.9 13.8 %slice-start.1 = ((s8[12582912]{0:T(1024)(128)(4,1)}), s8[4194304]{0:T(1024)(128)(4,1)S(1)}, s32[]{:S(2)}) async-start(s8[12582912]{0:T(1024)(128)(4,1)} %bitcast.194), calls=%async_computation.28 | async-start | bytes 8388608
  580.3 86.2 %copy-start.67 = (f32[1024]{0:T(1024)S(1)}, f32[1024]{0:T(1024)}, u32[]{:S(2)}) copy-start(f32[1024]{0:T(1024)} %copy-done.66) | copy-start | bytes 12292
  580.3 86.2 %copy-start.75 = (f32[768]{0:T(1024)S(1)}, f32[768]{0:T(1024)}, u32[]{:S(2)}) copy-start(f32[768]{0:T(1024)} %copy-done.74) | copy-start | bytes 9220
  580.3 146.1 %reduce-scatter.33.cloned.1.call-start = ((), (), s32[]{:S(2)}) async-start(), calls=%async_computation.25 | async-start | bytes 417792
  581.0 88.4 %copy-start.97 = (f32[1024]{0:T(1024)S(1)}, f32[1024]{0:T(1024)}, u32[]{:S(2)}) copy-start(f32[1024]{0:T(1024)} %copy-done.96) | copy-start | bytes 12292
  581.0 88.4 %copy-start.89 = (f32[1024]{0:T(1024)S(1)}, f32[1024]{0:T(1024)}, u32[]{:S(2)}) copy-start(f32[1024]{0:T(1024)} %copy-done.88) | copy-start | bytes 12292
  585.3 198.7 %reduce-scatter.31.cloned.1.call-start = ((), (), s32[]{:S(2)}) async-start(), calls=%async_computation.24 | async-start | bytes 417792
  672.4 173.3 %reduce-scatter.25.cloned.1.call-start = ((), (), s32[]{:S(2)}) async-start(), calls=%async_computation.21 | async-start | bytes 1253376 | tf_op jit(solution)/shard_map/reduce_scatter | solution.py:271
  676.1 231.3 %reduce-scatter.17.cloned.1.call-start = ((), (), s32[]{:S(2)}) async-start(), calls=%async_computation.17 | async-start | bytes 1253376 | tf_op jit(solution)/shard_map/reduce_scatter | solution.py:268
  680.2 299.1 %reduce-scatter.23.cloned.1.call-start = ((), (), s32[]{:S(2)}) async-start(), calls=%async_computation.20 | async-start | bytes 3760128 | tf_op jit(solution)/shard_map/reduce_scatter | solution.py:264
  687.5 371.1 %reduce-scatter.29.cloned.1.call-start = ((), (), s32[]{:S(2)}) async-start(), calls=%async_computation.23 | async-start | bytes 5013504 | tf_op jit(solution)/shard_map/reduce_scatter | solution.py:272
  694.8 442.8 %reduce-scatter.27.cloned.1.call-start = ((), (), s32[]{:S(2)}) async-start(), calls=%async_computation.22 | async-start | bytes 5013504 | tf_op jit(solution)/shard_map/reduce_scatter | solution.py:265
  703.4 506.0 %reduce-scatter.15.cloned.1.call-start = ((), (), s32[]{:S(2)}) async-start(), calls=%async_computation.16 | async-start | bytes 3760128 | tf_op jit(solution)/shard_map/reduce_scatter | solution.py:262
  710.6 578.1 %reduce-scatter.19.cloned.1.call-start = ((), (), s32[]{:S(2)}) async-start(), calls=%async_computation.18 | async-start | bytes 5013504 | tf_op jit(solution)/shard_map/reduce_scatter | solution.py:263
  718.7 648.8 %reduce-scatter.21.cloned.1.call-start = ((), (), s32[]{:S(2)}) async-start(), calls=%async_computation.19 | async-start | bytes 5013504 | tf_op jit(solution)/shard_map/reduce_scatter | solution.py:269
  (103 other events, 366.3 us)
Sparse Core Ops, SparseCore 0:
  33.8 54.1 all-reduce.12
  115.4 51.4 all-reduce.14
  190.9 51.4 all-reduce.16
  274.4 51.4 all-reduce.18
  390.8 51.4 all-reduce.20
  464.1 51.4 all-reduce.22
  580.4 85.9 all-reduce.24
  670.3 55.5 reduce-scatter.32
  729.4 54.5 reduce-scatter.30
  788.5 57.1 reduce-scatter.24
  850.3 57.0 reduce-scatter.16
  912.3 67.0 reduce-scatter.22
  984.3 74.3 reduce-scatter.28
  1062.9 74.5 reduce-scatter.26
  1142.3 67.0 reduce-scatter.14
  1214.2 74.4 reduce-scatter.18
  1292.9 74.5 reduce-scatter.20
where the time goes:
time: 1380 us; the launch traced here: 1370 us
  waiting for transfers between devices  1010 us (73%)
  matrix products  211 us (15%)
  other arithmetic  95 us (7%)
  local copies, waits for them, and re-layouts  41.5 us (3%)
  between operations  15.8 us (1%)
    psum x2, waiting for transfers between devices, layer_forward(): lax.psum(partial_mlp.astype(jnp.bfloat16), 'mp').astype(jnp.float32)  133 us
    psum x2, waiting for transfers between devices, layer_forward(): lax.psum(partial_attn.astype(jnp.bfloat16), 'mp').astype(jnp.float32)  106 us
    psum x2, waiting for transfers between devices, layer_backward(): lax.psum(partial_norm.astype(jnp.bfloat16), 'mp').astype(jnp.float32)  90.6 us
    reduce_scatter x1, waiting for transfers between devices, per_device(): lax.psum_scatter(second_grads[4], 'dp', scatter_dimension=1, tiled=True)  79.3 us
    reduce_scatter x1, waiting for transfers between devices, per_device(): lax.psum_scatter(first_grads[3], 'dp', scatter_dimension=0, tiled=True)  79.3 us
    reduce_scatter x1, waiting for transfers between devices, per_device(): lax.psum_scatter(second_grads[3], 'dp', scatter_dimension=0, tiled=True)  78.9 us
    reduce_scatter x1, waiting for transfers between devices, per_device(): lax.psum_scatter(first_grads[4], 'dp', scatter_dimension=1, tiled=True)  78.9 us
    reduce_scatter x1, waiting for transfers between devices, per_device(): lax.psum_scatter(second_grads[1], 'dp', scatter_dimension=0, tiled=True)  71.9 us
  transfers between devices with their start and end apart: 17, of which 16 were waited for; matrix products, arithmetic and copies ran while one was open for 6% of the time, Pallas kernels for 0%

commit v1 on v0

--- a/solution.py
+++ b/solution.py
@@ -9,6 +9,97 @@
 
 EPSILON = 1e-05
 NEG_FILL = -1e30
+
+
+BOTH = ("dp", "mp")
+
+
+def moves(pick):
+    n_dp, n_mp = lax.axis_size("dp"), lax.axis_size("mp")
+    pairs = []
+    for dp in range(n_dp):
+        for mp in range(n_mp):
+            source = pick(dp, mp)
+            if source is not None:
+                pairs.append((source[0] * n_mp + source[1], dp * n_mp + mp))
+    return pairs
+
+
+def from_core(values):
+    return lax.ppermute(values, BOTH, moves(lambda dp, mp: (dp ^ 1, mp)))
+
+
+def pair_sum(partial):
+    low = partial.astype(jnp.bfloat16)
+    return low.astype(jnp.float32) + from_core(low).astype(jnp.float32)
+
+
+def own_run(values, same):
+    other = lax.ppermute(
+        values, BOTH, moves(lambda dp, mp: (dp ^ 1, mp) if (dp & 1) != mp else None)
+    )
+    return jnp.where(same, values, other)
+
+
+def own_half(weight):
+    return lax.ppermute(
+        weight, BOTH, moves(lambda dp, mp: (dp, mp) if (dp & 1) == mp else (dp ^ 1, 1 - mp))
+    )
+
+
+def to_mesh_rows(values, same):
+    other = lax.ppermute(
+        values, BOTH, moves(lambda dp, mp: (dp ^ 1, 1 - mp) if (dp & 1) != mp else None)
+    )
+    return jnp.where(same, values, other)
+
+
+def bit_of(index, bit):
+    return (index >> bit) & 1
+
+
+def fold(parts, bit, axis, dtype):
+    mine = bit_of(lax.axis_index("dp"), bit)
+    send = lax.dynamic_index_in_dim(parts, 1 - mine, axis, keepdims=False)
+    keep = lax.dynamic_index_in_dim(parts, mine, axis, keepdims=False)
+    recv = lax.ppermute(send, "dp", [(i, i ^ (1 << bit)) for i in range(lax.axis_size("dp"))])
+    return (keep.astype(jnp.float32) + recv.astype(jnp.float32)).astype(dtype)
+
+
+def cross(parts, axis, same, dtype):
+    core = lax.axis_index("dp") & 1
+    mine = lax.dynamic_index_in_dim(parts, core, axis, keepdims=False)
+    away = lax.dynamic_index_in_dim(parts, 1 - core, axis, keepdims=False)
+    straight = lax.ppermute(
+        mine, BOTH, moves(lambda dp, mp: (dp, 1 - mp) if (dp & 1) == mp else None)
+    )
+    local = lax.ppermute(
+        away, BOTH, moves(lambda dp, mp: (dp ^ 1, mp) if (dp & 1) != mp else None)
+    )
+    diagonal = lax.ppermute(
+        away, BOTH, moves(lambda dp, mp: (dp ^ 1, 1 - mp) if (dp & 1) != mp else None)
+    )
+    first = jnp.where(same, mine, local).astype(jnp.float32)
+    second = jnp.where(same, straight, diagonal).astype(jnp.float32)
+    return (first + second).astype(dtype)
+
+
+def reduce_rows(grad, same, cross_first):
+    bits = lax.axis_size("dp").bit_length() - 1
+    rows, columns = grad.shape
+    parts = grad.astype(jnp.bfloat16).reshape((2,) * bits + (rows >> bits, columns))
+    axes = list(range(bits - 1, -1, -1))
+    order = list(range(1, bits))
+    if cross_first:
+        parts = cross(parts, axes.index(0), same, jnp.bfloat16)
+        axes.remove(0)
+    for bit in order:
+        last = cross_first and bit == order[-1]
+        parts = fold(parts, bit, axes.index(bit), jnp.float32 if last else jnp.bfloat16)
+        axes.remove(bit)
+    if not cross_first:
+        parts = cross(parts, 0, same, jnp.float32)
+    return parts
 
 
 def layer_norm(values, gain_row):
@@ -124,12 +215,12 @@
     )
     attended_low = attended.reshape(total_rows, local_width).astype(jnp.bfloat16)
     partial_attn = jnp.dot(attended_low, proj_weight, preferred_element_type=jnp.float32)
-    middle = residual + lax.psum(partial_attn.astype(jnp.bfloat16), "mp").astype(jnp.float32)
+    middle = residual + pair_sum(partial_attn)
     normed_second = layer_norm(middle, gain_pair[1]).astype(jnp.bfloat16)
     pre_act = jnp.dot(normed_second, up_weight, preferred_element_type=jnp.float32)
     hidden_low = exact_gelu(pre_act).astype(jnp.bfloat16)
     partial_mlp = jnp.dot(hidden_low, down_weight, preferred_element_type=jnp.float32)
-    output = middle + lax.psum(partial_mlp.astype(jnp.bfloat16), "mp").astype(jnp.float32)
+    output = middle + pair_sum(partial_mlp)
     stored = (
         residual,
         normed_first,
@@ -161,19 +252,19 @@
     total_rows, local_width = attended_low.shape
     head_count = local_width // HEAD_DIM
     grad_low = grad_out.astype(jnp.bfloat16)
-    grad_down = jnp.einsum("rf,rd->fd", hidden_low, grad_low, preferred_element_type=jnp.float32)
+    grad_down = jnp.einsum("rf,rd->df", hidden_low, grad_low, preferred_element_type=jnp.float32)
     grad_hidden = jnp.einsum("rd,fd->rf", grad_low, down_weight, preferred_element_type=jnp.float32)
     unused_value, gelu_back = jax.vjp(exact_gelu, stored_pre)
     grad_pre = gelu_back(grad_hidden)[0].astype(jnp.bfloat16)
     grad_up = jnp.einsum("rd,rf->df", normed_second, grad_pre, preferred_element_type=jnp.float32)
     partial_norm = jnp.einsum("rf,df->rd", grad_pre, up_weight, preferred_element_type=jnp.float32)
-    grad_normed = lax.psum(partial_norm.astype(jnp.bfloat16), "mp").astype(jnp.float32)
+    grad_normed = pair_sum(partial_norm)
     unused_norm, norm_back = jax.vjp(layer_norm, middle, gain_pair[1])
     grad_mid_part, grad_gain_second = norm_back(grad_normed)
     grad_middle = grad_out + grad_mid_part
     middle_low = grad_middle.astype(jnp.bfloat16)
     grad_proj = jnp.einsum(
-        "rn,rd->nd", attended_low, middle_low, preferred_element_type=jnp.float32
+        "rn,rd->dn", attended_low, middle_low, preferred_element_type=jnp.float32
     )
     grad_att = jnp.einsum("rd,nd->rn", middle_low, proj_weight, preferred_element_type=jnp.float32)
     grad_att = grad_att.astype(jnp.bfloat16).reshape(total_rows, head_count, HEAD_DIM)
@@ -189,7 +280,7 @@
     partial_first = jnp.einsum(
         "rcn,dcn->rd", grad_proj_in, qkv_weight, preferred_element_type=jnp.float32
     )
-    grad_first = lax.psum(partial_first.astype(jnp.bfloat16), "mp").astype(jnp.float32)
+    grad_first = pair_sum(partial_first)
     unused_first, first_back = jax.vjp(layer_norm, residual, gain_pair[0])
     grad_res_part, grad_gain_first = first_back(grad_first)
     grad_input = grad_middle + grad_res_part
@@ -213,6 +304,19 @@
     down_second,
     cotangent,
 ):
+    core = lax.axis_index("dp") & 1
+    same = core == lax.axis_index("mp")
+    tokens_in = own_run(tokens_in, same)
+    segments = own_run(segments, same)
+    cotangent = own_run(cotangent, same)
+    qkv_first = own_half(qkv_first)
+    proj_first = own_half(proj_first)
+    up_first = own_half(up_first)
+    down_first = own_half(down_first)
+    qkv_second = own_half(qkv_second)
+    proj_second = own_half(proj_second)
+    up_second = own_half(up_second)
+    down_second = own_half(down_second)
     total_rows = tokens_in.shape[0]
     residual = tokens_in.astype(jnp.float32)
     between, stored_first = layer_forward(
@@ -228,7 +332,7 @@
     top, stored_second = layer_forward(
         joined, segments, gains_second, qkv_second, proj_second, up_second, down_second
     )
-    output = top.astype(jnp.bfloat16)
+    output = to_mesh_rows(top.astype(jnp.bfloat16), same)
     second_grads = layer_backward(
         cotangent.astype(jnp.float32),
         segments,
@@ -258,37 +362,32 @@
         down_first,
         stored_first,
     )
-    rows_all = (
-        lax.psum_scatter(first_grads[1], "dp", scatter_dimension=0, tiled=True),
-        lax.psum_scatter(first_grads[3], "dp", scatter_dimension=0, tiled=True),
-        lax.psum_scatter(second_grads[1], "dp", scatter_dimension=0, tiled=True),
-        lax.psum_scatter(second_grads[3], "dp", scatter_dimension=0, tiled=True),
-    )
-    cols_all = (
-        lax.psum_scatter(first_grads[2], "dp", scatter_dimension=1, tiled=True),
-        lax.psum_scatter(first_grads[4], "dp", scatter_dimension=1, tiled=True),
-        lax.psum_scatter(first_grads[5], "dp", scatter_dimension=1, tiled=True),
-        lax.psum_scatter(second_grads[2], "dp", scatter_dimension=1, tiled=True),
-        lax.psum_scatter(second_grads[4], "dp", scatter_dimension=1, tiled=True),
-        lax.psum_scatter(small_second, "dp", scatter_dimension=1, tiled=True),
-    )
-    summed_first = (rows_all[0], rows_all[1], cols_all[0], cols_all[1], cols_all[2])
-    summed_second = (rows_all[2], rows_all[3], cols_all[3], cols_all[4], cols_all[5])
-    small_summed = summed_second[4]
+    grad_input = to_mesh_rows(first_grads[0].astype(jnp.bfloat16), same).astype(jnp.float32)
+    small = lax.psum(jnp.concatenate([small_second, first_grads[5]], axis=0), BOTH) * 0.5
+    width = small.shape[1] // lax.axis_size("dp")
+    small = lax.dynamic_slice_in_dim(small, lax.axis_index("dp") * width, width, 1)
+
+    def rows_of(grads, cross_first):
+        grad_qkv, grad_proj, grad_up, grad_down = grads[1:5]
+        width = grad_proj.shape[1]
+        qkv = reduce_rows(grad_qkv.reshape(grad_qkv.shape[0], -1), same, cross_first)
+        return (
+            qkv.reshape(qkv.shape[0], 3, width),
+            reduce_rows(grad_proj, same, cross_first).T,
+            reduce_rows(grad_up, same, cross_first),
+            reduce_rows(grad_down, same, not cross_first).T,
+        )
+
+    second = rows_of(second_grads, True)
+    first = rows_of(first_grads, True)
     return (
         output,
-        first_grads[0],
-        summed_first[4],
-        summed_first[0],
-        summed_first[2],
-        summed_first[1],
-        summed_first[3],
-        small_summed[2:],
-        small_summed[:2],
-        summed_second[0],
-        summed_second[2],
-        summed_second[1],
-        summed_second[3],
+        grad_input,
+        small[4:],
+        *first,
+        small[2:4],
+        small[:2],
+        *second,
     )
 
 

time: 1380 us -> 744 us (0.54)
  waiting for transfers between devices: 1010 us -> 125 us
  starting transfers between devices: 1.46 us -> 205 us
  blocking collectives: 0 us -> 51.3 us
  matrix products: 211 us -> 192 us
  local copies, waits for them, and re-layouts: 41.5 us -> 57.4 us
    reduce_scatter x8 -> x0, waiting for transfers between devices: 582 us -> none  [the longest x1 79.3 us: per_device(): lax.psum_scatter(second_grads[4], 'dp', scatter_dimension=1, tiled=True)]
    psum x7 -> x0, waiting for transfers between devices: 379 us -> none  [the longest x2 133 us: layer_forward(): lax.psum(partial_mlp.astype(jnp.bfloat16), 'mp').astype(jnp.float32)]
    ppermute x0 -> x69, starting transfers between devices: none -> 205 us  [the longest x8 68.7 us: own_half(): lax.ppermute(weight, BOTH, moves(lambda dp, mp: (dp, mp) if dp & 1 == mp...]
    ppermute x0 -> x69, waiting for transfers between devices: none -> 125 us  [the longest x24 76.6 us: fold(): lax.ppermute(send, 'dp', [(i, i ^ 1 << bit) for i in range(lax.axis_size(...]
    psum x0 -> x1, blocking collectives: none -> 51.3 us  [per_device(): lax.psum(jnp.concatenate([small_second, first_grads[5]], axis=0), BOTH)]
    unnamed x19 -> x0, waiting for transfers between devices: 48.4 us -> none
    dot_general x4, matrix products: 22.5 us -> 8.46 us  [the longest x2 5.61 us: layer_backward(): jnp.einsum('rf,rd->df', hidden_low, grad_low, preferred_element_type=jnp....]
    unnamed x273 -> x242, local copies, waits for them, and re-layouts: 29.6 us -> 24.4 us
  transfers between devices with their start and end apart: 17 -> 69, of which waited for: 16 -> 22; matrix products, arithmetic and copies ran while one was open for 6% -> 40% of each run, Pallas kernels for 0% -> 0%
where the time goes in v1:
time: 744 us; the launch traced here: 732 us
  starting transfers between devices  205 us (28%)
  matrix products  192 us (26%)
  waiting for transfers between devices  125 us (17%)
  other arithmetic  97.1 us (13%)
  local copies, waits for them, and re-layouts  57.4 us (8%)
  blocking collectives  51.3 us (7%)
    ppermute x24, waiting for transfers between devices, fold(): lax.ppermute(send, 'dp', [(i, i ^ 1 << bit) for i in range(lax.axis_size(...  76.6 us
    ppermute x8, starting transfers between devices, own_half(): lax.ppermute(weight, BOTH, moves(lambda dp, mp: (dp, mp) if dp & 1 == mp...  68.7 us
    ppermute x8, starting transfers between devices, from_core(): return lax.ppermute(values, BOTH, moves(lambda dp, mp: (dp ^ 1, mp)))  61.8 us
    psum x1, blocking collectives, per_device(): lax.psum(jnp.concatenate([small_second, first_grads[5]], axis=0), BOTH)  51.3 us
    ppermute x8, waiting for transfers between devices, cross(): lax.ppermute(mine, BOTH, moves(lambda dp, mp: (dp, 1 - mp) if dp & 1 == m...  47.4 us
    convert_element_type x4, other arithmetic, attention_backward(): grad_scores = (probs * (grad_probs - row_delta)).astype(jnp.bfloat16)  29.2 us
    dot_general x2, matrix products, layer_backward(): jnp.einsum('rd,fd->rf', grad_low, down_weight, preferred_element_type=jnp...  28.6 us
    dot_general x4, matrix products, attention_backward(): jnp.einsum('qhd,khd->hqk', grad_block, value_heads[:key_limit], preferred...  25.5 us
  transfers between devices with their start and end apart: 69, of which 22 were waited for; matrix products, arithmetic and copies ran while one was open for 40% of the time, Pallas kernels for 0%

profile of v1, /device:TPU:0, one launch (start us, length us, event | category | flops | bytes accessed | tf_op | source)
XLA Modules:
  0.0 732.2 jit_solution(17869515271952036100)
XLA Ops:
  7.3 6.0 collective-permute-start.3
  15.5 14.8 %collective-permute-start.1 = (bf16[768,3,384]{0,2,1:T(8,128)(2,1)}, bf16[768,3,384]{0,2,1:T(8,128)(2,1)}, u32[]{:S(2)}, u32[]{:S(2)}) collective-permute-start(bf16[768,3,384]{0,2,1:T(8,128)(2,1)} %copy.64), channel_id=1, source_target_pairs={{0,0},{2,1},{1,2},{3,3},{4,4},{6,5},{5,6},{7,7},{8,8},{10,9},{9,10... | collective-permute-start | bytes 5308424 | tf_op jit(solution)/shard_map/ppermute | solution.py:45
  52.9 4.4 collective-permute-start.4
  62.0 18.8 %multiply_convert_fusion.5 = (bf16[1024,1536]{1,0:T(8,128)(2,1)S(1)}, f32[1024,1536]{1,0:T(8,128)}, f32[1024,1536]{1,0:T(8,128)}) fusion(bf16[768,1536]{1,0:T(8,128)(2,1)S(1)} %collective-permute-done.5, f32[1024,768]{0,1:T(8,128)S(1)} %get-tuple-element.192, f32[768]{0:T(1024)S(1)} %get-tuple-element.177, f32[1024]{0:T(1024)S(1)} %fusion.138, ...), kind=kOutput, calls=%fused_computation.48 | convolution fusion | flops 2521300992 | bytes 21244928 | tf_op jit(solution)/shard_map/dot_general | solution.py:220
  84.6 32.1 %collective-permute-start.7 = (bf16[1024,768]{0,1:T(8,128)(2,1)}, bf16[1024,768]{0,1:T(8,128)(2,1)}, u32[]{:S(2)}, u32[]{:S(2)}) collective-permute-start(bf16[1024,768]{0,1:T(8,128)(2,1)} %convolution_convert_fusion.13), channel_id=1, source_target_pairs={{2,0},{3,1},{0,2},{1,3},{6,4},{7,5},{4,6},{5,7},{10,8},{11,9},{8,1... | collective-permute-start | bytes 4718600 | tf_op jit(solution)/shard_map/ppermute | solution.py:29
  116.7 5.9 collective-permute-start.9
  158.5 11.7 %collective-permute-start.10 = (bf16[1024,768]{0,1:T(8,128)(2,1)}, bf16[1024,768]{0,1:T(8,128)(2,1)}, u32[]{:S(2)}, u32[]{:S(2)}) collective-permute-start(bf16[1024,768]{0,1:T(8,128)(2,1)} %convolution_convert_fusion.8), channel_id=1, source_target_pairs={{2,0},{3,1},{0,2},{1,3},{6,4},{7,5},{4,6},{5,7},{10,8},{11,9},{8,1... | collective-permute-start | bytes 4718600 | tf_op jit(solution)/shard_map/ppermute | solution.py:29
  170.2 19.2 %collective-permute-start.11 = (bf16[768,1536]{1,0:T(8,128)(2,1)}, bf16[768,1536]{1,0:T(8,128)(2,1)}, u32[]{:S(2)}, u32[]{:S(2)}) collective-permute-start(bf16[768,1536]{1,0:T(8,128)(2,1)} %param.49), channel_id=1, source_target_pairs={{0,0},{2,1},{1,2},{3,3},{4,4},{6,5},{5,6},{7,7},{8,8},{10,9},{9,10... | collective-permute-start | bytes 7077896 | tf_op jit(solution)/shard_map/ppermute | solution.py:45
  189.3 19.2 %collective-permute-start.12 = (bf16[1536,768]{1,0:T(8,128)(2,1)}, bf16[1536,768]{1,0:T(8,128)(2,1)}, u32[]{:S(2)}, u32[]{:S(2)}) collective-permute-start(bf16[1536,768]{1,0:T(8,128)(2,1)} %param.50), channel_id=1, source_target_pairs={{0,0},{2,1},{1,2},{3,3},{4,4},{6,5},{5,6},{7,7},{8,8},{10,9},{9,10... | collective-permute-start | bytes 7077896 | tf_op jit(solution)/shard_map/ppermute | solution.py:45
  215.3 4.5 fusion.145
  219.8 20.1 %add_convert_fusion.1 = (bf16[1024,1536]{1,0:T(8,128)(2,1)}, f32[1024,1536]{1,0:T(8,128)}) fusion(f32[1024,1536]{1,0:T(8,128)S(1)} %fusion.145, bf16[1024,768]{0,1:T(8,128)(2,1)S(1)} %broadcast_select_fusion, bf16[1536,768]{1,0:T(8,128)(2,1)} %collective-permute-done.12), kind=kOutput, calls=%fused_computation.31 | convolution fusion | flops 2529165312 | bytes 19660800 | tf_op jit(solution)/shard_map/rd,fd->rf/dot_general | solution.py:256
  248.2 4.3 convolution_convert_fusion.11
  252.5 5.9 collective-permute-start.16
  258.3 4.4 convolution_convert_fusion.12
  262.8 4.5 convolution_convert_fusion.1
  283.8 5.0 multiply_reduce_fusion.3
  288.7 5.8 multiply_convert_fusion.3
  301.4 8.0 %multiply_reduce_fusion.1 = (f32[6,512]{1,0:T(8,128)}, f32[6,512,1024]{2,1,0:T(8,128)}) fusion(f32[6,512,1024]{2,1,0:T(8,128)S(1)} %bitcast.399, f32[6,512]{1,0:T(8,128)S(1)} %copy-done.64, bf16[512,6,64]{0,2,1:T(8,128)(2,1)S(1)} %bitcast.430, bf16[1024,3,6,64]{0,3,2,1:T(8,128)(2,1)} %bitcast.421), kind=kOutput, calls=%fused_computation.4 | convolution fusion | flops 412087296 | bytes 26370048 | tf_op jit(solution)/shard_map/qhd,khd->hqk/dot_general | solution.py:175
  314.8 9.7 %multiply_convert_fusion.1 = bf16[6,512,1024]{2,1,0:T(8,128)(2,1)S(1)} fusion(f32[6,512,1024]{2,1,0:T(8,128)} %get-tuple-element.233, f32[6,512,1024]{2,1,0:T(8,128)} %copy-done.3, f32[6,512]{1,0:T(8,128)} %get-tuple-element.232, f32[6,512]{1,0:T(8,128)} %log_add_fusion.2), kind=kLoop, calls=%fused_computation.3 | loop fusion | flops 12582912 | bytes 31481856 | tf_op jit(solution)/shard_map/convert_element_type | solution.py:179
  337.7 4.3 copy.94
  342.0 4.6 bitcast_convert_fusion.1
  346.6 5.2 collective-permute-start.17
  359.4 9.8 %collective-permute-done.65 = bf16[2,48,1536]{2,1,0:T(8,128)(2,1)S(1)} collective-permute-done((bf16[2,48,1536]{2,1,0:T(8,128)(2,1)S(1)}, bf16[2,48,1536]{2,1,0:T(8,128)(2,1)S(1)}, u32[]{:S(2)}, u32[]{:S(2)}) %collective-permute-start.65) | collective-permute-done | bytes 294944 | tf_op jit(solution)/shard_map/ppermute | solution.py:65
  386.3 8.5 %add_convert_fusion = bf16[1024,1536]{1,0:T(8,128)(2,1)S(1)} fusion(f32[1024,1536]{1,0:T(8,128)} %get-tuple-element.190, f32[1024,1536]{1,0:T(8,128)} %get-tuple-element.225, bf16[1536,768]{1,0:T(8,128)(2,1)S(1)} %copy-done.102, f32[1024,768]{0,1:T(8,128)S(1)} %add_add_fusion.5), kind=kOutput, calls=%fused_computation.26 | convolution fusion | flops 2438725632 | bytes 21233664 | tf_op jit(solution)/shard_map/rd,fd->rf/dot_general | solution.py:256
  402.6 5.6 collective-permute-start.33
  422.8 5.4 convolution_convert_fusion.10
  430.3 9.5 %collective-permute-done.39 = bf16[2,2,2,48,1536]{4,3,2,1,0:T(8,128)(2,1)} collective-permute-done((bf16[2,2,2,48,1536]{4,3,2,1,0:T(8,128)(2,1)}, bf16[2,2,2,48,1536]{4,3,2,1,0:T(8,128)(2,1)}, u32[]{:S(2)}, u32[]{:S(2)}) %collective-permute-start.39) | collective-permute-done | bytes 1179680 | tf_op jit(solution)/shard_map/ppermute | solution.py:65
  449.6 9.8 %collective-permute-done.58 = bf16[2,2,2,48,1536]{4,3,0,1,2:T(8,128)(2,1)S(1)} collective-permute-done((bf16[2,2,2,48,1536]{4,3,0,1,2:T(8,128)(2,1)S(1)}, bf16[2,2,2,48,1536]{4,3,0,1,2:T(8,128)(2,1)S(1)}, u32[]{:S(2)}, u32[]{:S(2)}) %collective-permute-start.58) | collective-permute-done | bytes 1179680 | tf_op jit(solution)/shard_map/ppermute | solution.py:73
  477.4 4.9 multiply_reduce_fusion.2
  482.3 4.2 multiply_convert_fusion.2
  492.1 7.6 %multiply_reduce_fusion = (f32[6,512]{1,0:T(8,128)S(1)}, f32[6,512,1024]{2,1,0:T(8,128)}) fusion(f32[6,512,1024]{2,1,0:T(8,128)S(1)} %bitcast.397, f32[6,512]{1,0:T(8,128)S(1)} %copy-done.62, bf16[512,6,64]{0,2,1:T(8,128)(2,1)S(1)} %bitcast.432, bf16[1024,3,6,64]{0,3,2,1:T(8,128)(2,1)} %bitcast.411), kind=kOutput, calls=%fused_computation.1 | convolution fusion | flops 412087296 | bytes 26370048 | tf_op jit(solution)/shard_map/qhd,khd->hqk/dot_general | solution.py:175
  502.3 9.5 %multiply_convert_fusion = bf16[6,512,1024]{2,1,0:T(8,128)(2,1)S(1)} fusion(f32[6,512,1024]{2,1,0:T(8,128)} %get-tuple-element.237, f32[6,512,1024]{2,1,0:T(8,128)} %copy-done.2, f32[6,512]{1,0:T(8,128)S(1)} %get-tuple-element.236, f32[6,512]{1,0:T(8,128)S(1)} %copy-done.62), kind=kLoop, calls=%fused_computation | loop fusion | flops 12582912 | bytes 31481856 | tf_op jit(solution)/shard_map/convert_element_type | solution.py:179
  518.6 4.6 copy.87
  523.3 4.1 convolution_convert_fusion.5
  541.5 6.0 collective-permute-done.28
  552.5 11.4 %collective-permute-done.52 = bf16[2,2,2,48,384]{4,3,0,1,2:T(8,128)(2,1)S(1)} collective-permute-done((bf16[2,2,2,48,384]{4,3,0,1,2:T(8,128)(2,1)S(1)}, bf16[2,2,2,48,384]{4,3,0,1,2:T(8,128)(2,1)S(1)}, u32[]{:S(2)}, u32[]{:S(2)}) %collective-permute-start.52) | collective-permute-done | bytes 294944 | tf_op jit(solution)/shard_map/ppermute | solution.py:73
  567.1 4.8 collective-permute-done.30
  573.5 4.1 collective-permute-done.54
  581.4 6.2 collective-permute-done.37
  589.8 4.2 collective-permute-done.61
  599.2 4.4 collective-permute-done.32
  604.7 4.0 collective-permute-done.56
  609.6 9.0 %collective-permute-done.38 = bf16[48,1536]{1,0:T(8,128)(2,1)S(1)} collective-permute-done((bf16[48,1536]{1,0:T(8,128)(2,1)S(1)}, bf16[48,1536]{1,0:T(8,128)(2,1)S(1)}, u32[]{:S(2)}, u32[]{:S(2)}) %collective-permute-start.38) | collective-permute-done | bytes 147488 | tf_op jit(solution)/shard_map/ppermute | solution.py:65
  620.6 4.0 collective-permute-done.62
  627.3 4.3 collective-permute-done.43
  638.6 13.1 %collective-permute-done.46 = bf16[2,2,2,48,1152]{4,3,0,1,2:T(8,128)(2,1)S(1)} collective-permute-done((bf16[2,2,2,48,1152]{4,3,0,1,2:T(8,128)(2,1)S(1)}, bf16[2,2,2,48,1152]{4,3,0,1,2:T(8,128)(2,1)S(1)}, u32[]{:S(2)}, u32[]{:S(2)}) %collective-permute-start.46) | collective-permute-done | bytes 884768 | tf_op jit(solution)/shard_map/ppermute | solution.py:73
  654.2 9.1 %collective-permute-done.48 = bf16[2,2,48,1152]{3,2,0,1:T(8,128)(2,1)S(1)} collective-permute-done((bf16[2,2,48,1152]{3,2,0,1:T(8,128)(2,1)S(1)}, bf16[2,2,48,1152]{3,2,0,1:T(8,128)(2,1)S(1)}, u32[]{:S(2)}, u32[]{:S(2)}) %collective-permute-start.48) | collective-permute-done | bytes 442400 | tf_op jit(solution)/shard_map/ppermute | solution.py:65
  674.3 51.3 %psum.7 = f32[6,768]{1,0:T(8,128)S(1)} all-reduce(f32[6,768]{1,0:T(8,128)S(1)} %concatenate.43), channel_id=1, replica_groups=mesh['dp'=16,'mp'=2] {'dp','mp'}, use_global_device_ids=true, to_apply=%region_32.33 | all-reduce | flops 4608 | bytes 36864 | tf_op jit(solution)/shard_map/psum | solution.py:366
  (547 shorter events, 290.9 us)
Async XLA Ops:
  2.5 28.7 %collective-permute-start = (bf16[1024,768]{0,1:T(8,128)(2,1)S(1)}, bf16[1024,768]{0,1:T(8,128)(2,1)}, u32[]{:S(2)}, u32[]{:S(2)}) collective-permute-start(bf16[1024,768]{0,1:T(8,128)(2,1)S(1)} %copy.63), channel_id=1, source_target_pairs={{3,1},{0,2},{7,5},{4,6},{11,9},{8,10},{15,13},{12,14},{19,17},{16,... | collective-permute-start | bytes 4718600 | tf_op jit(solution)/shard_map/ppermute | solution.py:38
  6.0 24.3 %collective-permute-start.2 = (s32[1024]{0:T(1024)S(1)}, s32[1024]{0:T(1024)S(1)}, u32[]{:S(2)}, u32[]{:S(2)}) collective-permute-start(s32[1024]{0:T(1024)S(1)} %copy-done.97), channel_id=1, source_target_pairs={{3,1},{0,2},{7,5},{4,6},{11,9},{8,10},{15,13},{12,14},{19,17},{16,... | collective-permute-start | bytes 12296 | tf_op jit(solution)/shard_map/ppermute | solution.py:38
  7.3 42.6 %collective-permute-start.3 = (bf16[384,768]{1,0:T(8,128)(2,1)}, bf16[384,768]{1,0:T(8,128)(2,1)}, u32[]{:S(2)}, u32[]{:S(2)}) collective-permute-start(bf16[384,768]{1,0:T(8,128)(2,1)} %param.42), channel_id=1, source_target_pairs={{0,0},{2,1},{1,2},{3,3},{4,4},{6,5},{5,6},{7,7},{8,8},{10,9},{9,10... | collective-permute-start | bytes 1769480 | tf_op jit(solution)/shard_map/ppermute | solution.py:45
  15.5 17.0 %collective-permute-start.1 = (bf16[768,3,384]{0,2,1:T(8,128)(2,1)}, bf16[768,3,384]{0,2,1:T(8,128)(2,1)}, u32[]{:S(2)}, u32[]{:S(2)}) collective-permute-start(bf16[768,3,384]{0,2,1:T(8,128)(2,1)} %copy.64), channel_id=1, source_target_pairs={{0,0},{2,1},{1,2},{3,3},{4,4},{6,5},{5,6},{7,7},{8,8},{10,9},{9,10... | collective-permute-start | bytes 5308424 | tf_op jit(solution)/shard_map/ppermute | solution.py:45
  58.2 22.6 %collective-permute-start.6 = (bf16[1536,768]{1,0:T(8,128)(2,1)S(1)}, bf16[1536,768]{1,0:T(8,128)(2,1)S(1)}, u32[]{:S(2)}, u32[]{:S(2)}) collective-permute-start(bf16[1536,768]{1,0:T(8,128)(2,1)S(1)} %copy-done.99), channel_id=1, source_target_pairs={{0,0},{2,1},{1,2},{3,3},{4,4},{6,5},{5,6},{7,7},{8,8},{10,9},{9,10... | collective-permute-start | bytes 7077896 | tf_op jit(solution)/shard_map/ppermute | solution.py:45
  84.6 49.1 %collective-permute-start.7 = (bf16[1024,768]{0,1:T(8,128)(2,1)}, bf16[1024,768]{0,1:T(8,128)(2,1)}, u32[]{:S(2)}, u32[]{:S(2)}) collective-permute-start(bf16[1024,768]{0,1:T(8,128)(2,1)} %convolution_convert_fusion.13), channel_id=1, source_target_pairs={{2,0},{3,1},{0,2},{1,3},{6,4},{7,5},{4,6},{5,7},{10,8},{11,9},{8,1... | collective-permute-start | bytes 4718600 | tf_op jit(solution)/shard_map/ppermute | solution.py:29
  116.7 37.7 %collective-permute-start.9 = (bf16[384,768]{1,0:T(8,128)(2,1)}, bf16[384,768]{1,0:T(8,128)(2,1)}, u32[]{:S(2)}, u32[]{:S(2)}) collective-permute-start(bf16[384,768]{1,0:T(8,128)(2,1)} %param.48), channel_id=1, source_target_pairs={{0,0},{2,1},{1,2},{3,3},{4,4},{6,5},{5,6},{7,7},{8,8},{10,9},{9,10... | collective-permute-start | bytes 1769480 | tf_op jit(solution)/shard_map/ppermute | solution.py:45
  124.3 84.2 %collective-permute-start.15 = (bf16[1024,768]{0,1:T(8,128)(2,1)}, bf16[1024,768]{0,1:T(8,128)(2,1)}, u32[]{:S(2)}, u32[]{:S(2)}) collective-permute-start(bf16[1024,768]{0,1:T(8,128)(2,1)} %copy.72), channel_id=1, source_target_pairs={{3,1},{0,2},{7,5},{4,6},{11,9},{8,10},{15,13},{12,14},{19,17},{16,... | collective-permute-start | bytes 4718600 | tf_op jit(solution)/shard_map/ppermute | solution.py:38
  158.5 53.5 %collective-permute-start.10 = (bf16[1024,768]{0,1:T(8,128)(2,1)}, bf16[1024,768]{0,1:T(8,128)(2,1)}, u32[]{:S(2)}, u32[]{:S(2)}) collective-permute-start(bf16[1024,768]{0,1:T(8,128)(2,1)} %convolution_convert_fusion.8), channel_id=1, source_target_pairs={{2,0},{3,1},{0,2},{1,3},{6,4},{7,5},{4,6},{5,7},{10,8},{11,9},{8,1... | collective-permute-start | bytes 4718600 | tf_op jit(solution)/shard_map/ppermute | solution.py:29
  170.2 45.1 %collective-permute-start.11 = (bf16[768,1536]{1,0:T(8,128)(2,1)}, bf16[768,1536]{1,0:T(8,128)(2,1)}, u32[]{:S(2)}, u32[]{:S(2)}) collective-permute-start(bf16[768,1536]{1,0:T(8,128)(2,1)} %param.49), channel_id=1, source_target_pairs={{0,0},{2,1},{1,2},{3,3},{4,4},{6,5},{5,6},{7,7},{8,8},{10,9},{9,10... | collective-permute-start | bytes 7077896 | tf_op jit(solution)/shard_map/ppermute | solution.py:45
  189.3 30.5 %collective-permute-start.12 = (bf16[1536,768]{1,0:T(8,128)(2,1)}, bf16[1536,768]{1,0:T(8,128)(2,1)}, u32[]{:S(2)}, u32[]{:S(2)}) collective-permute-start(bf16[1536,768]{1,0:T(8,128)(2,1)} %param.50), channel_id=1, source_target_pairs={{0,0},{2,1},{1,2},{3,3},{4,4},{6,5},{5,6},{7,7},{8,8},{10,9},{9,10... | collective-permute-start | bytes 7077896 | tf_op jit(solution)/shard_map/ppermute | solution.py:45
  246.6 23.7 %collective-permute-start.63 = (bf16[2,2,2,48,1536]{4,3,2,1,0:T(8,128)(2,1)S(1)}, bf16[2,2,2,48,1536]{4,3,2,1,0:T(8,128)(2,1)S(1)}, u32[]{:S(2)}, u32[]{:S(2)}) collective-permute-start(bf16[2,2,2,48,1536]{4,3,2,1,0:T(8,128)(2,1)S(1)} %dynamic-slice_bitcast_fusion), channel_id=1, source_target_pairs={{0,4},{2,6},{4,0},{6,2},{8,12},{10,14},{12,8},{14,10},{16,20},{18,... | collective-permute-start | bytes 3538952 | tf_op jit(solution)/shard_map/ppermute | solution.py:65
  252.5 20.7 %collective-permute-start.16 = (bf16[1024,768]{0,1:T(8,128)(2,1)S(1)}, bf16[1024,768]{0,1:T(8,128)(2,1)S(1)}, u32[]{:S(2)}, u32[]{:S(2)}) collective-permute-start(bf16[1024,768]{0,1:T(8,128)(2,1)S(1)} %convolution_convert_fusion.11), channel_id=1, source_target_pairs={{2,0},{3,1},{0,2},{1,3},{6,4},{7,5},{4,6},{5,7},{10,8},{11,9},{8,1... | collective-permute-start | bytes 4718600 | tf_op jit(solution)/shard_map/ppermute | solution.py:29
  262.7 11.7 %collective-permute-start.13 = (bf16[1024,768]{0,1:T(8,128)(2,1)S(1)}, bf16[1024,768]{0,1:T(8,128)(2,1)S(1)}, u32[]{:S(2)}, u32[]{:S(2)}) collective-permute-start(bf16[1024,768]{0,1:T(8,128)(2,1)S(1)} %convolution_convert_fusion.12), channel_id=1, source_target_pairs={{2,0},{3,1},{0,2},{1,3},{6,4},{7,5},{4,6},{5,7},{10,8},{11,9},{8,1... | collective-permute-start | bytes 4718600 | tf_op jit(solution)/shard_map/ppermute | solution.py:29
  271.6 80.2 %collective-permute-start.64 = (bf16[2,2,48,1536]{3,2,1,0:T(8,128)(2,1)}, bf16[2,2,48,1536]{3,2,1,0:T(8,128)(2,1)}, u32[]{:S(2)}, u32[]{:S(2)}) collective-permute-start(bf16[2,2,48,1536]{3,2,1,0:T(8,128)(2,1)} %dynamic-slice_bitcast_fusion.2), channel_id=1, source_target_pairs={{0,8},{2,10},{4,12},{6,14},{8,0},{10,2},{12,4},{14,6},{16,24},{18,... | collective-permute-start | bytes 1769480 | tf_op jit(solution)/shard_map/ppermute | solution.py:65
  346.6 34.4 %collective-permute-start.17 = (bf16[1024,768]{0,1:T(8,128)(2,1)S(1)}, bf16[1024,768]{0,1:T(8,128)(2,1)S(1)}, u32[]{:S(2)}, u32[]{:S(2)}) collective-permute-start(bf16[1024,768]{0,1:T(8,128)(2,1)S(1)} %bitcast_convert_fusion.1), channel_id=1, source_target_pairs={{2,0},{3,1},{0,2},{1,3},{6,4},{7,5},{4,6},{5,7},{10,8},{11,9},{8,1... | collective-permute-start | bytes 4718600 | tf_op jit(solution)/shard_map/ppermute | solution.py:29
  353.1 16.1 %collective-permute-start.65 = (bf16[2,48,1536]{2,1,0:T(8,128)(2,1)S(1)}, bf16[2,48,1536]{2,1,0:T(8,128)(2,1)S(1)}, u32[]{:S(2)}, u32[]{:S(2)}) collective-permute-start(bf16[2,48,1536]{2,1,0:T(8,128)(2,1)S(1)} %dynamic-slice_bitcast_fusion.8), channel_id=1, source_target_pairs={{0,16},{2,18},{4,20},{6,22},{8,24},{10,26},{12,28},{14,30},{16,0},... | collective-permute-start | bytes 884744 | tf_op jit(solution)/shard_map/ppermute | solution.py:65
  376.4 39.7 %collective-permute-start.14 = (bf16[1024,768]{0,1:T(8,128)(2,1)S(1)}, bf16[1024,768]{0,1:T(8,128)(2,1)S(1)}, u32[]{:S(2)}, u32[]{:S(2)}) collective-permute-start(bf16[1024,768]{0,1:T(8,128)(2,1)S(1)} %copy-done.26), channel_id=1, source_target_pairs={{2,1},{1,2},{6,5},{5,6},{10,9},{9,10},{14,13},{13,14},{18,17},{17,... | collective-permute-start | bytes 4718600 | tf_op jit(solution)/shard_map/ppermute | solution.py:51
  400.8 44.3 %collective-permute-start.35 = (bf16[2,2,2,48,1536]{4,3,0,1,2:T(8,128)(2,1)}, bf16[2,2,2,48,1536]{4,3,0,1,2:T(8,128)(2,1)}, u32[]{:S(2)}, u32[]{:S(2)}) collective-permute-start(bf16[2,2,2,48,1536]{4,3,0,1,2:T(8,128)(2,1)} %bitcast.384), channel_id=1, source_target_pairs={{2,1},{1,2},{6,5},{5,6},{10,9},{9,10},{14,13},{13,14},{18,17},{17,... | collective-permute-start | bytes 3538952 | tf_op jit(solution)/shard_map/ppermute | solution.py:79
  402.6 44.1 %collective-permute-start.33 = (bf16[2,2,2,48,1536]{4,3,0,1,2:T(8,128)(2,1)}, bf16[2,2,2,48,1536]{4,3,0,1,2:T(8,128)(2,1)}, u32[]{:S(2)}, u32[]{:S(2)}) collective-permute-start(bf16[2,2,2,48,1536]{4,3,0,1,2:T(8,128)(2,1)} %bitcast.384), channel_id=1, source_target_pairs={{3,1},{0,2},{7,5},{4,6},{11,9},{8,10},{15,13},{12,14},{19,17},{16,... | collective-permute-start | bytes 3538952 | tf_op jit(solution)/shard_map/ppermute | solution.py:76
  413.3 26.6 %collective-permute-start.39 = (bf16[2,2,2,48,1536]{4,3,2,1,0:T(8,128)(2,1)}, bf16[2,2,2,48,1536]{4,3,2,1,0:T(8,128)(2,1)}, u32[]{:S(2)}, u32[]{:S(2)}) collective-permute-start(bf16[2,2,2,48,1536]{4,3,2,1,0:T(8,128)(2,1)} %dynamic-slice_bitcast_fusion.1), channel_id=1, source_target_pairs={{0,4},{2,6},{4,0},{6,2},{8,12},{10,14},{12,8},{14,10},{16,20},{18,... | collective-permute-start | bytes 3538952 | tf_op jit(solution)/shard_map/ppermute | solution.py:65
  414.8 26.4 %collective-permute-start.34 = (bf16[2,2,2,48,1536]{4,3,0,1,2:T(8,128)(2,1)}, bf16[2,2,2,48,1536]{4,3,0,1,2:T(8,128)(2,1)}, u32[]{:S(2)}, u32[]{:S(2)}) collective-permute-start(bf16[2,2,2,48,1536]{4,3,0,1,2:T(8,128)(2,1)} %bitcast.385), channel_id=1, source_target_pairs={{1,0},{2,3},{5,4},{6,7},{9,8},{10,11},{13,12},{14,15},{17,16},{18,... | collective-permute-start | bytes 3538952 | tf_op jit(solution)/shard_map/ppermute | solution.py:73
  421.5 39.4 %collective-permute-start.59 = (bf16[2,2,2,48,1536]{4,3,0,1,2:T(8,128)(2,1)S(1)}, bf16[2,2,2,48,1536]{4,3,0,1,2:T(8,128)(2,1)S(1)}, u32[]{:S(2)}, u32[]{:S(2)}) collective-permute-start(bf16[2,2,2,48,1536]{4,3,0,1,2:T(8,128)(2,1)S(1)} %bitcast.448), channel_id=1, source_target_pairs={{2,1},{1,2},{6,5},{5,6},{10,9},{9,10},{14,13},{13,14},{18,17},{17,... | collective-permute-start | bytes 3538952 | tf_op jit(solution)/shard_map/ppermute | solution.py:79
  439.9 21.0 %collective-permute-start.57 = (bf16[2,2,2,48,1536]{4,3,0,1,2:T(8,128)(2,1)S(1)}, bf16[2,2,2,48,1536]{4,3,0,1,2:T(8,128)(2,1)S(1)}, u32[]{:S(2)}, u32[]{:S(2)}) collective-permute-start(bf16[2,2,2,48,1536]{4,3,0,1,2:T(8,128)(2,1)S(1)} %bitcast.449), channel_id=1, source_target_pairs={{3,1},{0,2},{7,5},{4,6},{11,9},{8,10},{15,13},{12,14},{19,17},{16,... | collective-permute-start | bytes 3538952 | tf_op jit(solution)/shard_map/ppermute | solution.py:76
  441.3 18.1 %collective-permute-start.58 = (bf16[2,2,2,48,1536]{4,3,0,1,2:T(8,128)(2,1)S(1)}, bf16[2,2,2,48,1536]{4,3,0,1,2:T(8,128)(2,1)S(1)}, u32[]{:S(2)}, u32[]{:S(2)}) collective-permute-start(bf16[2,2,2,48,1536]{4,3,0,1,2:T(8,128)(2,1)S(1)} %bitcast.450), channel_id=1, source_target_pairs={{1,0},{2,3},{5,4},{6,7},{9,8},{10,11},{13,12},{14,15},{17,16},{18,... | collective-permute-start | bytes 3538952 | tf_op jit(solution)/shard_map/ppermute | solution.py:73
  445.1 17.9 %collective-permute-start.18 = (bf16[1024,768]{0,1:T(8,128)(2,1)S(1)}, bf16[1024,768]{0,1:T(8,128)(2,1)S(1)}, u32[]{:S(2)}, u32[]{:S(2)}) collective-permute-start(bf16[1024,768]{0,1:T(8,128)(2,1)S(1)} %convolution_convert_fusion.10), channel_id=1, source_target_pairs={{2,0},{3,1},{0,2},{1,3},{6,4},{7,5},{4,6},{5,7},{10,8},{11,9},{8,1... | collective-permute-start | bytes 4718600 | tf_op jit(solution)/shard_map/ppermute | solution.py:29
  446.7 86.8 %collective-permute-start.40 = (bf16[2,2,48,1536]{3,2,1,0:T(8,128)(2,1)}, bf16[2,2,48,1536]{3,2,1,0:T(8,128)(2,1)}, u32[]{:S(2)}, u32[]{:S(2)}) collective-permute-start(bf16[2,2,48,1536]{3,2,1,0:T(8,128)(2,1)} %dynamic-slice_bitcast_fusion.4), channel_id=1, source_target_pairs={{0,8},{2,10},{4,12},{6,14},{8,0},{10,2},{12,4},{14,6},{16,24},{18,... | collective-permute-start | bytes 1769480 | tf_op jit(solution)/shard_map/ppermute | solution.py:65
  459.4 76.3 %collective-permute-start.36 = (bf16[2,2,48,1536]{3,2,0,1:T(8,128)(2,1)}, bf16[2,2,48,1536]{3,2,0,1:T(8,128)(2,1)}, u32[]{:S(2)}, u32[]{:S(2)}) collective-permute-start(bf16[2,2,48,1536]{3,2,0,1:T(8,128)(2,1)} %dynamic-slice_bitcast_fusion.5), channel_id=1, source_target_pairs={{0,4},{2,6},{4,0},{6,2},{8,12},{10,14},{12,8},{14,10},{16,20},{18,... | collective-permute-start | bytes 1769480 | tf_op jit(solution)/shard_map/ppermute | solution.py:65
  462.5 76.3 %collective-permute-start.60 = (bf16[2,2,48,1536]{3,2,0,1:T(8,128)(2,1)}, bf16[2,2,48,1536]{3,2,0,1:T(8,128)(2,1)}, u32[]{:S(2)}, u32[]{:S(2)}) collective-permute-start(bf16[2,2,48,1536]{3,2,0,1:T(8,128)(2,1)} %dynamic-slice_bitcast_fusion.3), channel_id=1, source_target_pairs={{0,4},{2,6},{4,0},{6,2},{8,12},{10,14},{12,8},{14,10},{16,20},{18,... | collective-permute-start | bytes 1769480 | tf_op jit(solution)/shard_map/ppermute | solution.py:65
  470.0 78.2 %collective-permute-start.29 = (bf16[2,2,2,48,384]{4,3,0,1,2:T(8,128)(2,1)}, bf16[2,2,2,48,384]{4,3,0,1,2:T(8,128)(2,1)}, u32[]{:S(2)}, u32[]{:S(2)}) collective-permute-start(bf16[2,2,2,48,384]{4,3,0,1,2:T(8,128)(2,1)} %bitcast.392), channel_id=1, source_target_pairs={{2,1},{1,2},{6,5},{5,6},{10,9},{9,10},{14,13},{13,14},{18,17},{17,... | collective-permute-start | bytes 884744 | tf_op jit(solution)/shard_map/ppermute | solution.py:79
  471.3 79.7 %collective-permute-start.27 = (bf16[2,2,2,48,384]{4,3,0,1,2:T(8,128)(2,1)}, bf16[2,2,2,48,384]{4,3,0,1,2:T(8,128)(2,1)}, u32[]{:S(2)}, u32[]{:S(2)}) collective-permute-start(bf16[2,2,2,48,384]{4,3,0,1,2:T(8,128)(2,1)} %bitcast.392), channel_id=1, source_target_pairs={{3,1},{0,2},{7,5},{4,6},{11,9},{8,10},{15,13},{12,14},{19,17},{16,... | collective-permute-start | bytes 884744 | tf_op jit(solution)/shard_map/ppermute | solution.py:76
  533.6 31.7 %collective-permute-start.53 = (bf16[2,2,2,48,384]{4,3,0,1,2:T(8,128)(2,1)S(1)}, bf16[2,2,2,48,384]{4,3,0,1,2:T(8,128)(2,1)S(1)}, u32[]{:S(2)}, u32[]{:S(2)}) collective-permute-start(bf16[2,2,2,48,384]{4,3,0,1,2:T(8,128)(2,1)S(1)} %bitcast.465), channel_id=1, source_target_pairs={{2,1},{1,2},{6,5},{5,6},{10,9},{9,10},{14,13},{13,14},{18,17},{17,... | collective-permute-start | bytes 884744 | tf_op jit(solution)/shard_map/ppermute | solution.py:79
  535.7 29.6 %collective-permute-start.51 = (bf16[2,2,2,48,384]{4,3,0,1,2:T(8,128)(2,1)S(1)}, bf16[2,2,2,48,384]{4,3,0,1,2:T(8,128)(2,1)S(1)}, u32[]{:S(2)}, u32[]{:S(2)}) collective-permute-start(bf16[2,2,2,48,384]{4,3,0,1,2:T(8,128)(2,1)S(1)} %bitcast.466), channel_id=1, source_target_pairs={{3,1},{0,2},{7,5},{4,6},{11,9},{8,10},{15,13},{12,14},{19,17},{16,... | collective-permute-start | bytes 884744 | tf_op jit(solution)/shard_map/ppermute | solution.py:76
  547.5 88.1 %collective-permute-start.23 = (bf16[2,2,2,48,1152]{4,3,0,1,2:T(8,128)(2,1)S(1)}, bf16[2,2,2,48,1152]{4,3,0,1,2:T(8,128)(2,1)S(1)}, u32[]{:S(2)}, u32[]{:S(2)}) collective-permute-start(bf16[2,2,2,48,1152]{4,3,0,1,2:T(8,128)(2,1)S(1)} %bitcast.454), channel_id=1, source_target_pairs={{2,1},{1,2},{6,5},{5,6},{10,9},{9,10},{14,13},{13,14},{18,17},{17,... | collective-permute-start | bytes 2654216 | tf_op jit(solution)/shard_map/ppermute | solution.py:79
  548.2 88.3 %collective-permute-start.21 = (bf16[2,2,2,48,1152]{4,3,0,1,2:T(8,128)(2,1)S(1)}, bf16[2,2,2,48,1152]{4,3,0,1,2:T(8,128)(2,1)S(1)}, u32[]{:S(2)}, u32[]{:S(2)}) collective-permute-start(bf16[2,2,2,48,1152]{4,3,0,1,2:T(8,128)(2,1)S(1)} %bitcast.455), channel_id=1, source_target_pairs={{3,1},{0,2},{7,5},{4,6},{11,9},{8,10},{15,13},{12,14},{19,17},{16,... | collective-permute-start | bytes 2654216 | tf_op jit(solution)/shard_map/ppermute | solution.py:76
  551.0 12.9 %collective-permute-start.52 = (bf16[2,2,2,48,384]{4,3,0,1,2:T(8,128)(2,1)S(1)}, bf16[2,2,2,48,384]{4,3,0,1,2:T(8,128)(2,1)S(1)}, u32[]{:S(2)}, u32[]{:S(2)}) collective-permute-start(bf16[2,2,2,48,384]{4,3,0,1,2:T(8,128)(2,1)S(1)} %bitcast.467), channel_id=1, source_target_pairs={{1,0},{2,3},{5,4},{6,7},{9,8},{10,11},{13,12},{14,15},{17,16},{18,... | collective-permute-start | bytes 884744 | tf_op jit(solution)/shard_map/ppermute | solution.py:73
  563.9 70.1 %collective-permute-start.22 = (bf16[2,2,2,48,1152]{4,3,0,1,2:T(8,128)(2,1)S(1)}, bf16[2,2,2,48,1152]{4,3,0,1,2:T(8,128)(2,1)S(1)}, u32[]{:S(2)}, u32[]{:S(2)}) collective-permute-start(bf16[2,2,2,48,1152]{4,3,0,1,2:T(8,128)(2,1)S(1)} %bitcast.456), channel_id=1, source_target_pairs={{1,0},{2,3},{5,4},{6,7},{9,8},{10,11},{13,12},{14,15},{17,16},{18,... | collective-permute-start | bytes 2654216 | tf_op jit(solution)/shard_map/ppermute | solution.py:73
  565.2 16.1 %collective-permute-start.41 = (bf16[2,48,1536]{2,1,0:T(8,128)(2,1)S(1)}, bf16[2,48,1536]{2,1,0:T(8,128)(2,1)S(1)}, u32[]{:S(2)}, u32[]{:S(2)}) collective-permute-start(bf16[2,48,1536]{2,1,0:T(8,128)(2,1)S(1)} %dynamic-slice_bitcast_fusion.10), channel_id=1, source_target_pairs={{0,16},{2,18},{4,20},{6,22},{8,24},{10,26},{12,28},{14,30},{16,0},... | collective-permute-start | bytes 884744 | tf_op jit(solution)/shard_map/ppermute | solution.py:65
  581.3 12.6 %collective-permute-start.61 = (bf16[2,48,1536]{2,1,0:T(8,128)(2,1)S(1)}, bf16[2,48,1536]{2,1,0:T(8,128)(2,1)S(1)}, u32[]{:S(2)}, u32[]{:S(2)}) collective-permute-start(bf16[2,48,1536]{2,1,0:T(8,128)(2,1)S(1)} %dynamic-slice_bitcast_fusion.9), channel_id=1, source_target_pairs={{0,8},{2,10},{4,12},{6,14},{8,0},{10,2},{12,4},{14,6},{16,24},{18,... | collective-permute-start | bytes 884744 | tf_op jit(solution)/shard_map/ppermute | solution.py:65
  595.5 23.8 %collective-permute-start.44 = (bf16[48,1536]{1,0:T(8,128)(2,1)S(1)}, bf16[48,1536]{1,0:T(8,128)(2,1)S(1)}, u32[]{:S(2)}, u32[]{:S(2)}) collective-permute-start(bf16[48,1536]{1,0:T(8,128)(2,1)S(1)} %get-tuple-element.214), channel_id=1, source_target_pairs={{2,1},{1,2},{6,5},{5,6},{10,9},{9,10},{14,13},{13,14},{18,17},{17,... | collective-permute-start | bytes 442376 | tf_op jit(solution)/shard_map/ppermute | solution.py:79
  626.6 25.0 %collective-permute-start.47 = (bf16[2,2,2,48,1152]{4,3,0,1,2:T(8,128)(2,1)S(1)}, bf16[2,2,2,48,1152]{4,3,0,1,2:T(8,128)(2,1)S(1)}, u32[]{:S(2)}, u32[]{:S(2)}) collective-permute-start(bf16[2,2,2,48,1152]{4,3,0,1,2:T(8,128)(2,1)S(1)} %bitcast.451), channel_id=1, source_target_pairs={{2,1},{1,2},{6,5},{5,6},{10,9},{9,10},{14,13},{13,14},{18,17},{17,... | collective-permute-start | bytes 2654216 | tf_op jit(solution)/shard_map/ppermute | solution.py:79
  631.6 20.1 %collective-permute-start.45 = (bf16[2,2,2,48,1152]{4,3,0,1,2:T(8,128)(2,1)S(1)}, bf16[2,2,2,48,1152]{4,3,0,1,2:T(8,128)(2,1)S(1)}, u32[]{:S(2)}, u32[]{:S(2)}) collective-permute-start(bf16[2,2,2,48,1152]{4,3,0,1,2:T(8,128)(2,1)S(1)} %bitcast.452), channel_id=1, source_target_pairs={{3,1},{0,2},{7,5},{4,6},{11,9},{8,10},{15,13},{12,14},{19,17},{16,... | collective-permute-start | bytes 2654216 | tf_op jit(solution)/shard_map/ppermute | solution.py:76
  634.1 17.6 %collective-permute-start.46 = (bf16[2,2,2,48,1152]{4,3,0,1,2:T(8,128)(2,1)S(1)}, bf16[2,2,2,48,1152]{4,3,0,1,2:T(8,128)(2,1)S(1)}, u32[]{:S(2)}, u32[]{:S(2)}) collective-permute-start(bf16[2,2,2,48,1152]{4,3,0,1,2:T(8,128)(2,1)S(1)} %bitcast.453), channel_id=1, source_target_pairs={{1,0},{2,3},{5,4},{6,7},{9,8},{10,11},{13,12},{14,15},{17,16},{18,... | collective-permute-start | bytes 2654216 | tf_op jit(solution)/shard_map/ppermute | solution.py:73
  635.6 31.6 %collective-permute-start.19 = (bf16[1024,768]{0,1:T(8,128)(2,1)S(1)}, bf16[1024,768]{0,1:T(8,128)(2,1)S(1)}, u32[]{:S(2)}, u32[]{:S(2)}) collective-permute-start(bf16[1024,768]{0,1:T(8,128)(2,1)S(1)} %bitcast_convert_fusion), channel_id=1, source_target_pairs={{2,0},{3,1},{0,2},{1,3},{6,4},{7,5},{4,6},{5,7},{10,8},{11,9},{8,1... | collective-permute-start | bytes 4718600 | tf_op jit(solution)/shard_map/ppermute | solution.py:29
  637.0 16.8 %collective-permute-start.24 = (bf16[2,2,48,1152]{3,2,0,1:T(8,128)(2,1)S(1)}, bf16[2,2,48,1152]{3,2,0,1:T(8,128)(2,1)S(1)}, u32[]{:S(2)}, u32[]{:S(2)}) collective-permute-start(bf16[2,2,48,1152]{3,2,0,1:T(8,128)(2,1)S(1)} %dynamic-slice_bitcast_fusion.7), channel_id=1, source_target_pairs={{0,4},{2,6},{4,0},{6,2},{8,12},{10,14},{12,8},{14,10},{16,20},{18,... | collective-permute-start | bytes 1327112 | tf_op jit(solution)/shard_map/ppermute | solution.py:65
  664.4 61.9 %collective-permute-start.26 = (bf16[48,1152]{1,0:T(8,128)(2,1)}, bf16[48,1152]{1,0:T(8,128)(2,1)S(1)}, u32[]{:S(2)}, u32[]{:S(2)}) collective-permute-start(bf16[48,1152]{1,0:T(8,128)(2,1)} %dynamic-slice_bitcast_fusion.23), channel_id=1, source_target_pairs={{0,16},{2,18},{4,20},{6,22},{8,24},{10,26},{12,28},{14,30},{16,0},... | collective-permute-start | bytes 331784 | tf_op jit(solution)/shard_map/ppermute | solution.py:65
  672.2 55.5 %collective-permute-start.20 = (bf16[1024,768]{0,1:T(8,128)(2,1)S(1)}, bf16[1024,768]{0,1:T(8,128)(2,1)}, u32[]{:S(2)}, u32[]{:S(2)}) collective-permute-start(bf16[1024,768]{0,1:T(8,128)(2,1)S(1)} %add_convert_fusion.2), channel_id=1, source_target_pairs={{2,1},{1,2},{6,5},{5,6},{10,9},{9,10},{14,13},{13,14},{18,17},{17,... | collective-permute-start | bytes 4718600 | tf_op jit(solution)/shard_map/ppermute | solution.py:51
  674.1 52.9 %collective-permute-start.50 = (bf16[48,1152]{1,0:T(8,128)(2,1)S(1)}, bf16[48,1152]{1,0:T(8,128)(2,1)S(1)}, u32[]{:S(2)}, u32[]{:S(2)}) collective-permute-start(bf16[48,1152]{1,0:T(8,128)(2,1)S(1)} %dynamic-slice_bitcast_fusion.22), channel_id=1, source_target_pairs={{0,16},{2,18},{4,20},{6,22},{8,24},{10,26},{12,28},{14,30},{16,0},... | collective-permute-start | bytes 331784 | tf_op jit(solution)/shard_map/ppermute | solution.py:65
  (139 other events, 1394.4 us)

commit v2 on v1

v2 whole, which is shorter than its diff:
```python
import functools

import jax
import jax.numpy as jnp
from jax import lax
from jax.experimental import pallas as pl
from jax.experimental.pallas import tpu as pltpu
from jax.sharding import PartitionSpec as P

HEAD_DIM = 64
PASSES = 2
EPSILON = 1e-05
NEG_FILL = -1e30
LANES = 128
BLOCK = 256
LOW = jnp.bfloat16
F32 = jnp.float32
SCALE = HEAD_DIM**-0.5


BOTH = ("dp", "mp")


def moves(pick):
    n_dp, n_mp = lax.axis_size("dp"), lax.axis_size("mp")
    pairs = []
    for dp in range(n_dp):
        for mp in range(n_mp):
            source = pick(dp, mp)
            if source is not None:
                pairs.append((source[0] * n_mp + source[1], dp * n_mp + mp))
    return pairs


def from_core(values):
    return lax.ppermute(values, BOTH, moves(lambda dp, mp: (dp ^ 1, mp)))


def own_run(values, same):
    other = lax.ppermute(
        values, BOTH, moves(lambda dp, mp: (dp ^ 1, mp) if (dp & 1) != mp else None)
    )
    return jnp.where(same, values, other)


def tie(*values):
    return lax.optimization_barrier(values)


def near_piece(dp):
    return bit_of(dp, 1) ^ bit_of(dp, 2)


def across(values):
    return lax.ppermute(
        values, BOTH, moves(lambda dp, mp: (dp ^ 1, 1 - mp) if (dp & 1) != mp else None)
    )


def start_halves(weight):
    pieces = weight.reshape(2, weight.shape[0] // 2, weight.shape[1])
    index = near_piece(lax.axis_index("dp"))
    return across(lax.dynamic_index_in_dim(pieces, index, 0, keepdims=False))


def relay(straight):
    half = straight.shape[0] // 2

    def from_neighbour(values, bit):
        return lax.ppermute(
            values, BOTH, moves(lambda dp, mp: (dp ^ (1 << bit), mp) if (dp & 1) != mp else None)
        )

    return (straight, from_neighbour(straight[:half], 1), from_neighbour(straight[half:], 2))


def to_mesh_rows(values, same):
    other = lax.ppermute(
        values, BOTH, moves(lambda dp, mp: (dp ^ 1, 1 - mp) if (dp & 1) != mp else None)
    )
    return jnp.where(same, values, other)


def bit_of(index, bit):
    return (index >> bit) & 1


def fold(parts, bit, axis, dtype):
    mine = bit_of(lax.axis_index("dp"), bit)
    send = lax.dynamic_index_in_dim(parts, 1 - mine, axis, keepdims=False)
    keep = lax.dynamic_index_in_dim(parts, mine, axis, keepdims=False)
    recv = lax.ppermute(send, "dp", [(i, i ^ (1 << bit)) for i in range(lax.axis_size("dp"))])
    return (keep.astype(jnp.float32) + recv.astype(jnp.float32)).astype(dtype)


def cross(parts, axis, same, dtype):
    mp = lax.axis_index("mp")

    def shards(index):
        return lax.dynamic_index_in_dim(parts, index, axis, keepdims=False)

    round_trip = lax.ppermute(
        shards(1 - mp),
        BOTH,
        moves(lambda dp, mp: (dp, 1 - mp) if (dp & 1) == mp else (dp ^ 1, mp)),
    )
    diagonal = lax.ppermute(
        shards(mp),
        BOTH,
        moves(lambda dp, mp: (dp ^ 1, 1 - mp) if (dp & 1) != mp else None),
    )
    other = jnp.where(same, shards(mp), diagonal)
    return (round_trip.astype(jnp.float32) + other.astype(jnp.float32)).astype(dtype)


class Reduction:
    def __init__(self, pair, same):
        self.same = same
        self.bits = lax.axis_size("dp").bit_length() - 1
        self.widths = [x.shape[1] for x in pair]
        self.pair = [
            x.reshape((2,) * self.bits + (x.shape[0] >> self.bits, x.shape[1])) for x in pair
        ]
        self.next_bit = 2

    def first(self):
        one, two = self.pair
        one = cross(one, self.bits - 1, self.same, LOW)
        two = fold(two, 1, self.bits - 2, LOW)
        self.pair = [one, two]
        return self.pair

    def second(self):
        one, two = self.pair
        one = fold(one, 1, self.bits - 2, LOW)
        two = cross(two, self.bits - 2, self.same, LOW)
        self.pair = [jnp.concatenate([one, two], axis=-1)]
        return self.pair

    def further(self):
        bit = self.next_bit
        last = bit == self.bits - 1
        axis = self.bits - 1 - bit
        self.pair = [fold(self.pair[0], bit, axis, F32 if last else LOW)]
        self.next_bit += 1
        return self.pair

    def rest(self):
        while self.next_bit < self.bits:
            self.further()
        return self.pair[0][:, : self.widths[0]], self.pair[0][:, self.widths[0] :]


def dot(left, right, contract=((1,), (0,)), precision=None):
    return lax.dot_general(
        left, right, (contract, ((), ())), precision=precision, preferred_element_type=F32
    )


ROWS_BOTH = ((1,), (1,))
COLS_BOTH = ((0,), (0,))


def spread(values):
    centered = values - jnp.mean(values, axis=-1, keepdims=True)
    inverse = lax.rsqrt(jnp.mean(centered * centered, axis=-1, keepdims=True) + EPSILON)
    return centered * inverse, inverse


def norm_back(grad, gain_row, normal, inverse):
    grad = grad * gain_row
    along = jnp.mean(grad * normal, axis=-1, keepdims=True)
    return inverse * (grad - jnp.mean(grad, axis=-1, keepdims=True) - normal * along)


def add_pair(own_ref, other_ref):
    return own_ref[...].astype(F32) + other_ref[...].astype(F32)


def lane_masks(dtype):
    low_lanes = lax.broadcasted_iota(jnp.int32, (1, LANES), 1) < HEAD_DIM
    first = jnp.where(low_lanes, 1.0, 0.0)
    return first.astype(dtype), (1.0 - first).astype(dtype)


def stack_heads(pair):
    first, second = lane_masks(pair.dtype)
    return jnp.concatenate([pair * first, pair * second], axis=0)


def join_heads(stacked):
    rows = stacked.shape[0] // 2
    low_lanes = lax.broadcasted_iota(jnp.int32, (rows, LANES), 1) < HEAD_DIM
    return jnp.where(low_lanes, stacked[:rows], stacked[rows:])


def lanes_of(index, base=0):
    return pl.ds(pl.multiple_of(base + index * LANES, LANES), LANES)


def rows_of_block(index):
    return pl.ds(pl.multiple_of(index * BLOCK, BLOCK), BLOCK)


def normal_parts(values):
    size = jnp.abs(values)
    point = 1.0 / (1.0 + (0.3275911 * 0.5**0.5) * size)
    bell = jnp.exp(values * values * -0.5)
    series = 0.5 * 1.061405429
    for factor in (-1.453152027, 1.421413741, -0.284496736, 0.254829592):
        series = series * point + 0.5 * factor
    upper = series * point * bell
    return jnp.where(values < 0, upper, 1.0 - upper), bell * 0.3989422804014327


def weight_copies(flags, parts, room, sems):
    own, straight, around_first, around_second = parts
    quarter = room.shape[0] // 4

    def place(index):
        return pl.ds(pl.multiple_of(index * quarter, quarter), quarter)

    @pl.when(flags[0] == 1)
    def _():
        for index in range(4):
            source = own.at[place(index)]
            pltpu.make_async_copy(source, room.at[place(index)], sems.at[index]).start()

    @pl.when(flags[0] == 0)
    def _():
        near, far = 2 * flags[1], 2 - 2 * flags[1]
        sources = (straight.at[place(0)], straight.at[place(1)], around_first, around_second)
        targets = (near, near + 1, far, far + 1)
        for index in range(4):
            target = room.at[place(targets[index])]
            pltpu.make_async_copy(sources[index], target, sems.at[index]).start()


def weight_wait(parts, room, sems):
    quarter = room.shape[0] // 4
    for index in range(4):
        place = pl.ds(index * quarter, quarter)
        pltpu.make_async_copy(parts[0].at[place], room.at[place], sems.at[index]).wait()


def at_first(action):
    pl.when(pl.program_id(0) == 0)(action)


def attention_forward_body(second, *refs):
    if second:
        (mid_ref, own_ref, other_ref, table_ref), refs = refs[:4], refs[4:]
    else:
        (mid_ref,), refs = refs[:1], refs[1:]
    (seg_col, seg_row, gain_ref, flags), refs = refs[:4], refs[4:]
    parts, refs = refs[:4], refs[4:]
    if second:
        (joined_ref,), refs = refs[:1], refs[1:]
    normed_ref, qkv_ref, att_ref, log_ref, part_ref, keys, values, bias, room, sems = refs
    at_first(lambda: weight_copies(flags, parts, room, sems))
    step = pl.program_id(0)
    blocks = keys.shape[0] // BLOCK
    width = att_ref.shape[1]
    residual = mid_ref[...].astype(F32)
    if second:
        residual = residual + add_pair(own_ref, other_ref)
        odd = lax.broadcasted_iota(jnp.int32, residual.shape, 0) % PASSES == 1
        table = table_ref[...].astype(F32)
        residual = residual + jnp.where(odd, table[1:2], table[0:1])
        joined_ref[...] = residual
    normal, _ = spread(residual)
    normed = (normal * gain_ref[0:1, :]).astype(LOW)
    normed_ref[...] = normed
    at_first(lambda: weight_wait(parts, room, sems))
    qkv_ref[...] = dot(normed, room[: 3 * width, :], ROWS_BOTH).astype(LOW)
    here = rows_of_block(step)
    keys[here, :] = qkv_ref[:, width : 2 * width]
    values[here, :] = qkv_ref[:, 2 * width :]

    def attend(last):
        limit = (last + 1) * BLOCK
        query = last * BLOCK + lax.broadcasted_iota(jnp.int32, (BLOCK, limit), 0)
        key = lax.broadcasted_iota(jnp.int32, (BLOCK, limit), 1)
        allowed = jnp.logical_and(seg_col[...] == seg_row[:, :limit], key <= query)
        bias[:, :limit] = jnp.where(allowed, 0.0, NEG_FILL)
        lanes = lax.broadcasted_iota(jnp.int32, (BLOCK, LANES), 1)

        def pair(index, logs):
            stacked = stack_heads(qkv_ref[:, lanes_of(index)] * jnp.asarray(SCALE, LOW))
            scores = dot(stacked, keys[:limit, lanes_of(index)], ROWS_BOTH)
            scores = scores.reshape(2, BLOCK, limit) + bias[:, :limit][None]
            scores = scores.reshape(2 * BLOCK, limit)
            largest = jnp.max(scores, axis=-1, keepdims=True)
            weights = jnp.exp(scores - largest)
            totals = jnp.sum(weights, axis=-1, keepdims=True)
            out = dot(weights.astype(LOW), values[:limit, lanes_of(index)]) * (1.0 / totals)
            att_ref[:, lanes_of(index)] = join_heads(out).astype(LOW)
            sums = largest + jnp.log(totals)
            logs = jnp.where(lanes == 2 * index, sums[:BLOCK], logs)
            return jnp.where(lanes == 2 * index + 1, sums[BLOCK:], logs)

        logs = lax.fori_loop(0, width // LANES, pair, jnp.zeros((BLOCK, LANES), F32))
        log_ref[...] = logs.T[: log_ref.shape[0], :]

    for last in range(blocks):
        pl.when(step == last)(functools.partial(attend, last))
    part_ref[...] = dot(att_ref[...], room[3 * width :, :]).astype(LOW)


def mlp_forward_body(
    res_ref, own_ref, other_ref, gain_ref, flags, up_a, up_b, up_c, up_d, down_a, down_b, down_c, down_d,
    mid_ref, normed_ref, hidden_ref, slope_ref, part_ref,
    up_weight, down_weight, sems,
):
    up_parts = (up_a, up_b, up_c, up_d)
    down_parts = (down_a, down_b, down_c, down_d)

    @at_first
    def _():
        weight_copies(flags, up_parts, up_weight, sems.at[0])
        weight_copies(flags, down_parts, down_weight, sems.at[1])

    middle = res_ref[...].astype(F32) + add_pair(own_ref, other_ref)
    mid_ref[...] = middle
    normal, _ = spread(middle)
    normed = (normal * gain_ref[1:2, :]).astype(LOW)
    normed_ref[...] = normed
    at_first(lambda: weight_wait(up_parts, up_weight, sems.at[0]))
    units = up_weight.shape[1]
    cut = 512 if units % 512 == 0 else units
    for start in range(0, units, cut):
        columns = slice(start, start + cut)
        before = dot(normed, up_weight[:, columns])
        below, density = normal_parts(before)
        hidden_ref[:, columns] = (before * below).astype(LOW)
        slope_ref[:, columns] = (below + before * density).astype(LOW)
    at_first(lambda: weight_wait(down_parts, down_weight, sems.at[1]))
    part_ref[...] = dot(hidden_ref[...], down_weight[...]).astype(LOW)


def add_rows(total_ref, row, values):
    total_ref[row : row + 1, :] += jnp.sum(values, axis=0, keepdims=True)


def mlp_backward_body(joined, *refs):
    if joined:
        (grad_mid, own_ref, other_ref, res_ref, gain_ref), refs = refs[:5], refs[5:]
    else:
        (low_ref,), refs = refs[:1], refs[1:]
    (slope_ref, flags), refs = refs[:2], refs[2:]
    up_parts, down_parts, refs = refs[:4], refs[4:8], refs[8:]
    if joined:
        (grad_ref, low_ref, small_ref), refs = refs[:3], refs[3:]
    pre_ref, part_ref, up_weight, down_weight, sems = refs

    @at_first
    def _():
        weight_copies(flags, down_parts, down_weight, sems.at[1])
        weight_copies(flags, up_parts, up_weight, sems.at[0])

    if joined:

        @pl.when(pl.program_id(0) == 0)
        def _():
            small_ref[...] = jnp.zeros_like(small_ref)

        grad_normed = add_pair(own_ref, other_ref)
        normal, inverse = spread(res_ref[...])
        add_rows(small_ref, 0, grad_normed * normal)
        grad = grad_mid[...] + norm_back(grad_normed, gain_ref[0:1, :], normal, inverse)
        odd = lax.broadcasted_iota(jnp.int32, grad.shape, 0) % PASSES == 1
        add_rows(small_ref, 1, jnp.where(odd, 0.0, grad))
        add_rows(small_ref, 2, jnp.where(odd, grad, 0.0))
        grad_ref[...] = grad
        low_ref[...] = grad.astype(LOW)
    at_first(lambda: weight_wait(down_parts, down_weight, sems.at[1]))
    units = up_weight.shape[1]
    cut = 512 if units % 512 == 0 else units
    for start in range(0, units, cut):
        columns = slice(start, start + cut)
        grad_hidden = dot(low_ref[...], down_weight[columns, :], ROWS_BOTH)
        pre_ref[:, columns] = (grad_hidden * slope_ref[:, columns].astype(F32)).astype(LOW)
    at_first(lambda: weight_wait(up_parts, up_weight, sems.at[0]))
    part_ref[...] = dot(pre_ref[...], up_weight[...], ROWS_BOTH).astype(LOW)


def attention_backward_body(
    grad_ref, own_ref, other_ref, mid_ref, gain_ref, qkv_ref, att_ref, log_ref, seg_col, seg_row,
    flags, weight_a, weight_b, weight_c, weight_d,
    gm_ref, low_ref, grads_ref, part_ref, small_ref,
    grad_att, grad_keys, grad_values, bias, lines, room, sems,
):
    parts = (weight_a, weight_b, weight_c, weight_d)
    at_first(lambda: weight_copies(flags, parts, room, sems))
    step = pl.program_id(0)
    blocks = pl.num_programs(0)
    block = blocks - 1 - step
    width = att_ref.shape[1]
    heads = width // HEAD_DIM
    pairs = width // LANES

    @pl.when(step == 0)
    def _():
        small_ref[...] = jnp.zeros_like(small_ref)
        grad_keys[...] = jnp.zeros_like(grad_keys)
        grad_values[...] = jnp.zeros_like(grad_values)

    grad_normed = add_pair(own_ref, other_ref)
    normal, inverse = spread(mid_ref[...])
    add_rows(small_ref, 0, grad_normed * normal)
    grad_middle = grad_ref[...].astype(F32)
    grad_middle = grad_middle + norm_back(grad_normed, gain_ref[1:2, :], normal, inverse)
    gm_ref[...] = grad_middle
    low_ref[...] = grad_middle.astype(LOW)
    at_first(lambda: weight_wait(parts, room, sems))
    grad_att[...] = dot(low_ref[...], room[3 * width :, :], ROWS_BOTH).astype(LOW)
    product = grad_att[...].astype(F32) * att_ref[...].astype(F32)
    head_of = lax.broadcasted_iota(jnp.int32, (8, width), 1) // HEAD_DIM
    chosen = head_of == lax.broadcasted_iota(jnp.int32, (8, width), 0)
    deltas = dot(jnp.where(chosen, 1.0, 0.0), product, ROWS_BOTH, lax.Precision.HIGHEST)
    for pair in range(pairs):
        for half in range(2):
            head = 2 * pair + half
            if head < heads:
                columns = slice(half * BLOCK, (half + 1) * BLOCK)
                lines[pair : pair + 1, columns] = log_ref[head : head + 1, :]
                lines[pairs + pair : pairs + pair + 1, columns] = deltas[head : head + 1, :]

    def attend(last):
        limit = (last + 1) * BLOCK
        key = lax.broadcasted_iota(jnp.int32, (limit, BLOCK), 0)
        query = last * BLOCK + lax.broadcasted_iota(jnp.int32, (limit, BLOCK), 1)
        allowed = jnp.logical_and(seg_col[:limit, :] == seg_row[...], key <= query)
        fill = jnp.where(allowed, 0.0, NEG_FILL)
        bias[:limit, :BLOCK] = fill
        bias[:limit, BLOCK:] = fill

        def pair(index, carry):
            here = slice(last * BLOCK, limit)
            queries = stack_heads(qkv_ref[here, lanes_of(index)] * jnp.asarray(SCALE, LOW))
            grads = stack_heads(grad_att[:, lanes_of(index)])
            keys = qkv_ref[:limit, lanes_of(index, width)]
            values = qkv_ref[:limit, lanes_of(index, 2 * width)]
            scores = dot(keys, queries, ROWS_BOTH) + bias[:limit, :]
            probs = jnp.exp(scores - lines[pl.ds(index, 1), :])
            grad_probs = dot(values, grads, ROWS_BOTH)
            grad_scores = (probs * (grad_probs - lines[pl.ds(pairs + index, 1), :])).astype(LOW)
            grad_values[:limit, lanes_of(index)] += dot(probs.astype(LOW), grads)
            grad_keys[:limit, lanes_of(index)] += dot(grad_scores, queries)
            grad_query = join_heads(dot(grad_scores, keys, COLS_BOTH)) * SCALE
            grads_ref[:, lanes_of(index)] = grad_query.astype(LOW)
            return carry

        lax.fori_loop(0, pairs, pair, 0)

    for last in range(blocks):
        pl.when(block == last)(functools.partial(attend, last))
    done = rows_of_block(block)
    grads_ref[:, width : 2 * width] = grad_keys[done, :].astype(LOW)
    grads_ref[:, 2 * width :] = grad_values[done, :].astype(LOW)
    part_ref[...] = dot(grads_ref[...], room[: 3 * width, :]).astype(LOW)


def weight_grads_body(first_steps, steps, left_a, right_a, left_b, right_b, one, two, turned):
    step = pl.program_id(0)

    @pl.when(step == 0)
    def _():
        turned[...] = left_a[...].T

    @pl.when(step == first_steps)
    def _():
        turned[...] = left_b[...].T

    cuts = sorted({0, first_steps, steps // 2, steps})
    for start, stop in zip(cuts, cuts[1:]):
        right = right_a if start < first_steps else right_b
        out = one if start < steps // 2 else two

        @pl.when(jnp.logical_and(step >= start, step < stop))
        def _(right=right, out=out):
            out[...] = dot(turned[...], right[...]).astype(LOW)


def input_grad_body(grad_mid, own_ref, other_ref, res_ref, gain_ref, out_ref, low_ref, small_ref):
    @pl.when(pl.program_id(0) == 0)
    def _():
        small_ref[...] = jnp.zeros_like(small_ref)

    grad_normed = add_pair(own_ref, other_ref)
    normal, inverse = spread(res_ref[...].astype(F32))
    add_rows(small_ref, 0, grad_normed * normal)
    grad = grad_mid[...] + norm_back(grad_normed, gain_ref[0:1, :], normal, inverse)
    out_ref[...] = grad
    low_ref[...] = grad.astype(LOW)


def call(body, steps, inputs, outputs, scratch=(), flops=0, limit=56):
    moved = sum(x.size * x.dtype.itemsize for x, _ in inputs)
    return pl.pallas_call(
        body,
        grid=(steps,),
        in_specs=[spec for _, spec in inputs],
        out_specs=[spec for _, _, spec in outputs],
        out_shape=[jax.ShapeDtypeStruct(shape, dtype) for shape, dtype, _ in outputs],
        scratch_shapes=list(scratch),
        compiler_params=pltpu.CompilerParams(
            dimension_semantics=("arbitrary",), vmem_limit_bytes=limit << 20
        ),
        cost_estimate=pl.CostEstimate(flops=flops, bytes_accessed=moved, transcendentals=0),
    )(*[x for x, _ in inputs])


def whole(array):
    return (array, pl.BlockSpec(array.shape, lambda i: (0,) * array.ndim))


def left_there(array):
    return (array, pl.BlockSpec(memory_space=pl.ANY))


def scalars(array):
    return (array, pl.BlockSpec(memory_space=pltpu.SMEM))


def room_for(*weights):
    return [pltpu.VMEM(weight[0].shape, LOW) for weight in weights]


def rows(array):
    return (array, pl.BlockSpec((BLOCK, array.shape[1]), lambda i: (i, 0)))


def rows_out(count, width, dtype):
    return ((count, width), dtype, pl.BlockSpec((BLOCK, width), lambda i: (i, 0)))


def small_out(width):
    return ((8, width), F32, pl.BlockSpec((8, width), lambda i: (0, 0)))


def attention_forward(residual, seg_col, seg_row, gains, flags, weight):
    second = len(residual) > 1
    count, width = residual[0].shape
    local = weight[0].shape[0] // 4
    inputs = [rows(x) for x in residual[:3]] + [whole(x) for x in residual[3:]]
    inputs += [rows(seg_col), whole(seg_row), whole(gains), scalars(flags)]
    inputs += [left_there(x) for x in weight]
    outputs = [rows_out(count, width, F32)] if second else []
    outputs += [
        rows_out(count, width, LOW),
        rows_out(count, 3 * local, LOW),
        rows_out(count, local, LOW),
        ((8, count), F32, pl.BlockSpec((8, BLOCK), lambda i: (0, i))),
        rows_out(count, width, LOW),
    ]
    scratch = [
        pltpu.VMEM((count, local), LOW),
        pltpu.VMEM((count, local), LOW),
        pltpu.VMEM((BLOCK, count), F32),
        *room_for(weight),
        pltpu.SemaphoreType.DMA((4,)),
    ]
    flops = 2 * count * width * 4 * local + 4 * count * count * local
    body = functools.partial(attention_forward_body, second)
    return call(body, count // BLOCK, inputs, outputs, scratch, flops)


def mlp_forward(residual, own, other, gains, flags, up_weight, down_weight):
    count, width = residual.shape
    units = up_weight[0].shape[1]
    inputs = [rows(residual), rows(own), rows(other), whole(gains), scalars(flags)]
    inputs += [left_there(x) for x in up_weight + down_weight]
    scratch = room_for(up_weight, down_weight) + [pltpu.SemaphoreType.DMA((2, 4))]
    outputs = [
        rows_out(count, width, F32),
        rows_out(count, width, LOW),
        rows_out(count, units, LOW),
        rows_out(count, units, LOW),
        rows_out(count, width, LOW),
    ]
    flops = 4 * count * width * units
    return call(mlp_forward_body, count // BLOCK, inputs, outputs, scratch, flops)


def mlp_backward(grad, slope, flags, up_weight, down_weight):
    joined = len(grad) > 1
    count, width = grad[0].shape
    units = up_weight[0].shape[1]
    inputs = [rows(x) for x in grad[:4]] + [whole(x) for x in grad[4:]]
    inputs += [rows(slope), scalars(flags)]
    inputs += [left_there(x) for x in up_weight + down_weight]
    scratch = room_for(up_weight, down_weight) + [pltpu.SemaphoreType.DMA((2, 4))]
    outputs = []
    if joined:
        outputs = [rows_out(count, width, F32), rows_out(count, width, LOW), small_out(width)]
    outputs += [rows_out(count, units, LOW), rows_out(count, width, LOW)]
    body = functools.partial(mlp_backward_body, joined)
    return call(body, count // BLOCK, inputs, outputs, scratch, 4 * count * width * units)


def attention_backward(
    grad, own, other, middle, gains, qkv, attended, logs, seg_col, seg_row, flags, weight
):
    count, width = grad.shape
    local = attended.shape[1]
    steps = count // BLOCK

    def back(array):
        return (array, pl.BlockSpec((BLOCK, array.shape[1]), lambda i: (steps - 1 - i, 0)))

    def back_out(columns, dtype):
        spec = pl.BlockSpec((BLOCK, columns), lambda i: (steps - 1 - i, 0))
        return ((count, columns), dtype, spec)

    inputs = [back(grad), back(own), back(other), back(middle), whole(gains), whole(qkv)]
    inputs += [back(attended)]
    inputs += [(logs, pl.BlockSpec((8, BLOCK), lambda i: (0, steps - 1 - i))), whole(seg_col)]
    inputs += [(seg_row, pl.BlockSpec((1, BLOCK), lambda i: (0, steps - 1 - i)))]
    inputs += [scalars(flags)] + [left_there(x) for x in weight]
    outputs = [
        back_out(width, F32),
        back_out(width, LOW),
        back_out(3 * local, LOW),
        back_out(width, LOW),
        small_out(width),
    ]
    scratch = [
        pltpu.VMEM((BLOCK, local), LOW),
        pltpu.VMEM((count, local), F32),
        pltpu.VMEM((count, local), F32),
        pltpu.VMEM((count, 2 * BLOCK), F32),
        pltpu.VMEM((8, 2 * BLOCK), F32),
        *room_for(weight),
        pltpu.SemaphoreType.DMA((4,)),
    ]
    flops = 2 * count * width * 4 * local + 10 * count * count * local
    return call(attention_backward_body, steps, inputs, outputs, scratch, flops)


def weight_grads(left_a, right_a, left_b, right_b):
    count, width = left_a.shape
    cut = 384
    steps_a, steps_b = right_a.shape[1] // cut, right_b.shape[1] // cut
    total = right_a.shape[1] + right_b.shape[1]
    inputs = [
        whole(left_a),
        (right_a, pl.BlockSpec((count, cut), lambda i: (0, jnp.minimum(i, steps_a - 1)))),
        whole(left_b),
        (right_b, pl.BlockSpec((count, cut), lambda i: (0, jnp.maximum(i - steps_a, 0)))),
    ]
    steps = steps_a + steps_b
    half = steps // 2
    columns = ((width, total // 2), LOW)
    outputs = [
        (*columns, pl.BlockSpec((width, cut), lambda i: (0, jnp.minimum(i, half - 1)))),
        (*columns, pl.BlockSpec((width, cut), lambda i: (0, jnp.maximum(i - half, 0)))),
    ]
    body = functools.partial(weight_grads_body, steps_a, steps)
    scratch = [pltpu.VMEM((width, count), LOW)]
    flops = 2 * count * width * total
    return call(body, steps, inputs, outputs, scratch, flops)


def input_grad(grad_mid, own, other, residual, gains):
    count, width = grad_mid.shape
    inputs = [rows(grad_mid), rows(own), rows(other), rows(residual), whole(gains)]
    outputs = [rows_out(count, width, F32), rows_out(count, width, LOW), small_out(width)]
    return call(input_grad_body, count // BLOCK, inputs, outputs)


def per_device(
    tokens_in,
    segments,
    gains_first,
    qkv_first,
    proj_first,
    up_first,
    down_first,
    pass_embed,
    gains_second,
    qkv_second,
    proj_second,
    up_second,
    down_second,
    cotangent,
):
    dp = lax.axis_index("dp")
    same = (dp & 1) == lax.axis_index("mp")
    flags = jnp.stack([same.astype(jnp.int32), near_piece(dp)])

    def joint(qkv_weight, proj_weight):
        qkv_weight = qkv_weight.transpose(1, 2, 0).reshape(-1, qkv_weight.shape[0])
        return jnp.concatenate([qkv_weight, proj_weight], axis=0)

    weights = [
        joint(qkv_first, proj_first),
        up_first,
        down_first,
        joint(qkv_second, proj_second),
        up_second,
        down_second,
    ]
    tokens_in = own_run(tokens_in, same)
    segments = own_run(segments, same)
    came_att1, came_up1, came_down1, came_att2, came_up2, came_down2 = map(start_halves, weights)
    own_att1, own_up1, own_down1, own_att2, own_up2, own_down2 = weights
    cotangent = own_run(cotangent, same)
    seg_col, seg_row = segments[:, None], segments[None, :]

    att_w1 = (own_att1, *relay(came_att1))
    relay_up1 = relay(came_up1)
    tokens_in, came_up1 = tie(tokens_in, came_up1)
    normed_a1, qkv1, att1, logs1, part = attention_forward(
        (tokens_in,), seg_col, seg_row, gains_first, flags, att_w1
    )
    part, relay_up1, came_down1, came_att2 = tie(part, relay_up1, came_down1, came_att2)
    up_w1 = (own_up1, *relay_up1)
    down_w1 = (own_down1, *relay(came_down1))
    relay_att2 = relay(came_att2)
    mid1, normed_b1, hidden1, slope1, part = mlp_forward(
        tokens_in, part, from_core(part), gains_first, flags, up_w1, down_w1
    )
    part, relay_att2, came_up2 = tie(part, relay_att2, came_up2)
    att_w2 = (own_att2, *relay_att2)
    relay_up2 = relay(came_up2)
    joined, normed_a2, qkv2, att2, logs2, part = attention_forward(
        (mid1, part, from_core(part), pass_embed),
        seg_col, seg_row, gains_second, flags, att_w2,
    )
    part, relay_up2, came_down2, cotangent = tie(part, relay_up2, came_down2, cotangent)
    up_w2 = (own_up2, *relay_up2)
    down_w2 = (own_down2, *relay(came_down2))
    mid2, normed_b2, hidden2, slope2, part = mlp_forward(
        joined, part, from_core(part), gains_second, flags, up_w2, down_w2
    )
    top = mid2 + (part.astype(F32) + from_core(part).astype(F32))
    output = to_mesh_rows(top.astype(LOW), same)

    pre2, part = mlp_backward((cotangent,), slope2, flags, up_w2, down_w2)
    other = from_core(part)
    mlp2 = Reduction(weight_grads(cotangent, hidden2, normed_b2, pre2), same)
    other, mlp2.pair, output = tie(other, mlp2.pair, output)
    sums = mlp2.first()
    gm2, gm_low2, grad_rows2, part, small_b2 = attention_backward(
        cotangent, part, other, mid2, gains_second, qkv2, att2, logs2, seg_col, seg_row,
        flags, att_w2,
    )
    part, gm_low2, mlp2.pair = tie(part, gm_low2, sums)
    other = from_core(part)
    sums = mlp2.second()
    att_2 = Reduction(weight_grads(gm_low2, att2, normed_a2, grad_rows2), same)
    other, att_2.pair, mlp2.pair = tie(other, att_2.pair, sums)
    sums = (mlp2.further(), att_2.first())
    grad, grad_low, small_a2, pre1, part = mlp_backward(
        (gm2, part, other, joined, gains_second), slope1, flags, up_w1, down_w1
    )
    part, grad_low, (mlp2.pair, att_2.pair) = tie(part, grad_low, sums)
    other = from_core(part)
    sums = (mlp2.further(), att_2.second())
    mlp1 = Reduction(weight_grads(grad_low, hidden1, normed_b1, pre1), same)
    other, mlp1.pair, (mlp2.pair, att_2.pair) = tie(other, mlp1.pair, sums)
    sums = (att_2.further(), mlp1.first())
    gm1, gm_low1, grad_rows1, part, small_b1 = attention_backward(
        grad, part, other, mid1, gains_first, qkv1, att1, logs1, seg_col, seg_row,
        flags, att_w1,
    )
    part, gm_low1, (att_2.pair, mlp1.pair) = tie(part, gm_low1, sums)
    other = from_core(part)
    sums = (att_2.further(), mlp1.second())
    att_1 = Reduction(weight_grads(gm_low1, att1, normed_a1, grad_rows1), same)
    other, att_1.pair, (att_2.pair, mlp1.pair) = tie(other, att_1.pair, sums)
    sums = (mlp1.further(), att_1.first())
    grad_in, grad_in_low, small_a1 = input_grad(gm1, part, other, tokens_in, gains_first)
    grad_in_low, (mlp1.pair, att_1.pair) = tie(grad_in_low, sums)
    grad_input = to_mesh_rows(grad_in_low, same).astype(F32)
    grad_input = jnp.where(same, grad_in, grad_input)
    att_1.second()

    small = jnp.concatenate([small_a1[:1], small_b1[:1], small_a2[1:3], small_a2[:1], small_b2[:1]])
    runs = lax.axis_size("dp")
    for bit in range(1, runs.bit_length() - 1):
        small = small + lax.ppermute(small, "dp", [(i, i ^ (1 << bit)) for i in range(runs)])
    small = small + lax.ppermute(small, "mp", [(0, 1), (1, 0)])
    width = small.shape[1] // runs
    small = lax.dynamic_slice_in_dim(small, dp * width, width, 1)

    def placed(mlp, att):
        local = att1.shape[1]
        down, up = mlp.rest()
        proj_qkv = jnp.concatenate(att.rest(), axis=1)
        return proj_qkv[:, local:].reshape(-1, 3, local), proj_qkv[:, :local].T, up, down.T

    second = placed(mlp2, att_2)
    first = placed(mlp1, att_1)
    return (
        output,
        grad_input,
        small[:2],
        *first,
        small[2:4],
        small[4:],
        *second,
    )


def solution(mesh):
    placed = (
        P("dp", None),
        P("dp"),
        P(),
        P(None, None, "mp"),
        P("mp", None),
        P(None, "mp"),
        P("mp", None),
        P(),
        P(),
        P(None, None, "mp"),
        P("mp", None),
        P(None, "mp"),
        P("mp", None),
        P("dp", None),
    )
    return jax.shard_map(
        per_device,
        mesh=mesh,
        in_specs=placed,
        out_specs=(
            P("dp", None),
            P("dp", None),
            P(None, "dp"),
            P("dp", None, "mp"),
            P("mp", "dp"),
            P("dp", "mp"),
            P("mp", "dp"),
            P(None, "dp"),
            P(None, "dp"),
            P("dp", None, "mp"),
            P("mp", "dp"),
            P("dp", "mp"),
            P("mp", "dp"),
        ),
        check_vma=False,
    )
```

time: 744 us -> 462 us (0.62)
  Pallas kernels: 0 us -> 210 us
  matrix products: 192 us -> 0 us
  starting transfers between devices: 205 us -> 121 us
  waiting for transfers between devices: 125 us -> 49.4 us
  other arithmetic: 97.1 us -> 23.7 us
  blocking collectives: 51.3 us -> 0 us
  local copies, waits for them, and re-layouts: 57.4 us -> 46.3 us
    pallas_call x0 -> x13, Pallas kernels: none -> 210 us  [call(): pl.pallas_call(body, grid=(steps,), in_specs=[spec for _, spec in inputs]...]
    dot_general x50 -> x0, matrix products: 192 us -> none  [the longest x2 28.6 us: layer_backward(): jnp.einsum('rd,fd->rf', grad_low, down_weight, preferred_element_type=jnp...]
    ppermute x32 -> x38, starting transfers between devices: 108 us -> 41.1 us  [the longest x12 11.3 us: from_neighbour(): lax.ppermute(values, BOTH, moves(lambda dp, mp: (dp ^ 1 << bit, mp) if dp...]
    psum x1 -> x0, blocking collectives: 51.3 us -> none  [per_device(): lax.psum(jnp.concatenate([small_second, first_grads[5]], axis=0), BOTH)]
    ppermute x24 -> x16, waiting for transfers between devices: 76.6 us -> 26.2 us  [fold(): lax.ppermute(send, 'dp', [(i, i ^ 1 << bit) for i in range(lax.axis_size(...]
    convert_element_type x15 -> x9, other arithmetic: 41.6 us -> 6.1 us  [the longest x8 3.27 us: cross(): (round_trip.astype(jnp.float32) + other.astype(jnp.float32)).astype(dtype)]
    reduce_sum x20 -> x0, other arithmetic: 29.4 us -> none  [the longest x6 12.7 us: layer_norm(): centered = values - jnp.mean(values, axis=-1, keepdims=True)]
    ppermute x32 -> x38, waiting for transfers between devices: 47.5 us -> 18.7 us  [the longest x1 10.9 us: per_device(): small = small + lax.ppermute(small, 'mp', [(0, 1), (1, 0)])]
  transfers between devices with their start and end apart: 69 -> 67, of which waited for: 22 -> 12; matrix products, arithmetic and copies ran while one was open for 40% -> 10% of each run, Pallas kernels for 0% -> 41%
where the time goes in v2:
time: 462 us; the launch traced here: 453 us
  Pallas kernels  210 us (45%)
  starting transfers between devices  121 us (26%)
  waiting for transfers between devices  49.4 us (11%)
  local copies, waits for them, and re-layouts  46.3 us (10%)
  other arithmetic  23.7 us (5%)
    pallas_call x13, Pallas kernels, call(): pl.pallas_call(body, grid=(steps,), in_specs=[spec for _, spec in inputs]...  210 us
    ppermute x8, starting transfers between devices, from_core(): return lax.ppermute(values, BOTH, moves(lambda dp, mp: (dp ^ 1, mp)))  38.5 us
    ppermute x16, waiting for transfers between devices, fold(): lax.ppermute(send, 'dp', [(i, i ^ 1 << bit) for i in range(lax.axis_size(...  26.2 us
    ppermute x3, starting transfers between devices, own_run(): lax.ppermute(values, BOTH, moves(lambda dp, mp: (dp ^ 1, mp) if dp & 1 !=...  22.9 us
    ppermute x16, starting transfers between devices, fold(): lax.ppermute(send, 'dp', [(i, i ^ 1 << bit) for i in range(lax.axis_size(...  16.7 us
    ppermute x12, starting transfers between devices, from_neighbour(): lax.ppermute(values, BOTH, moves(lambda dp, mp: (dp ^ 1 << bit, mp) if dp...  11.3 us
    ppermute x1, waiting for transfers between devices, per_device(): small = small + lax.ppermute(small, 'mp', [(0, 1), (1, 0)])  10.9 us
    unnamed x86, local copies, waits for them, and re-layouts  10.3 us
  transfers between devices with their start and end apart: 67, of which 12 were waited for; matrix products, arithmetic and copies ran while one was open for 10% of the time, Pallas kernels for 41%

profile of v2, /device:TPU:0, one launch (start us, length us, event | category | flops | bytes accessed | tf_op | source)
XLA Modules:
  0.0 452.5 jit_solution(7505828211155632212)
XLA Ops:
  0.7 2.7 copy.45
  4.7 1.9 collective-permute-start.3
  8.5 7.5 %collective-permute-start = (bf16[1024,768]{1,0:T(8,128)(2,1)}, bf16[1024,768]{1,0:T(8,128)(2,1)}, u32[]{:S(2)}, u32[]{:S(2)}) collective-permute-start(bf16[1024,768]{1,0:T(8,128)(2,1)} %param.14), channel_id=1, source_target_pairs={{3,1},{0,2},{7,5},{4,6},{11,9},{8,10},{15,13},{12,14},{19,17},{16,... | collective-permute-start | bytes 4718600 | tf_op jit(solution)/shard_map/ppermute | solution.py:40
  17.3 2.7 copy.47
  22.7 1.7 collective-permute-start.9
  26.8 2.1 fusion.22
  33.7 2.8 broadcast_select_fusion.2.refs_0_.res_ref
  37.3 22.1 %shard_map.237 = (bf16[1024,768]{1,0:T(8,128)(2,1)}, bf16[1024,1152]{1,0:T(8,128)(2,1)}, bf16[1024,384]{1,0:T(8,128)(2,1)}, f32[8,1024]{1,0:T(8,128)}, bf16[1024,768]{1,0:T(8,128)(2,1)}) custom-call(bf16[1024,768]{1,0:T(8,128)(2,1)} %broadcast_select_fusion.2.refs_0_.res_ref, s32[1024,1]{1,0:T(8,128)} %copy.46.refs_1_.refs_4_.seg_col, s32[1,1024]{1,0:T(1,128)} %bitcast.233, ...), custom_call_target="tpu_custom_call" | custom-call | flops 4026531840 | bytes 6305800 | tf_op jit(solution)/shard_map/pallas_call | solution.py:500
  59.4 11.6 %collective-permute-start.10 = (bf16[1024,768]{1,0:T(8,128)(2,1)}, bf16[1024,768]{1,0:T(8,128)(2,1)}, u32[]{:S(2)}, u32[]{:S(2)}) collective-permute-start(bf16[1024,768]{1,0:T(8,128)(2,1)} %get-tuple-element.118.own_ref), channel_id=1, source_target_pairs={{2,0},{3,1},{0,2},{1,3},{6,4},{7,5},{4,6},{5,7},{10,8},{11,9},{8,1... | collective-permute-start | bytes 4718600 | tf_op jit(solution)/shard_map/ppermute | solution.py:36
  77.9 14.1 %collective-permute-start.20 = (bf16[1024,768]{1,0:T(8,128)(2,1)S(1)}, bf16[1024,768]{1,0:T(8,128)(2,1)S(1)}, u32[]{:S(2)}, u32[]{:S(2)}) collective-permute-start(bf16[1024,768]{1,0:T(8,128)(2,1)S(1)} %copy-done.12), channel_id=1, source_target_pairs={{3,1},{0,2},{7,5},{4,6},{11,9},{8,10},{15,13},{12,14},{19,17},{16,... | collective-permute-start | bytes 4718600 | tf_op jit(solution)/shard_map/ppermute | solution.py:40
  92.1 15.7 %shard_map.238 = (f32[1024,768]{1,0:T(8,128)}, bf16[1024,768]{1,0:T(8,128)(2,1)}, bf16[1024,1536]{1,0:T(8,128)(2,1)}, bf16[1024,1536]{1,0:T(8,128)(2,1)}, bf16[1024,768]{1,0:T(8,128)(2,1)}) custom-call(bf16[1024,768]{1,0:T(8,128)(2,1)} %broadcast_select_fusion.2.refs_0_.res_ref, bf16[1024,768]{1,0:T(8,128)(2,1)} %get-tuple-element.118.own_ref, ...), custom_call_target="tpu_custom_call" | custom-call | flops 4831838208 | bytes 14161928 | tf_op jit(solution)/shard_map/pallas_call | solution.py:500
  107.9 1.7 dynamic-slice_bitcast_fusion.2
  113.2 23.0 %shard_map.239 = (f32[1024,768]{1,0:T(8,128)}, bf16[1024,768]{1,0:T(8,128)(2,1)}, bf16[1024,1152]{1,0:T(8,128)(2,1)}, bf16[1024,384]{1,0:T(8,128)(2,1)}, f32[8,1024]{1,0:T(8,128)}, /*index=5*/bf16[1024,768]{1,0:T(8,128)(2,1)}) custom-call(f32[1024,768]{1,0:T(8,128)} %get-tuple-element.123.refs_0_.mid_ref, bf16[1024,768]{1,0:T(8,128)(2,1)} %get-tuple-element.126.refs_1_, ...), custom_call_target="tpu_custom_call" | custom-call | flops 4026531840 | bytes 11027464 | tf_op jit(solution)/shard_map/pallas_call | solution.py:500
  136.2 6.9 %collective-permute-start.21 = (bf16[1024,768]{1,0:T(8,128)(2,1)}, bf16[1024,768]{1,0:T(8,128)(2,1)S(1)}, u32[]{:S(2)}, u32[]{:S(2)}) collective-permute-start(bf16[1024,768]{1,0:T(8,128)(2,1)} %get-tuple-element.134.own_ref), channel_id=1, source_target_pairs={{2,0},{3,1},{0,2},{1,3},{6,4},{7,5},{4,6},{5,7},{10,8},{11,9},{8,1... | collective-permute-start | bytes 4718600 | tf_op jit(solution)/shard_map/ppermute | solution.py:36
  147.5 15.8 %shard_map.240 = (f32[1024,768]{1,0:T(8,128)}, bf16[1024,768]{1,0:T(8,128)(2,1)}, bf16[1024,1536]{1,0:T(8,128)(2,1)}, bf16[1024,1536]{1,0:T(8,128)(2,1)}, bf16[1024,768]{1,0:T(8,128)(2,1)}) custom-call(f32[1024,768]{1,0:T(8,128)} %get-tuple-element.133.res_ref.refs_3_, bf16[1024,768]{1,0:T(8,128)(2,1)} %get-tuple-element.134.own_ref, ...), custom_call_target="tpu_custom_call" | custom-call | flops 4831838208 | bytes 15734792 | tf_op jit(solution)/shard_map/pallas_call | solution.py:500
  163.3 10.8 %collective-permute-start.25 = (bf16[1024,768]{1,0:T(8,128)(2,1)}, bf16[1024,768]{1,0:T(8,128)(2,1)S(1)}, u32[]{:S(2)}, u32[]{:S(2)}) collective-permute-start(bf16[1024,768]{1,0:T(8,128)(2,1)} %get-tuple-element.147), channel_id=1, source_target_pairs={{2,0},{3,1},{0,2},{1,3},{6,4},{7,5},{4,6},{5,7},{10,8},{11,9},{8,1... | collective-permute-start | bytes 4718600 | tf_op jit(solution)/shard_map/ppermute | solution.py:36
  174.2 3.2 collective-permute-done.25
  177.4 2.8 add_convert_fusion
  181.0 12.1 %shard_map.241 = (bf16[1024,1536]{1,0:T(8,128)(2,1)}, bf16[1024,768]{1,0:T(8,128)(2,1)}) custom-call(bf16[1024,768]{1,0:T(8,128)(2,1)} %broadcast_select_fusion.1.refs_0_.left_a.grad_ref, bf16[1024,1536]{1,0:T(8,128)(2,1)} %get-tuple-element.139.refs_1_, s32[2]{0:T(128)} %pad_add_fusion.refs_4_.flags.refs_7_.refs_2_.refs_6_, bf16[768,1536]{1,0:T(8,128)(2,1)} %refs_3_.5, ...), custom_call_target="tpu_custom_call" | custom-call | flops 4831838208 | bytes 14155784 | tf_op jit(solution)/shard_map/pallas_call | solution.py:500
  193.1 3.9 collective-permute-start.24
  197.0 13.4 %shard_map.242 = (bf16[768,1536]{1,0:T(8,128)(2,1)}, bf16[768,1536]{1,0:T(8,128)(2,1)}) custom-call(bf16[1024,768]{1,0:T(8,128)(2,1)} %broadcast_select_fusion.1.refs_0_.left_a.grad_ref, bf16[1024,1536]{1,0:T(8,128)(2,1)} %get-tuple-element.141.right_a, bf16[1024,768]{1,0:T(8,128)(2,1)} %get-tuple-element.142.left_b, ...), custom_call_target="tpu_custom_call" | custom-call | flops 4831838208 | bytes 9437184 | tf_op jit(solution)/shard_map/pallas_call | solution.py:500
  216.8 1.8 collective-permute-start.28
  218.7 27.6 %shard_map.243 = (f32[1024,768]{1,0:T(8,128)}, bf16[1024,768]{1,0:T(8,128)(2,1)}, bf16[1024,1152]{1,0:T(8,128)(2,1)}, bf16[1024,768]{1,0:T(8,128)(2,1)}, f32[8,768]{1,0:T(8,128)}) custom-call(bf16[1024,768]{1,0:T(8,128)(2,1)} %broadcast_select_fusion.1.refs_0_.left_a.grad_ref, bf16[1024,768]{1,0:T(8,128)(2,1)} %get-tuple-element.140.own_ref, ...), custom_call_target="tpu_custom_call" | custom-call | flops 6442450944 | bytes 15775752 | tf_op jit(solution)/shard_map/pallas_call | solution.py:500
  248.9 1.7 add_convert_fusion.2
  253.0 2.4 collective-permute-start.32
  256.2 1.7 collective-permute-start.30
  258.0 8.7 %shard_map.244 = (bf16[768,768]{1,0:T(8,128)(2,1)}, bf16[768,768]{1,0:T(8,128)(2,1)}) custom-call(bf16[1024,768]{1,0:T(8,128)(2,1)} %get-tuple-element.159.left_a, bf16[1024,384]{1,0:T(8,128)(2,1)} %get-tuple-element.151.att_ref.right_a, bf16[1024,768]{1,0:T(8,128)(2,1)} %get-tuple-element.160.left_b, bf16[1024,1152]{1,0:T(8,128)(2,1)} %get-tuple-element.161.right_b), custom_call_target="tpu_custom_call" | custom-call | flops 2415919104 | bytes 6291456 | tf_op jit(solution)/shard_map/pallas_call | solution.py:500
  274.7 15.0 %shard_map.245 = (f32[1024,768]{1,0:T(8,128)}, bf16[1024,768]{1,0:T(8,128)(2,1)}, f32[8,768]{1,0:T(8,128)}, bf16[1024,1536]{1,0:T(8,128)(2,1)}, bf16[1024,768]{1,0:T(8,128)(2,1)}) custom-call(f32[1024,768]{1,0:T(8,128)} %get-tuple-element.153.refs_0_, bf16[1024,768]{1,0:T(8,128)(2,1)} %get-tuple-element.158.refs_1_, bf16[1024,768]{1,0:T(8,128)(2,1)} %copy-done.17, ...), custom_call_target="tpu_custom_call" | custom-call | flops 4831838208 | bytes 22026248 | tf_op jit(solution)/shard_map/pallas_call | solution.py:500
  293.7 2.4 collective-permute-start.41
  296.9 2.7 collective-permute-start.39
  301.1 13.4 %shard_map.246 = (bf16[768,1536]{1,0:T(8,128)(2,1)}, bf16[768,1536]{1,0:T(8,128)(2,1)}) custom-call(bf16[1024,768]{1,0:T(8,128)(2,1)} %get-tuple-element.175.left_a, bf16[1024,1536]{1,0:T(8,128)(2,1)} %get-tuple-element.176.right_a, bf16[1024,768]{1,0:T(8,128)(2,1)} %get-tuple-element.177.left_b, bf16[1024,1536]{1,0:T(8,128)(2,1)} %get-tuple-element.178.right_b), custom_call_target="tpu_custom_call" | custom-call | flops 4831838208 | bytes 9437184 | tf_op jit(solution)/shard_map/pallas_call | solution.py:500
  323.3 27.5 %shard_map.247 = (f32[1024,768]{1,0:T(8,128)}, bf16[1024,768]{1,0:T(8,128)(2,1)}, bf16[1024,1152]{1,0:T(8,128)(2,1)}, bf16[1024,768]{1,0:T(8,128)(2,1)}, f32[8,768]{1,0:T(8,128)}) custom-call(f32[1024,768]{1,0:T(8,128)} %get-tuple-element.168.grad_ref, bf16[1024,768]{1,0:T(8,128)(2,1)} %get-tuple-element.174.own_ref, bf16[1024,768]{1,0:T(8,128)(2,1)} %copy-done.36, ...), custom_call_target="tpu_custom_call" | custom-call | flops 6442450944 | bytes 17348616 | tf_op jit(solution)/shard_map/pallas_call | solution.py:500
  353.4 1.6 fusion
  357.9 2.8 collective-permute-start.50
  363.4 1.9 collective-permute-start.47
  365.4 8.6 %shard_map.248 = (bf16[768,768]{1,0:T(8,128)(2,1)}, bf16[768,768]{1,0:T(8,128)(2,1)}) custom-call(bf16[1024,768]{1,0:T(8,128)(2,1)} %get-tuple-element.195.left_a, bf16[1024,384]{1,0:T(8,128)(2,1)} %get-tuple-element.186.att_ref.right_a, bf16[1024,768]{1,0:T(8,128)(2,1)} %get-tuple-element.196.left_b, bf16[1024,1152]{1,0:T(8,128)(2,1)} %get-tuple-element.197.right_b), custom_call_target="tpu_custom_call" | custom-call | flops 2415919104 | bytes 6291456 | tf_op jit(solution)/shard_map/pallas_call | solution.py:500
  377.0 6.9 %shard_map.249 = (f32[1024,768]{1,0:T(8,128)}, bf16[1024,768]{1,0:T(8,128)(2,1)}, f32[8,768]{1,0:T(8,128)}) custom-call(f32[1024,768]{1,0:T(8,128)} %get-tuple-element.188.grad_mid, bf16[1024,768]{1,0:T(8,128)(2,1)} %get-tuple-element.194.own_ref, bf16[1024,768]{1,0:T(8,128)(2,1)} %copy-done.15, bf16[1024,768]{1,0:T(8,128)(2,1)} %broadcast_select_fusion.2.refs_0_.res_ref, ...), custom_call_target="tpu_custom_call" | custom-call | bytes 7870464 | tf_op jit(solution)/shard_map/pallas_call | solution.py:500
  386.4 2.4 collective-permute-done.57
  392.6 2.5 collective-permute-start.59
  397.3 2.0 collective-permute-start.60
  401.1 10.9 %collective-permute-done.60 = f32[6,768]{1,0:T(8,128)S(1)} collective-permute-done((f32[6,768]{1,0:T(8,128)S(1)}, f32[6,768]{1,0:T(8,128)S(1)}, u32[]{:S(2)}, u32[]{:S(2)}) %collective-permute-start.60) | collective-permute-done | bytes 18464 | tf_op jit(solution)/shard_map/ppermute | solution.py:784
  412.8 2.0 collective-permute-done.52
  418.4 3.6 collective-permute-done.62
  422.2 1.7 collective-permute-done.61
  424.9 8.7 %collective-permute-done.66 = bf16[48,3072]{1,0:T(8,128)(2,1)S(1)} collective-permute-done((bf16[48,3072]{1,0:T(8,128)(2,1)S(1)}, bf16[48,3072]{1,0:T(8,128)(2,1)S(1)}, u32[]{:S(2)}, u32[]{:S(2)}) %collective-permute-start.66) | collective-permute-done | bytes 294944 | tf_op jit(solution)/shard_map/ppermute | solution.py:92
  433.7 4.9 %collective-permute-done.64 = bf16[2,48,1536]{2,1,0:T(8,128)(2,1)S(1)} collective-permute-done((bf16[2,48,1536]{2,1,0:T(8,128)(2,1)S(1)}, bf16[2,48,1536]{2,1,0:T(8,128)(2,1)S(1)}, u32[]{:S(2)}, u32[]{:S(2)}) %collective-permute-start.64) | collective-permute-done | bytes 294944 | tf_op jit(solution)/shard_map/ppermute | solution.py:92
  439.7 8.8 %collective-permute-done.65 = bf16[48,1536]{1,0:T(8,128)(2,1)S(1)} collective-permute-done((bf16[48,1536]{1,0:T(8,128)(2,1)S(1)}, bf16[48,1536]{1,0:T(8,128)(2,1)S(1)}, u32[]{:S(2)}, u32[]{:S(2)}) %collective-permute-start.65) | collective-permute-done | bytes 147488 | tf_op jit(solution)/shard_map/ppermute | solution.py:92
  449.9 2.1 convert_select_fusion
  (296 shorter events, 95.0 us)
Async XLA Ops:
  4.7 21.4 %collective-permute-start.3 = (bf16[768,768]{1,0:T(8,128)(2,1)}, bf16[768,768]{1,0:T(8,128)(2,1)}, u32[]{:S(2)}, u32[]{:S(2)}) collective-permute-start(bf16[768,768]{1,0:T(8,128)(2,1)} %dynamic-slice_bitcast_fusion.6), channel_id=1, source_target_pairs={{2,1},{1,2},{6,5},{5,6},{10,9},{9,10},{14,13},{13,14},{18,17},{17,... | collective-permute-start | bytes 3538952 | tf_op jit(solution)/shard_map/ppermute | solution.py:55
  7.8 23.7 %collective-permute-start.1 = (bf16[384,1536]{1,0:T(8,128)(2,1)}, bf16[384,1536]{1,0:T(8,128)(2,1)S(1)}, u32[]{:S(2)}, u32[]{:S(2)}) collective-permute-start(bf16[384,1536]{1,0:T(8,128)(2,1)} %dynamic-slice_bitcast_fusion.7), channel_id=1, source_target_pairs={{2,1},{1,2},{6,5},{5,6},{10,9},{9,10},{14,13},{13,14},{18,17},{17,... | collective-permute-start | bytes 3538952 | tf_op jit(solution)/shard_map/ppermute | solution.py:55
  8.5 23.7 %collective-permute-start = (bf16[1024,768]{1,0:T(8,128)(2,1)}, bf16[1024,768]{1,0:T(8,128)(2,1)}, u32[]{:S(2)}, u32[]{:S(2)}) collective-permute-start(bf16[1024,768]{1,0:T(8,128)(2,1)} %param.14), channel_id=1, source_target_pairs={{3,1},{0,2},{7,5},{4,6},{11,9},{8,10},{15,13},{12,14},{19,17},{16,... | collective-permute-start | bytes 4718600 | tf_op jit(solution)/shard_map/ppermute | solution.py:40
  16.0 12.9 %collective-permute-start.2 = (s32[1024]{0:T(1024)S(1)}, s32[1024]{0:T(1024)S(1)}, u32[]{:S(2)}, u32[]{:S(2)}) collective-permute-start(s32[1024]{0:T(1024)S(1)} %copy-done.34), channel_id=1, source_target_pairs={{3,1},{0,2},{7,5},{4,6},{11,9},{8,10},{15,13},{12,14},{19,17},{16,... | collective-permute-start | bytes 12296 | tf_op jit(solution)/shard_map/ppermute | solution.py:40
  22.7 36.7 %collective-permute-start.9 = (bf16[768,768]{1,0:T(8,128)(2,1)}, bf16[768,768]{1,0:T(8,128)(2,1)}, u32[]{:S(2)}, u32[]{:S(2)}) collective-permute-start(bf16[768,768]{1,0:T(8,128)(2,1)} %dynamic-slice_bitcast_fusion.4), channel_id=1, source_target_pairs={{2,1},{1,2},{6,5},{5,6},{10,9},{9,10},{14,13},{13,14},{18,17},{17,... | collective-permute-start | bytes 3538952 | tf_op jit(solution)/shard_map/ppermute | solution.py:55
  26.0 33.4 %collective-permute-start.8 = (bf16[768,768]{1,0:T(8,128)(2,1)}, bf16[768,768]{1,0:T(8,128)(2,1)S(1)}, u32[]{:S(2)}, u32[]{:S(2)}) collective-permute-start(bf16[768,768]{1,0:T(8,128)(2,1)} %dynamic-slice_bitcast_fusion.5), channel_id=1, source_target_pairs={{2,1},{1,2},{6,5},{5,6},{10,9},{9,10},{14,13},{13,14},{18,17},{17,... | collective-permute-start | bytes 3538952 | tf_op jit(solution)/shard_map/ppermute | solution.py:55
  32.2 27.2 %collective-permute-start.6 = (bf16[192,1536]{1,0:T(8,128)(2,1)S(1)}, bf16[192,1536]{1,0:T(8,128)(2,1)S(1)}, u32[]{:S(2)}, u32[]{:S(2)}) collective-permute-start(bf16[192,1536]{1,0:T(8,128)(2,1)S(1)} %get-tuple-element.253), channel_id=1, source_target_pairs={{5,1},{6,2},{1,5},{2,6},{13,9},{14,10},{9,13},{10,14},{21,17},{22,... | collective-permute-start | bytes 1769480 | tf_op jit(solution)/shard_map/ppermute | solution.py:70
  33.0 26.5 %collective-permute-start.7 = (bf16[192,1536]{1,0:T(8,128)(2,1)S(1)}, bf16[192,1536]{1,0:T(8,128)(2,1)S(1)}, u32[]{:S(2)}, u32[]{:S(2)}) collective-permute-start(bf16[192,1536]{1,0:T(8,128)(2,1)S(1)} %get-tuple-element.252), channel_id=1, source_target_pairs={{9,1},{10,2},{13,5},{14,6},{1,9},{2,10},{5,13},{6,14},{25,17},{26,... | collective-permute-start | bytes 1769480 | tf_op jit(solution)/shard_map/ppermute | solution.py:70
  59.4 32.6 %collective-permute-start.10 = (bf16[1024,768]{1,0:T(8,128)(2,1)}, bf16[1024,768]{1,0:T(8,128)(2,1)}, u32[]{:S(2)}, u32[]{:S(2)}) collective-permute-start(bf16[1024,768]{1,0:T(8,128)(2,1)} %get-tuple-element.118.own_ref), channel_id=1, source_target_pairs={{2,0},{3,1},{0,2},{1,3},{6,4},{7,5},{4,6},{5,7},{10,8},{11,9},{8,1... | collective-permute-start | bytes 4718600 | tf_op jit(solution)/shard_map/ppermute | solution.py:36
  71.2 36.6 %collective-permute-start.15 = (bf16[384,1536]{1,0:T(8,128)(2,1)S(1)}, bf16[384,1536]{1,0:T(8,128)(2,1)S(1)}, u32[]{:S(2)}, u32[]{:S(2)}) collective-permute-start(bf16[384,1536]{1,0:T(8,128)(2,1)S(1)} %dynamic-slice_bitcast_fusion.3), channel_id=1, source_target_pairs={{2,1},{1,2},{6,5},{5,6},{10,9},{9,10},{14,13},{13,14},{18,17},{17,... | collective-permute-start | bytes 3538952 | tf_op jit(solution)/shard_map/ppermute | solution.py:55
  74.9 32.9 %collective-permute-start.13 = (bf16[384,768]{1,0:T(8,128)(2,1)S(1)}, bf16[384,768]{1,0:T(8,128)(2,1)}, u32[]{:S(2)}, u32[]{:S(2)}) collective-permute-start(bf16[384,768]{1,0:T(8,128)(2,1)S(1)} %get-tuple-element.249), channel_id=1, source_target_pairs={{5,1},{6,2},{1,5},{2,6},{13,9},{14,10},{9,13},{10,14},{21,17},{22,... | collective-permute-start | bytes 1769480 | tf_op jit(solution)/shard_map/ppermute | solution.py:70
  76.4 31.4 %collective-permute-start.14 = (bf16[384,768]{1,0:T(8,128)(2,1)S(1)}, bf16[384,768]{1,0:T(8,128)(2,1)}, u32[]{:S(2)}, u32[]{:S(2)}) collective-permute-start(bf16[384,768]{1,0:T(8,128)(2,1)S(1)} %get-tuple-element.248), channel_id=1, source_target_pairs={{9,1},{10,2},{13,5},{14,6},{1,9},{2,10},{5,13},{6,14},{25,17},{26,... | collective-permute-start | bytes 1769480 | tf_op jit(solution)/shard_map/ppermute | solution.py:70
  77.9 34.0 %collective-permute-start.20 = (bf16[1024,768]{1,0:T(8,128)(2,1)S(1)}, bf16[1024,768]{1,0:T(8,128)(2,1)S(1)}, u32[]{:S(2)}, u32[]{:S(2)}) collective-permute-start(bf16[1024,768]{1,0:T(8,128)(2,1)S(1)} %copy-done.12), channel_id=1, source_target_pairs={{3,1},{0,2},{7,5},{4,6},{11,9},{8,10},{15,13},{12,14},{19,17},{16,... | collective-permute-start | bytes 4718600 | tf_op jit(solution)/shard_map/ppermute | solution.py:40
  109.6 26.6 %collective-permute-start.19 = (bf16[768,768]{1,0:T(8,128)(2,1)S(1)}, bf16[768,768]{1,0:T(8,128)(2,1)S(1)}, u32[]{:S(2)}, u32[]{:S(2)}) collective-permute-start(bf16[768,768]{1,0:T(8,128)(2,1)S(1)} %dynamic-slice_bitcast_fusion.2), channel_id=1, source_target_pairs={{2,1},{1,2},{6,5},{5,6},{10,9},{9,10},{14,13},{13,14},{18,17},{17,... | collective-permute-start | bytes 3538952 | tf_op jit(solution)/shard_map/ppermute | solution.py:55
  110.4 25.8 %collective-permute-start.17 = (bf16[192,1536]{1,0:T(8,128)(2,1)S(1)}, bf16[192,1536]{1,0:T(8,128)(2,1)S(1)}, u32[]{:S(2)}, u32[]{:S(2)}) collective-permute-start(bf16[192,1536]{1,0:T(8,128)(2,1)S(1)} %get-tuple-element.247), channel_id=1, source_target_pairs={{5,1},{6,2},{1,5},{2,6},{13,9},{14,10},{9,13},{10,14},{21,17},{22,... | collective-permute-start | bytes 1769480 | tf_op jit(solution)/shard_map/ppermute | solution.py:70
  111.1 25.1 %collective-permute-start.18 = (bf16[192,1536]{1,0:T(8,128)(2,1)S(1)}, bf16[192,1536]{1,0:T(8,128)(2,1)S(1)}, u32[]{:S(2)}, u32[]{:S(2)}) collective-permute-start(bf16[192,1536]{1,0:T(8,128)(2,1)S(1)} %get-tuple-element.246), channel_id=1, source_target_pairs={{9,1},{10,2},{13,5},{14,6},{1,9},{2,10},{5,13},{6,14},{25,17},{26,... | collective-permute-start | bytes 1769480 | tf_op jit(solution)/shard_map/ppermute | solution.py:70
  163.3 14.1 %collective-permute-start.25 = (bf16[1024,768]{1,0:T(8,128)(2,1)}, bf16[1024,768]{1,0:T(8,128)(2,1)S(1)}, u32[]{:S(2)}, u32[]{:S(2)}) collective-permute-start(bf16[1024,768]{1,0:T(8,128)(2,1)} %get-tuple-element.147), channel_id=1, source_target_pairs={{2,0},{3,1},{0,2},{1,3},{6,4},{7,5},{4,6},{5,7},{10,8},{11,9},{8,1... | collective-permute-start | bytes 4718600 | tf_op jit(solution)/shard_map/ppermute | solution.py:36
  180.2 30.1 %collective-permute-start.26 = (bf16[1024,768]{1,0:T(8,128)(2,1)S(1)}, bf16[1024,768]{1,0:T(8,128)(2,1)S(1)}, u32[]{:S(2)}, u32[]{:S(2)}) collective-permute-start(bf16[1024,768]{1,0:T(8,128)(2,1)S(1)} %add_convert_fusion), channel_id=1, source_target_pairs={{2,1},{1,2},{6,5},{5,6},{10,9},{9,10},{14,13},{13,14},{18,17},{17,... | collective-permute-start | bytes 4718600 | tf_op jit(solution)/shard_map/ppermute | solution.py:78
  193.1 18.6 %collective-permute-start.24 = (bf16[1024,768]{1,0:T(8,128)(2,1)}, bf16[1024,768]{1,0:T(8,128)(2,1)}, u32[]{:S(2)}, u32[]{:S(2)}) collective-permute-start(bf16[1024,768]{1,0:T(8,128)(2,1)} %get-tuple-element.140.own_ref), channel_id=1, source_target_pairs={{2,0},{3,1},{0,2},{1,3},{6,4},{7,5},{4,6},{5,7},{10,8},{11,9},{8,1... | collective-permute-start | bytes 4718600 | tf_op jit(solution)/shard_map/ppermute | solution.py:36
  213.7 32.6 %collective-permute-start.29 = (bf16[2,2,2,48,1536]{4,3,2,1,0:T(8,128)(2,1)}, bf16[2,2,2,48,1536]{4,3,2,1,0:T(8,128)(2,1)}, u32[]{:S(2)}, u32[]{:S(2)}) collective-permute-start(bf16[2,2,2,48,1536]{4,3,2,1,0:T(8,128)(2,1)} %dynamic-slice_bitcast_fusion.1), channel_id=1, source_target_pairs={{0,4},{2,6},{4,0},{6,2},{8,12},{10,14},{12,8},{14,10},{16,20},{18,... | collective-permute-start | bytes 3538952 | tf_op jit(solution)/shard_map/ppermute | solution.py:92
  215.7 32.1 %collective-permute-start.27 = (bf16[2,2,2,48,1536]{4,3,0,1,2:T(8,128)(2,1)}, bf16[2,2,2,48,1536]{4,3,0,1,2:T(8,128)(2,1)S(1)}, u32[]{:S(2)}, u32[]{:S(2)}) collective-permute-start(bf16[2,2,2,48,1536]{4,3,0,1,2:T(8,128)(2,1)} %bitcast.181), channel_id=1, source_target_pairs={{1,0},{3,1},{0,2},{2,3},{5,4},{7,5},{4,6},{6,7},{9,8},{11,9},{8,10... | collective-permute-start | bytes 3538952 | tf_op jit(solution)/shard_map/ppermute | solution.py:102
  216.8 32.1 %collective-permute-start.28 = (bf16[2,2,2,48,1536]{4,3,0,1,2:T(8,128)(2,1)}, bf16[2,2,2,48,1536]{4,3,0,1,2:T(8,128)(2,1)}, u32[]{:S(2)}, u32[]{:S(2)}) collective-permute-start(bf16[2,2,2,48,1536]{4,3,0,1,2:T(8,128)(2,1)} %bitcast.180), channel_id=1, source_target_pairs={{2,1},{1,2},{6,5},{5,6},{10,9},{9,10},{14,13},{13,14},{18,17},{17,... | collective-permute-start | bytes 3538952 | tf_op jit(solution)/shard_map/ppermute | solution.py:107
  250.7 15.9 %collective-permute-start.31 = (bf16[2,2,48,1536]{3,2,0,1:T(8,128)(2,1)S(1)}, bf16[2,2,48,1536]{3,2,0,1:T(8,128)(2,1)}, u32[]{:S(2)}, u32[]{:S(2)}) collective-permute-start(bf16[2,2,48,1536]{3,2,0,1:T(8,128)(2,1)S(1)} %dynamic-slice_bitcast_fusion.13), channel_id=1, source_target_pairs={{0,4},{2,6},{4,0},{6,2},{8,12},{10,14},{12,8},{14,10},{16,20},{18,... | collective-permute-start | bytes 1769480 | tf_op jit(solution)/shard_map/ppermute | solution.py:92
  253.0 14.8 %collective-permute-start.32 = (bf16[2,2,48,1536]{3,2,0,1:T(8,128)(2,1)S(1)}, bf16[2,2,48,1536]{3,2,0,1:T(8,128)(2,1)S(1)}, u32[]{:S(2)}, u32[]{:S(2)}) collective-permute-start(bf16[2,2,48,1536]{3,2,0,1:T(8,128)(2,1)S(1)} %bitcast.224), channel_id=1, source_target_pairs={{1,0},{3,1},{0,2},{2,3},{5,4},{7,5},{4,6},{6,7},{9,8},{11,9},{8,10... | collective-permute-start | bytes 1769480 | tf_op jit(solution)/shard_map/ppermute | solution.py:102
  269.8 21.4 %collective-permute-start.37 = (bf16[2,2,2,48,768]{4,3,2,1,0:T(8,128)(2,1)S(1)}, bf16[2,2,2,48,768]{4,3,2,1,0:T(8,128)(2,1)S(1)}, u32[]{:S(2)}, u32[]{:S(2)}) collective-permute-start(bf16[2,2,2,48,768]{4,3,2,1,0:T(8,128)(2,1)S(1)} %dynamic-slice_bitcast_fusion.11), channel_id=1, source_target_pairs={{0,4},{2,6},{4,0},{6,2},{8,12},{10,14},{12,8},{14,10},{16,20},{18,... | collective-permute-start | bytes 1769480 | tf_op jit(solution)/shard_map/ppermute | solution.py:92
  270.7 20.6 %collective-permute-start.35 = (bf16[2,2,2,48,768]{4,3,0,1,2:T(8,128)(2,1)S(1)}, bf16[2,2,2,48,768]{4,3,0,1,2:T(8,128)(2,1)S(1)}, u32[]{:S(2)}, u32[]{:S(2)}) collective-permute-start(bf16[2,2,2,48,768]{4,3,0,1,2:T(8,128)(2,1)S(1)} %bitcast.222), channel_id=1, source_target_pairs={{1,0},{3,1},{0,2},{2,3},{5,4},{7,5},{4,6},{6,7},{9,8},{11,9},{8,10... | collective-permute-start | bytes 1769480 | tf_op jit(solution)/shard_map/ppermute | solution.py:102
  272.3 19.1 %collective-permute-start.36 = (bf16[2,2,2,48,768]{4,3,0,1,2:T(8,128)(2,1)S(1)}, bf16[2,2,2,48,768]{4,3,0,1,2:T(8,128)(2,1)S(1)}, u32[]{:S(2)}, u32[]{:S(2)}) collective-permute-start(bf16[2,2,2,48,768]{4,3,0,1,2:T(8,128)(2,1)S(1)} %bitcast.223), channel_id=1, source_target_pairs={{2,1},{1,2},{6,5},{5,6},{10,9},{9,10},{14,13},{13,14},{18,17},{17,... | collective-permute-start | bytes 1769480 | tf_op jit(solution)/shard_map/ppermute | solution.py:107
  273.3 18.3 %collective-permute-start.34 = (bf16[2,48,3072]{2,1,0:T(8,128)(2,1)S(1)}, bf16[2,48,3072]{2,1,0:T(8,128)(2,1)}, u32[]{:S(2)}, u32[]{:S(2)}) collective-permute-start(bf16[2,48,3072]{2,1,0:T(8,128)(2,1)S(1)} %dynamic-slice_bitcast_fusion.12), channel_id=1, source_target_pairs={{0,8},{2,10},{4,12},{6,14},{8,0},{10,2},{12,4},{14,6},{16,24},{18,... | collective-permute-start | bytes 1769480 | tf_op jit(solution)/shard_map/ppermute | solution.py:92
  292.9 21.7 %collective-permute-start.40 = (bf16[2,2,48,768]{3,2,0,1:T(8,128)(2,1)S(1)}, bf16[2,2,48,768]{3,2,0,1:T(8,128)(2,1)S(1)}, u32[]{:S(2)}, u32[]{:S(2)}) collective-permute-start(bf16[2,2,48,768]{3,2,0,1:T(8,128)(2,1)S(1)} %dynamic-slice_bitcast_fusion.17), channel_id=1, source_target_pairs={{0,4},{2,6},{4,0},{6,2},{8,12},{10,14},{12,8},{14,10},{16,20},{18,... | collective-permute-start | bytes 884744 | tf_op jit(solution)/shard_map/ppermute | solution.py:92
  293.7 20.8 %collective-permute-start.41 = (bf16[2,2,48,768]{3,2,0,1:T(8,128)(2,1)S(1)}, bf16[2,2,48,768]{3,2,0,1:T(8,128)(2,1)S(1)}, u32[]{:S(2)}, u32[]{:S(2)}) collective-permute-start(bf16[2,2,48,768]{3,2,0,1:T(8,128)(2,1)S(1)} %bitcast.226), channel_id=1, source_target_pairs={{1,0},{3,1},{0,2},{2,3},{5,4},{7,5},{4,6},{6,7},{9,8},{11,9},{8,10... | collective-permute-start | bytes 884744 | tf_op jit(solution)/shard_map/ppermute | solution.py:102
  296.2 18.3 %collective-permute-start.42 = (bf16[2,2,48,768]{3,2,0,1:T(8,128)(2,1)S(1)}, bf16[2,2,48,768]{3,2,0,1:T(8,128)(2,1)S(1)}, u32[]{:S(2)}, u32[]{:S(2)}) collective-permute-start(bf16[2,2,48,768]{3,2,0,1:T(8,128)(2,1)S(1)} %bitcast.228), channel_id=1, source_target_pairs={{2,1},{1,2},{6,5},{5,6},{10,9},{9,10},{14,13},{13,14},{18,17},{17,... | collective-permute-start | bytes 884744 | tf_op jit(solution)/shard_map/ppermute | solution.py:107
  296.9 17.9 %collective-permute-start.39 = (bf16[48,3072]{1,0:T(8,128)(2,1)S(1)}, bf16[48,3072]{1,0:T(8,128)(2,1)S(1)}, u32[]{:S(2)}, u32[]{:S(2)}) collective-permute-start(bf16[48,3072]{1,0:T(8,128)(2,1)S(1)} %dynamic-slice_bitcast_fusion.18), channel_id=1, source_target_pairs={{0,16},{2,18},{4,20},{6,22},{8,24},{10,26},{12,28},{14,30},{16,0},... | collective-permute-start | bytes 884744 | tf_op jit(solution)/shard_map/ppermute | solution.py:92
  299.5 15.3 %collective-permute-start.38 = (bf16[1024,768]{1,0:T(8,128)(2,1)S(1)}, bf16[1024,768]{1,0:T(8,128)(2,1)S(1)}, u32[]{:S(2)}, u32[]{:S(2)}) collective-permute-start(bf16[1024,768]{1,0:T(8,128)(2,1)S(1)} %copy-done.35), channel_id=1, source_target_pairs={{2,0},{3,1},{0,2},{1,3},{6,4},{7,5},{4,6},{5,7},{10,8},{11,9},{8,1... | collective-permute-start | bytes 4718600 | tf_op jit(solution)/shard_map/ppermute | solution.py:36
  316.9 36.5 %collective-permute-start.46 = (bf16[2,2,2,48,1536]{4,3,2,1,0:T(8,128)(2,1)S(1)}, bf16[2,2,2,48,1536]{4,3,2,1,0:T(8,128)(2,1)}, u32[]{:S(2)}, u32[]{:S(2)}) collective-permute-start(bf16[2,2,2,48,1536]{4,3,2,1,0:T(8,128)(2,1)S(1)} %dynamic-slice_bitcast_fusion), channel_id=1, source_target_pairs={{0,4},{2,6},{4,0},{6,2},{8,12},{10,14},{12,8},{14,10},{16,20},{18,... | collective-permute-start | bytes 3538952 | tf_op jit(solution)/shard_map/ppermute | solution.py:92
  319.7 35.3 %collective-permute-start.44 = (bf16[2,2,2,48,1536]{4,3,0,1,2:T(8,128)(2,1)}, bf16[2,2,2,48,1536]{4,3,0,1,2:T(8,128)(2,1)S(1)}, u32[]{:S(2)}, u32[]{:S(2)}) collective-permute-start(bf16[2,2,2,48,1536]{4,3,0,1,2:T(8,128)(2,1)} %bitcast.179), channel_id=1, source_target_pairs={{1,0},{3,1},{0,2},{2,3},{5,4},{7,5},{4,6},{6,7},{9,8},{11,9},{8,10... | collective-permute-start | bytes 3538952 | tf_op jit(solution)/shard_map/ppermute | solution.py:102
  320.9 34.2 %collective-permute-start.45 = (bf16[2,2,2,48,1536]{4,3,0,1,2:T(8,128)(2,1)}, bf16[2,2,2,48,1536]{4,3,0,1,2:T(8,128)(2,1)S(1)}, u32[]{:S(2)}, u32[]{:S(2)}) collective-permute-start(bf16[2,2,2,48,1536]{4,3,0,1,2:T(8,128)(2,1)} %bitcast.178), channel_id=1, source_target_pairs={{2,1},{1,2},{6,5},{5,6},{10,9},{9,10},{14,13},{13,14},{18,17},{17,... | collective-permute-start | bytes 3538952 | tf_op jit(solution)/shard_map/ppermute | solution.py:107
  322.6 29.8 %collective-permute-start.43 = (bf16[2,48,1536]{2,1,0:T(8,128)(2,1)}, bf16[2,48,1536]{2,1,0:T(8,128)(2,1)}, u32[]{:S(2)}, u32[]{:S(2)}) collective-permute-start(bf16[2,48,1536]{2,1,0:T(8,128)(2,1)} %dynamic-slice_bitcast_fusion.16), channel_id=1, source_target_pairs={{0,8},{2,10},{4,12},{6,14},{8,0},{10,2},{12,4},{14,6},{16,24},{18,... | collective-permute-start | bytes 884744 | tf_op jit(solution)/shard_map/ppermute | solution.py:92
  355.5 18.5 %collective-permute-start.49 = (bf16[2,2,48,1536]{3,2,0,1:T(8,128)(2,1)S(1)}, bf16[2,2,48,1536]{3,2,0,1:T(8,128)(2,1)}, u32[]{:S(2)}, u32[]{:S(2)}) collective-permute-start(bf16[2,2,48,1536]{3,2,0,1:T(8,128)(2,1)S(1)} %dynamic-slice_bitcast_fusion.10), channel_id=1, source_target_pairs={{0,4},{2,6},{4,0},{6,2},{8,12},{10,14},{12,8},{14,10},{16,20},{18,... | collective-permute-start | bytes 1769480 | tf_op jit(solution)/shard_map/ppermute | solution.py:92
  357.9 17.5 %collective-permute-start.50 = (bf16[2,2,48,1536]{3,2,0,1:T(8,128)(2,1)}, bf16[2,2,48,1536]{3,2,0,1:T(8,128)(2,1)S(1)}, u32[]{:S(2)}, u32[]{:S(2)}) collective-permute-start(bf16[2,2,48,1536]{3,2,0,1:T(8,128)(2,1)} %bitcast.185), channel_id=1, source_target_pairs={{1,0},{3,1},{0,2},{2,3},{5,4},{7,5},{4,6},{6,7},{9,8},{11,9},{8,10... | collective-permute-start | bytes 1769480 | tf_op jit(solution)/shard_map/ppermute | solution.py:102
  361.6 13.8 %collective-permute-start.51 = (bf16[2,2,48,1536]{3,2,0,1:T(8,128)(2,1)}, bf16[2,2,48,1536]{3,2,0,1:T(8,128)(2,1)S(1)}, u32[]{:S(2)}, u32[]{:S(2)}) collective-permute-start(bf16[2,2,48,1536]{3,2,0,1:T(8,128)(2,1)} %bitcast.184), channel_id=1, source_target_pairs={{2,1},{1,2},{6,5},{5,6},{10,9},{9,10},{14,13},{13,14},{18,17},{17,... | collective-permute-start | bytes 1769480 | tf_op jit(solution)/shard_map/ppermute | solution.py:107
  390.8 21.9 %collective-permute-start.55 = (bf16[2,2,2,48,768]{4,3,2,1,0:T(8,128)(2,1)S(1)}, bf16[2,2,2,48,768]{4,3,2,1,0:T(8,128)(2,1)S(1)}, u32[]{:S(2)}, u32[]{:S(2)}) collective-permute-start(bf16[2,2,2,48,768]{4,3,2,1,0:T(8,128)(2,1)S(1)} %dynamic-slice_bitcast_fusion.8), channel_id=1, source_target_pairs={{0,4},{2,6},{4,0},{6,2},{8,12},{10,14},{12,8},{14,10},{16,20},{18,... | collective-permute-start | bytes 1769480 | tf_op jit(solution)/shard_map/ppermute | solution.py:92
  395.2 19.7 %collective-permute-start.53 = (bf16[2,2,2,48,768]{4,3,0,1,2:T(8,128)(2,1)S(1)}, bf16[2,2,2,48,768]{4,3,0,1,2:T(8,128)(2,1)S(1)}, u32[]{:S(2)}, u32[]{:S(2)}) collective-permute-start(bf16[2,2,2,48,768]{4,3,0,1,2:T(8,128)(2,1)S(1)} %bitcast.220), channel_id=1, source_target_pairs={{1,0},{3,1},{0,2},{2,3},{5,4},{7,5},{4,6},{6,7},{9,8},{11,9},{8,10... | collective-permute-start | bytes 1769480 | tf_op jit(solution)/shard_map/ppermute | solution.py:102
  395.3 19.7 %collective-permute-start.54 = (bf16[2,2,2,48,768]{4,3,0,1,2:T(8,128)(2,1)S(1)}, bf16[2,2,2,48,768]{4,3,0,1,2:T(8,128)(2,1)S(1)}, u32[]{:S(2)}, u32[]{:S(2)}) collective-permute-start(bf16[2,2,2,48,768]{4,3,0,1,2:T(8,128)(2,1)S(1)} %bitcast.221), channel_id=1, source_target_pairs={{2,1},{1,2},{6,5},{5,6},{10,9},{9,10},{14,13},{13,14},{18,17},{17,... | collective-permute-start | bytes 1769480 | tf_op jit(solution)/shard_map/ppermute | solution.py:107
  397.3 14.7 %collective-permute-start.60 = (f32[6,768]{1,0:T(8,128)S(1)}, f32[6,768]{1,0:T(8,128)S(1)}, u32[]{:S(2)}, u32[]{:S(2)}) collective-permute-start(f32[6,768]{1,0:T(8,128)S(1)} %add.221), channel_id=1, source_target_pairs={{0,1},{1,0},{2,3},{3,2},{4,5},{5,4},{6,7},{7,6},{8,9},{9,8},{10,11... | collective-permute-start | bytes 55304 | tf_op jit(solution)/shard_map/ppermute | solution.py:784
  399.4 15.4 %collective-permute-start.52 = (bf16[2,48,3072]{2,1,0:T(8,128)(2,1)S(1)}, bf16[2,48,3072]{2,1,0:T(8,128)(2,1)S(1)}, u32[]{:S(2)}, u32[]{:S(2)}) collective-permute-start(bf16[2,48,3072]{2,1,0:T(8,128)(2,1)S(1)} %dynamic-slice_bitcast_fusion.9), channel_id=1, source_target_pairs={{0,8},{2,10},{4,12},{6,14},{8,0},{10,2},{12,4},{14,6},{16,24},{18,... | collective-permute-start | bytes 1769480 | tf_op jit(solution)/shard_map/ppermute | solution.py:92
  417.2 16.5 %collective-permute-start.66 = (bf16[48,3072]{1,0:T(8,128)(2,1)S(1)}, bf16[48,3072]{1,0:T(8,128)(2,1)S(1)}, u32[]{:S(2)}, u32[]{:S(2)}) collective-permute-start(bf16[48,3072]{1,0:T(8,128)(2,1)S(1)} %dynamic-slice_bitcast_fusion.14), channel_id=1, source_target_pairs={{0,16},{2,18},{4,20},{6,22},{8,24},{10,26},{12,28},{14,30},{16,0},... | collective-permute-start | bytes 884744 | tf_op jit(solution)/shard_map/ppermute | solution.py:92
  417.7 32.3 %collective-permute-start.56 = (bf16[1024,768]{1,0:T(8,128)(2,1)S(1)}, bf16[1024,768]{1,0:T(8,128)(2,1)S(1)}, u32[]{:S(2)}, u32[]{:S(2)}) collective-permute-start(bf16[1024,768]{1,0:T(8,128)(2,1)S(1)} %copy-done.13), channel_id=1, source_target_pairs={{2,1},{1,2},{6,5},{5,6},{10,9},{9,10},{14,13},{13,14},{18,17},{17,... | collective-permute-start | bytes 4718600 | tf_op jit(solution)/shard_map/ppermute | solution.py:78
  424.0 14.7 %collective-permute-start.64 = (bf16[2,48,1536]{2,1,0:T(8,128)(2,1)S(1)}, bf16[2,48,1536]{2,1,0:T(8,128)(2,1)S(1)}, u32[]{:S(2)}, u32[]{:S(2)}) collective-permute-start(bf16[2,48,1536]{2,1,0:T(8,128)(2,1)S(1)} %fusion.13), channel_id=1, source_target_pairs={{0,8},{2,10},{4,12},{6,14},{8,0},{10,2},{12,4},{14,6},{16,24},{18,... | collective-permute-start | bytes 884744 | tf_op jit(solution)/shard_map/ppermute | solution.py:92
  (63 other events, 443.5 us)

commit v3 on v2

--- a/solution.py
+++ b/solution.py
@@ -63,15 +63,18 @@
     return across(lax.dynamic_index_in_dim(pieces, index, 0, keepdims=False))
 
 
-def relay(straight):
+def from_neighbour(values, bit):
+    return lax.ppermute(
+        values, BOTH, moves(lambda dp, mp: (dp ^ (1 << bit), mp) if (dp & 1) != mp else None)
+    )
+
+
+def relay(straight, *bits):
+    if len(bits) == 1:
+        return (straight, from_neighbour(straight, bits[0]))
     half = straight.shape[0] // 2
-
-    def from_neighbour(values, bit):
-        return lax.ppermute(
-            values, BOTH, moves(lambda dp, mp: (dp ^ (1 << bit), mp) if (dp & 1) != mp else None)
-        )
-
-    return (straight, from_neighbour(straight[:half], 1), from_neighbour(straight[half:], 2))
+    first, second = tie(straight[:half], straight[half:])
+    return (straight, from_neighbour(first, bits[0]), from_neighbour(second, bits[1]))
 
 
 def to_mesh_rows(values, same):
@@ -85,75 +88,82 @@
     return (index >> bit) & 1
 
 
-def fold(parts, bit, axis, dtype):
-    mine = bit_of(lax.axis_index("dp"), bit)
-    send = lax.dynamic_index_in_dim(parts, 1 - mine, axis, keepdims=False)
-    keep = lax.dynamic_index_in_dim(parts, mine, axis, keepdims=False)
-    recv = lax.ppermute(send, "dp", [(i, i ^ (1 << bit)) for i in range(lax.axis_size("dp"))])
-    return (keep.astype(jnp.float32) + recv.astype(jnp.float32)).astype(dtype)
-
-
-def cross(parts, axis, same, dtype):
-    mp = lax.axis_index("mp")
-
-    def shards(index):
-        return lax.dynamic_index_in_dim(parts, index, axis, keepdims=False)
-
-    round_trip = lax.ppermute(
-        shards(1 - mp),
-        BOTH,
-        moves(lambda dp, mp: (dp, 1 - mp) if (dp & 1) == mp else (dp ^ 1, mp)),
-    )
-    diagonal = lax.ppermute(
-        shards(mp),
-        BOTH,
-        moves(lambda dp, mp: (dp ^ 1, 1 - mp) if (dp & 1) != mp else None),
-    )
-    other = jnp.where(same, shards(mp), diagonal)
-    return (round_trip.astype(jnp.float32) + other.astype(jnp.float32)).astype(dtype)
+def sum_of(values):
+    total = values[0].astype(jnp.float32)
+    for value in values[1:]:
+        total = total + value.astype(jnp.float32)
+    return total
+
+
+def shards(values, axis, index):
+    return [lax.dynamic_index_in_dim(x, index, axis, keepdims=False) for x in values]
 
 
 class Reduction:
-    def __init__(self, pair, same):
+    def __init__(self, parts, same):
         self.same = same
-        self.bits = lax.axis_size("dp").bit_length() - 1
-        self.widths = [x.shape[1] for x in pair]
-        self.pair = [
-            x.reshape((2,) * self.bits + (x.shape[0] >> self.bits, x.shape[1])) for x in pair
-        ]
-        self.next_bit = 2
+        self.dp, self.mp = lax.axis_index("dp"), lax.axis_index("mp")
+        self.runs = lax.axis_size("dp")
+        self.bits = self.runs.bit_length() - 1
+        self.parts = parts
+
+    def shape(self, values):
+        lead = (2,) * (self.bits - 1)
+        return values.reshape(*lead, (2 * values.shape[0]) >> self.bits, values.shape[1])
+
+    def along_mp(self, stays, goes):
+        cycle = moves(lambda dp, mp: (dp, 1 - mp) if (dp & 1) == mp else (dp ^ 1, mp))
+        return [lax.ppermute(goes, BOTH, cycle), across(stays)]
+
+    def along_bit(self, goes):
+        return [lax.ppermute(goes, "dp", [(i, i ^ 2) for i in range(self.runs)])]
 
     def first(self):
-        one, two = self.pair
-        one = cross(one, self.bits - 1, self.same, LOW)
-        two = fold(two, 1, self.bits - 2, LOW)
-        self.pair = [one, two]
-        return self.pair
-
-    def second(self):
-        one, two = self.pair
-        one = fold(one, 1, self.bits - 2, LOW)
-        two = cross(two, self.bits - 2, self.same, LOW)
-        self.pair = [jnp.concatenate([one, two], axis=-1)]
-        return self.pair
-
-    def further(self):
-        bit = self.next_bit
-        last = bit == self.bits - 1
-        axis = self.bits - 1 - bit
-        self.pair = [fold(self.pair[0], bit, axis, F32 if last else LOW)]
-        self.next_bit += 1
-        return self.pair
-
-    def rest(self):
-        while self.next_bit < self.bits:
-            self.further()
-        return self.pair[0][:, : self.widths[0]], self.pair[0][:, self.widths[0] :]
-
-
-def dot(left, right, contract=((1,), (0,)), precision=None):
+        one_stays, one_goes, two_stays, two_goes = self.parts
+        self.one, self.two = one_stays, two_stays
+        return self.along_mp(one_stays, one_goes) + self.along_bit(two_goes)
+
+    def second(self, came):
+        one = [self.shape(came[0]), self.shape(jnp.where(self.same, self.one, came[1]))]
+        two = [self.shape(self.two), self.shape(came[2])]
+        last = self.bits - 2
+        mine = bit_of(self.dp, 1)
+        one_goes = sum_of(shards(one, last, 1 - mine)).astype(LOW)
+        self.one = shards(one, last, mine)
+        self.two = sum_of(shards(two, last, self.mp)).astype(LOW)
+        two_goes = sum_of(shards(two, last, 1 - self.mp)).astype(LOW)
+        return self.along_bit(one_goes) + self.along_mp(self.two, two_goes)
+
+    def third(self, came):
+        one = sum_of(self.one + [came[0]])
+        two = sum_of([came[1], jnp.where(self.same, self.two, came[2])])
+        self.width = one.shape[-1]
+        self.rest = [jnp.concatenate([one, two], axis=-1).astype(LOW)]
+        return self.step(2)
+
+    def step(self, bit):
+        mine, last = bit_of(self.dp, bit), self.rest[0].ndim - 3
+        goes = sum_of(shards(self.rest, last, 1 - mine)).astype(LOW)
+        self.rest = shards(self.rest, last, mine)
+        pairs = [(i, i ^ (1 << bit)) for i in range(self.runs)]
+        return [lax.ppermute(goes, "dp", pairs)]
+
+    def fourth(self, came):
+        self.rest = self.rest + came
+        return self.step(3)
+
+    def done(self, came):
+        self.rest = self.rest + came
+        for bit in range(4, self.bits):
+            came = self.step(bit)
+            self.rest = self.rest + came
+        total = sum_of(self.rest)
+        return total[:, : self.width], total[:, self.width :]
+
+
+def dot(left, right, contract=((1,), (0,))):
     return lax.dot_general(
-        left, right, (contract, ((), ())), precision=precision, preferred_element_type=F32
+        left, right, (contract, ((), ())), preferred_element_type=F32
     )
 
 
@@ -195,7 +205,7 @@
 
 
 def lanes_of(index, base=0):
-    return pl.ds(pl.multiple_of(base + index * LANES, LANES), LANES)
+    return pl.ds(base + index * LANES, LANES)
 
 
 def rows_of_block(index):
@@ -214,7 +224,7 @@
 
 
 def weight_copies(flags, parts, room, sems):
-    own, straight, around_first, around_second = parts
+    own, straight, *around = parts
     quarter = room.shape[0] // 4
 
     def place(index):
@@ -229,7 +239,11 @@
     @pl.when(flags[0] == 0)
     def _():
         near, far = 2 * flags[1], 2 - 2 * flags[1]
-        sources = (straight.at[place(0)], straight.at[place(1)], around_first, around_second)
+        sources = [straight.at[place(0)], straight.at[place(1)]]
+        if len(around) == 1:
+            around.extend([around[0].at[place(1)]])
+            around[0] = around[0].at[place(0)]
+        sources += around
         targets = (near, near + 1, far, far + 1)
         for index in range(4):
             target = room.at[place(targets[index])]
@@ -247,13 +261,13 @@
     pl.when(pl.program_id(0) == 0)(action)
 
 
-def attention_forward_body(second, *refs):
+def attention_forward_body(second, pieces, *refs):
     if second:
         (mid_ref, own_ref, other_ref, table_ref), refs = refs[:4], refs[4:]
     else:
         (mid_ref,), refs = refs[:1], refs[1:]
     (seg_col, seg_row, gain_ref, flags), refs = refs[:4], refs[4:]
-    parts, refs = refs[:4], refs[4:]
+    parts, refs = refs[:pieces], refs[pieces:]
     if second:
         (joined_ref,), refs = refs[:1], refs[1:]
     normed_ref, qkv_ref, att_ref, log_ref, part_ref, keys, values, bias, room, sems = refs
@@ -299,7 +313,9 @@
             logs = jnp.where(lanes == 2 * index, sums[:BLOCK], logs)
             return jnp.where(lanes == 2 * index + 1, sums[BLOCK:], logs)
 
-        logs = lax.fori_loop(0, width // LANES, pair, jnp.zeros((BLOCK, LANES), F32))
+        logs = jnp.zeros((BLOCK, LANES), F32)
+        for index in range(width // LANES):
+            logs = pair(index, logs)
         log_ref[...] = logs.T[: log_ref.shape[0], :]
 
     for last in range(blocks):
@@ -307,13 +323,10 @@
     part_ref[...] = dot(att_ref[...], room[3 * width :, :]).astype(LOW)
 
 
-def mlp_forward_body(
-    res_ref, own_ref, other_ref, gain_ref, flags, up_a, up_b, up_c, up_d, down_a, down_b, down_c, down_d,
-    mid_ref, normed_ref, hidden_ref, slope_ref, part_ref,
-    up_weight, down_weight, sems,
-):
-    up_parts = (up_a, up_b, up_c, up_d)
-    down_parts = (down_a, down_b, down_c, down_d)
+def mlp_forward_body(up_pieces, down_pieces, res_ref, own_ref, other_ref, gain_ref, flags, *refs):
+    up_parts, refs = refs[:up_pieces], refs[up_pieces:]
+    down_parts, refs = refs[:down_pieces], refs[down_pieces:]
+    mid_ref, kept_ref, part_ref, up_weight, down_weight, sems = refs
 
     @at_first
     def _():
@@ -324,7 +337,7 @@
     mid_ref[...] = middle
     normal, _ = spread(middle)
     normed = (normal * gain_ref[1:2, :]).astype(LOW)
-    normed_ref[...] = normed
+    kept_ref[:, 2 * up_weight.shape[1] :] = normed
     at_first(lambda: weight_wait(up_parts, up_weight, sems.at[0]))
     units = up_weight.shape[1]
     cut = 512 if units % 512 == 0 else units
@@ -332,23 +345,25 @@
         columns = slice(start, start + cut)
         before = dot(normed, up_weight[:, columns])
         below, density = normal_parts(before)
-        hidden_ref[:, columns] = (before * below).astype(LOW)
-        slope_ref[:, columns] = (below + before * density).astype(LOW)
+        kept_ref[:, columns] = (before * below).astype(LOW)
+        slopes = slice(units + start, units + start + cut)
+        kept_ref[:, slopes] = (below + before * density).astype(LOW)
     at_first(lambda: weight_wait(down_parts, down_weight, sems.at[1]))
-    part_ref[...] = dot(hidden_ref[...], down_weight[...]).astype(LOW)
+    part_ref[...] = dot(kept_ref[:, :units], down_weight[...]).astype(LOW)
 
 
 def add_rows(total_ref, row, values):
     total_ref[row : row + 1, :] += jnp.sum(values, axis=0, keepdims=True)
 
 
-def mlp_backward_body(joined, *refs):
+def mlp_backward_body(joined, up_pieces, down_pieces, *refs):
     if joined:
         (grad_mid, own_ref, other_ref, res_ref, gain_ref), refs = refs[:5], refs[5:]
     else:
         (low_ref,), refs = refs[:1], refs[1:]
     (slope_ref, flags), refs = refs[:2], refs[2:]
-    up_parts, down_parts, refs = refs[:4], refs[4:8], refs[8:]
+    up_parts, refs = refs[:up_pieces], refs[up_pieces:]
+    down_parts, refs = refs[:down_pieces], refs[down_pieces:]
     if joined:
         (grad_ref, low_ref, small_ref), refs = refs[:3], refs[3:]
     pre_ref, part_ref, up_weight, down_weight, sems = refs
@@ -385,12 +400,12 @@
 
 
 def attention_backward_body(
-    grad_ref, own_ref, other_ref, mid_ref, gain_ref, qkv_ref, att_ref, log_ref, seg_col, seg_row,
-    flags, weight_a, weight_b, weight_c, weight_d,
-    gm_ref, low_ref, grads_ref, part_ref, small_ref,
-    grad_att, grad_keys, grad_values, bias, lines, room, sems,
+    pieces, grad_ref, own_ref, other_ref, mid_ref, gain_ref, qkv_ref, att_ref, log_ref,
+    seg_col, seg_row, flags, *refs,
 ):
-    parts = (weight_a, weight_b, weight_c, weight_d)
+    parts, refs = refs[:pieces], refs[pieces:]
+    gm_ref, low_ref, grads_ref, part_ref, small_ref = refs[:5]
+    grad_att, grad_keys, grad_values, bias, lines, room, sems = refs[5:]
     at_first(lambda: weight_copies(flags, parts, room, sems))
     step = pl.program_id(0)
     blocks = pl.num_programs(0)
@@ -417,7 +432,10 @@
     product = grad_att[...].astype(F32) * att_ref[...].astype(F32)
     head_of = lax.broadcasted_iota(jnp.int32, (8, width), 1) // HEAD_DIM
     chosen = head_of == lax.broadcasted_iota(jnp.int32, (8, width), 0)
-    deltas = dot(jnp.where(chosen, 1.0, 0.0), product, ROWS_BOTH, lax.Precision.HIGHEST)
+    chosen = jnp.where(chosen, 1.0, 0.0).astype(LOW)
+    high = product.astype(LOW)
+    rest = (product - high.astype(F32)).astype(LOW)
+    deltas = dot(chosen, high, ROWS_BOTH) + dot(chosen, rest, ROWS_BOTH)
     for pair in range(pairs):
         for half in range(2):
             head = 2 * pair + half
@@ -435,23 +453,20 @@
         bias[:limit, :BLOCK] = fill
         bias[:limit, BLOCK:] = fill
 
-        def pair(index, carry):
+        for index in range(pairs):
             here = slice(last * BLOCK, limit)
             queries = stack_heads(qkv_ref[here, lanes_of(index)] * jnp.asarray(SCALE, LOW))
             grads = stack_heads(grad_att[:, lanes_of(index)])
             keys = qkv_ref[:limit, lanes_of(index, width)]
             values = qkv_ref[:limit, lanes_of(index, 2 * width)]
             scores = dot(keys, queries, ROWS_BOTH) + bias[:limit, :]
-            probs = jnp.exp(scores - lines[pl.ds(index, 1), :])
+            probs = jnp.exp(scores - lines[index : index + 1, :])
             grad_probs = dot(values, grads, ROWS_BOTH)
-            grad_scores = (probs * (grad_probs - lines[pl.ds(pairs + index, 1), :])).astype(LOW)
+            grad_scores = (probs * (grad_probs - lines[pairs + index : pairs + index + 1, :])).astype(LOW)
             grad_values[:limit, lanes_of(index)] += dot(probs.astype(LOW), grads)
             grad_keys[:limit, lanes_of(index)] += dot(grad_scores, queries)
             grad_query = join_heads(dot(grad_scores, keys, COLS_BOTH)) * SCALE
             grads_ref[:, lanes_of(index)] = grad_query.astype(LOW)
-            return carry
-
-        lax.fori_loop(0, pairs, pair, 0)
 
     for last in range(blocks):
         pl.when(block == last)(functools.partial(attend, last))
@@ -461,7 +476,8 @@
     part_ref[...] = dot(grads_ref[...], room[: 3 * width, :]).astype(LOW)
 
 
-def weight_grads_body(first_steps, steps, left_a, right_a, left_b, right_b, one, two, turned):
+def weight_grads_body(first_steps, steps, runs, choice, left_a, right_a, left_b, right_b, *refs):
+    outs, turned = refs[:4], refs[4]
     step = pl.program_id(0)
 
     @pl.when(step == 0)
@@ -472,14 +488,27 @@
     def _():
         turned[...] = left_b[...].T
 
+    def write(group, product):
+        count = product.shape[0] // runs
+        stays, goes = outs[2 * group : 2 * group + 2]
+        for mine in range(2):
+
+            @pl.when(choice[group] == mine)
+            def _(mine=mine):
+                for shard in range(runs):
+                    place = shard >> 1 if group == 0 else ((shard >> 2) << 1) | (shard & 1)
+                    out = stays if bit_of(shard, group) == mine else goes
+                    rows_in = slice(shard * count, (shard + 1) * count)
+                    out[place * count : (place + 1) * count, :] = product[rows_in]
+
     cuts = sorted({0, first_steps, steps // 2, steps})
     for start, stop in zip(cuts, cuts[1:]):
         right = right_a if start < first_steps else right_b
-        out = one if start < steps // 2 else two
+        group = 0 if start < steps // 2 else 1
 
         @pl.when(jnp.logical_and(step >= start, step < stop))
-        def _(right=right, out=out):
-            out[...] = dot(turned[...], right[...]).astype(LOW)
+        def _(right=right, group=group):
+            write(group, dot(turned[...], right[...]).astype(LOW))
 
 
 def input_grad_body(grad_mid, own_ref, other_ref, res_ref, gain_ref, out_ref, low_ref, small_ref):
@@ -495,20 +524,34 @@
     low_ref[...] = grad.astype(LOW)
 
 
-def call(body, steps, inputs, outputs, scratch=(), flops=0, limit=56):
-    moved = sum(x.size * x.dtype.itemsize for x, _ in inputs)
+def in_hbm(item):
+    return (*item, pltpu.HBM)
+
+
+def in_vmem(item):
+    return (*item, pltpu.VMEM)
+
+
+def call(body, steps, inputs, outputs, scratch=(), flops=0, limit=32):
+    moved = sum(x[0].size * x[0].dtype.itemsize for x in inputs)
+    arrays = [
+        pltpu.with_memory_space_constraint(x[0], x[2]) if len(x) > 2 else x[0] for x in inputs
+    ]
+    shapes = [
+        x[3](x[0], x[1]) if len(x) > 3 else jax.ShapeDtypeStruct(x[0], x[1]) for x in outputs
+    ]
     return pl.pallas_call(
         body,
         grid=(steps,),
-        in_specs=[spec for _, spec in inputs],
-        out_specs=[spec for _, _, spec in outputs],
-        out_shape=[jax.ShapeDtypeStruct(shape, dtype) for shape, dtype, _ in outputs],
+        in_specs=[x[1] for x in inputs],
+        out_specs=[x[2] for x in outputs],
+        out_shape=shapes,
         scratch_shapes=list(scratch),
         compiler_params=pltpu.CompilerParams(
             dimension_semantics=("arbitrary",), vmem_limit_bytes=limit << 20
         ),
         cost_estimate=pl.CostEstimate(flops=flops, bytes_accessed=moved, transcendentals=0),
-    )(*[x for x, _ in inputs])
+    )(*arrays)
 
 
 def whole(array):
@@ -516,7 +559,7 @@
 
 
 def left_there(array):
-    return (array, pl.BlockSpec(memory_space=pl.ANY))
+    return in_hbm((array, pl.BlockSpec(memory_space=pl.ANY)))
 
 
 def scalars(array):
@@ -543,14 +586,15 @@
     second = len(residual) > 1
     count, width = residual[0].shape
     local = weight[0].shape[0] // 4
-    inputs = [rows(x) for x in residual[:3]] + [whole(x) for x in residual[3:]]
+    inputs = [in_hbm(rows(residual[0]))] if second else [rows(residual[0])]
+    inputs += [rows(x) for x in residual[1:3]] + [whole(x) for x in residual[3:]]
     inputs += [rows(seg_col), whole(seg_row), whole(gains), scalars(flags)]
     inputs += [left_there(x) for x in weight]
-    outputs = [rows_out(count, width, F32)] if second else []
+    outputs = [in_vmem(rows_out(count, width, F32))] if second else []
     outputs += [
-        rows_out(count, width, LOW),
-        rows_out(count, 3 * local, LOW),
-        rows_out(count, local, LOW),
+        in_hbm(rows_out(count, width, LOW)),
+        in_hbm(rows_out(count, 3 * local, LOW)),
+        in_hbm(rows_out(count, local, LOW)),
         ((8, count), F32, pl.BlockSpec((8, BLOCK), lambda i: (0, i))),
         rows_out(count, width, LOW),
     ]
@@ -562,40 +606,41 @@
         pltpu.SemaphoreType.DMA((4,)),
     ]
     flops = 2 * count * width * 4 * local + 4 * count * count * local
-    body = functools.partial(attention_forward_body, second)
+    body = functools.partial(attention_forward_body, second, len(weight))
     return call(body, count // BLOCK, inputs, outputs, scratch, flops)
 
 
-def mlp_forward(residual, own, other, gains, flags, up_weight, down_weight):
+def mlp_forward(residual, own, other, gains, flags, up_weight, down_weight, stay):
     count, width = residual.shape
     units = up_weight[0].shape[1]
     inputs = [rows(residual), rows(own), rows(other), whole(gains), scalars(flags)]
     inputs += [left_there(x) for x in up_weight + down_weight]
     scratch = room_for(up_weight, down_weight) + [pltpu.SemaphoreType.DMA((2, 4))]
     outputs = [
-        rows_out(count, width, F32),
-        rows_out(count, width, LOW),
-        rows_out(count, units, LOW),
-        rows_out(count, units, LOW),
+        in_hbm(rows_out(count, width, F32)),
+        stay(rows_out(count, 2 * units + width, LOW)),
         rows_out(count, width, LOW),
     ]
     flops = 4 * count * width * units
-    return call(mlp_forward_body, count // BLOCK, inputs, outputs, scratch, flops)
-
-
-def mlp_backward(grad, slope, flags, up_weight, down_weight):
+    body = functools.partial(mlp_forward_body, len(up_weight), len(down_weight))
+    return call(body, count // BLOCK, inputs, outputs, scratch, flops)
+
+
+def mlp_backward(grad, kept, flags, up_weight, down_weight, stay):
     joined = len(grad) > 1
     count, width = grad[0].shape
     units = up_weight[0].shape[1]
     inputs = [rows(x) for x in grad[:4]] + [whole(x) for x in grad[4:]]
-    inputs += [rows(slope), scalars(flags)]
+    slope = pl.BlockSpec((BLOCK, units), lambda i: (i, 1))
+    inputs += [stay((kept, slope)), scalars(flags)]
     inputs += [left_there(x) for x in up_weight + down_weight]
     scratch = room_for(up_weight, down_weight) + [pltpu.SemaphoreType.DMA((2, 4))]
     outputs = []
     if joined:
-        outputs = [rows_out(count, width, F32), rows_out(count, width, LOW), small_out(width)]
-    outputs += [rows_out(count, units, LOW), rows_out(count, width, LOW)]
-    body = functools.partial(mlp_backward_body, joined)
+        outputs = [in_hbm(rows_out(count, width, F32)), in_hbm(rows_out(count, width, LOW))]
+        outputs += [small_out(width)]
+    outputs += [in_hbm(rows_out(count, units, LOW)), rows_out(count, width, LOW)]
+    body = functools.partial(mlp_backward_body, joined, len(up_weight), len(down_weight))
     return call(body, count // BLOCK, inputs, outputs, scratch, 4 * count * width * units)
 
 
@@ -613,15 +658,15 @@
         spec = pl.BlockSpec((BLOCK, columns), lambda i: (steps - 1 - i, 0))
         return ((count, columns), dtype, spec)
 
-    inputs = [back(grad), back(own), back(other), back(middle), whole(gains), whole(qkv)]
-    inputs += [back(attended)]
+    inputs = [back(grad), back(own), back(other), in_hbm(back(middle)), whole(gains)]
+    inputs += [in_hbm(whole(qkv)), in_hbm(back(attended))]
     inputs += [(logs, pl.BlockSpec((8, BLOCK), lambda i: (0, steps - 1 - i))), whole(seg_col)]
     inputs += [(seg_row, pl.BlockSpec((1, BLOCK), lambda i: (0, steps - 1 - i)))]
     inputs += [scalars(flags)] + [left_there(x) for x in weight]
     outputs = [
-        back_out(width, F32),
-        back_out(width, LOW),
-        back_out(3 * local, LOW),
+        in_hbm(back_out(width, F32)),
+        in_hbm(back_out(width, LOW)),
+        in_hbm(back_out(3 * local, LOW)),
         back_out(width, LOW),
         small_out(width),
     ]
@@ -635,31 +680,50 @@
         pltpu.SemaphoreType.DMA((4,)),
     ]
     flops = 2 * count * width * 4 * local + 10 * count * count * local
-    return call(attention_backward_body, steps, inputs, outputs, scratch, flops)
-
-
-def weight_grads(left_a, right_a, left_b, right_b):
+    body = functools.partial(attention_backward_body, len(weight))
+    return call(body, steps, inputs, outputs, scratch, flops)
+
+
+def weight_grads(left_a, right_a, left_b, right_b, choice, runs, stay, columns_a=None, place_b=0):
     count, width = left_a.shape
+    whole_shards = (width // runs) % 16 == 0
     cut = 384
-    steps_a, steps_b = right_a.shape[1] // cut, right_b.shape[1] // cut
-    total = right_a.shape[1] + right_b.shape[1]
+    columns_a = columns_a or right_a.shape[1]
+    steps_a, steps_b = columns_a // cut, right_b.shape[1] // cut
+    total = columns_a + right_b.shape[1]
     inputs = [
+        scalars(choice),
         whole(left_a),
-        (right_a, pl.BlockSpec((count, cut), lambda i: (0, jnp.minimum(i, steps_a - 1)))),
-        whole(left_b),
+        stay((right_a, pl.BlockSpec((count, cut), lambda i: (0, jnp.minimum(i, steps_a - 1))))),
+        stay((left_b, pl.BlockSpec((count, width), lambda i: (0, place_b)))),
         (right_b, pl.BlockSpec((count, cut), lambda i: (0, jnp.maximum(i - steps_a, 0)))),
     ]
     steps = steps_a + steps_b
     half = steps // 2
-    columns = ((width, total // 2), LOW)
-    outputs = [
-        (*columns, pl.BlockSpec((width, cut), lambda i: (0, jnp.minimum(i, half - 1)))),
-        (*columns, pl.BlockSpec((width, cut), lambda i: (0, jnp.maximum(i - half, 0)))),
-    ]
-    body = functools.partial(weight_grads_body, steps_a, steps)
+    columns = ((width // 2, total // 2), LOW)
+    one = (*columns, pl.BlockSpec((width // 2, cut), lambda i: (0, jnp.minimum(i, half - 1))))
+    two = (*columns, pl.BlockSpec((width // 2, cut), lambda i: (0, jnp.maximum(i - half, 0))))
+    parts = runs if whole_shards else 4
+    body = functools.partial(weight_grads_body, steps_a, steps, parts)
+    if not whole_shards:
+        inputs[0] = scalars(jnp.zeros_like(choice))
     scratch = [pltpu.VMEM((width, count), LOW)]
     flops = 2 * count * width * total
-    return call(body, steps, inputs, outputs, scratch, flops)
+    got = call(body, steps, inputs, [one, one, two, two], scratch, flops)
+    return got if whole_shards else regroup(got, choice, runs)
+
+
+def regroup(got, choice, runs):
+    quarter = got[0].shape[0] // 2
+    first = jnp.concatenate([got[0][:quarter], got[1][:quarter], got[0][quarter:], got[1][quarter:]])
+    second = jnp.concatenate([got[2], got[3]])
+    parts = []
+    for group, values in enumerate((first, second)):
+        split = values.reshape(runs >> (group + 1), 2, -1, values.shape[1])
+        for index in (choice[group], 1 - choice[group]):
+            part = lax.dynamic_index_in_dim(split, index, 1, keepdims=False)
+            parts.append(part.reshape(-1, values.shape[1]))
+    return parts
 
 
 def input_grad(grad_mid, own, other, residual, gains):
@@ -708,91 +772,100 @@
     cotangent = own_run(cotangent, same)
     seg_col, seg_row = segments[:, None], segments[None, :]
 
-    att_w1 = (own_att1, *relay(came_att1))
-    relay_up1 = relay(came_up1)
-    tokens_in, came_up1 = tie(tokens_in, came_up1)
+    runs = lax.axis_size("dp")
+    choice = jnp.stack([lax.axis_index("mp"), bit_of(dp, 1)])
+
+    att_w1 = (own_att1, *relay(came_att1, 1, 2))
     normed_a1, qkv1, att1, logs1, part = attention_forward(
         (tokens_in,), seg_col, seg_row, gains_first, flags, att_w1
     )
-    part, relay_up1, came_down1, came_att2 = tie(part, relay_up1, came_down1, came_att2)
-    up_w1 = (own_up1, *relay_up1)
-    down_w1 = (own_down1, *relay(came_down1))
-    relay_att2 = relay(came_att2)
-    mid1, normed_b1, hidden1, slope1, part = mlp_forward(
-        tokens_in, part, from_core(part), gains_first, flags, up_w1, down_w1
-    )
-    part, relay_att2, came_up2 = tie(part, relay_att2, came_up2)
+    part, came_up1, came_down1, came_att2 = tie(part, came_up1, came_down1, came_att2)
+    up_w1 = (own_up1, *relay(came_up1, 1))
+    down_w1 = (own_down1, *relay(came_down1, 2))
+    relay_att2 = relay(came_att2, 1)
+    mid1, kept1, part = mlp_forward(
+        tokens_in, part, from_core(part), gains_first, flags, up_w1, down_w1, in_hbm
+    )
+    part, relay_att2, came_up2, came_down2 = tie(part, relay_att2, came_up2, came_down2)
     att_w2 = (own_att2, *relay_att2)
-    relay_up2 = relay(came_up2)
+    relay_up2, relay_down2 = relay(came_up2, 1), relay(came_down2, 2)
     joined, normed_a2, qkv2, att2, logs2, part = attention_forward(
         (mid1, part, from_core(part), pass_embed),
         seg_col, seg_row, gains_second, flags, att_w2,
     )
-    part, relay_up2, came_down2, cotangent = tie(part, relay_up2, came_down2, cotangent)
-    up_w2 = (own_up2, *relay_up2)
-    down_w2 = (own_down2, *relay(came_down2))
-    mid2, normed_b2, hidden2, slope2, part = mlp_forward(
-        joined, part, from_core(part), gains_second, flags, up_w2, down_w2
+    part, relay_up2, relay_down2, cotangent = tie(part, relay_up2, relay_down2, cotangent)
+    up_w2, down_w2 = (own_up2, *relay_up2), (own_down2, *relay_down2)
+    mid2, kept2, part = mlp_forward(
+        joined, part, from_core(part), gains_second, flags, up_w2, down_w2, in_vmem
     )
     top = mid2 + (part.astype(F32) + from_core(part).astype(F32))
     output = to_mesh_rows(top.astype(LOW), same)
 
-    pre2, part = mlp_backward((cotangent,), slope2, flags, up_w2, down_w2)
+    units = up_first.shape[1]
+    place = (units, 2 * units // up_first.shape[0])
+    pre2, part = mlp_backward((cotangent,), kept2, flags, up_w2, down_w2, in_vmem)
     other = from_core(part)
-    mlp2 = Reduction(weight_grads(cotangent, hidden2, normed_b2, pre2), same)
-    other, mlp2.pair, output = tie(other, mlp2.pair, output)
-    sums = mlp2.first()
+    mlp2 = weight_grads(cotangent, kept2, kept2, pre2, choice, runs, in_vmem, *place)
+    other, mlp2, output = tie(other, mlp2, output)
+    mlp2 = Reduction(mlp2, same)
+    got_m2 = mlp2.first()
     gm2, gm_low2, grad_rows2, part, small_b2 = attention_backward(
         cotangent, part, other, mid2, gains_second, qkv2, att2, logs2, seg_col, seg_row,
         flags, att_w2,
     )
-    part, gm_low2, mlp2.pair = tie(part, gm_low2, sums)
+    part, gm_low2, got_m2 = tie(part, gm_low2, got_m2)
     other = from_core(part)
-    sums = mlp2.second()
-    att_2 = Reduction(weight_grads(gm_low2, att2, normed_a2, grad_rows2), same)
-    other, att_2.pair, mlp2.pair = tie(other, att_2.pair, sums)
-    sums = (mlp2.further(), att_2.first())
+    got_m2 = mlp2.second(got_m2)
+    att_2 = weight_grads(gm_low2, att2, normed_a2, grad_rows2, choice, runs, in_hbm)
+    other, att_2, got_m2 = tie(other, att_2, got_m2)
+    att_2 = Reduction(att_2, same)
+    got_m2, got_t2 = mlp2.third(got_m2), att_2.first()
     grad, grad_low, small_a2, pre1, part = mlp_backward(
-        (gm2, part, other, joined, gains_second), slope1, flags, up_w1, down_w1
-    )
-    part, grad_low, (mlp2.pair, att_2.pair) = tie(part, grad_low, sums)
+        (gm2, part, other, joined, gains_second), kept1, flags, up_w1, down_w1, in_hbm
+    )
+    part, grad_low, got_t2, got_m2 = tie(part, grad_low, got_t2, got_m2)
     other = from_core(part)
-    sums = (mlp2.further(), att_2.second())
-    mlp1 = Reduction(weight_grads(grad_low, hidden1, normed_b1, pre1), same)
-    other, mlp1.pair, (mlp2.pair, att_2.pair) = tie(other, mlp1.pair, sums)
-    sums = (att_2.further(), mlp1.first())
+    got_t2, got_m2 = att_2.second(got_t2), mlp2.fourth(got_m2)
+    mlp1 = weight_grads(grad_low, kept1, kept1, pre1, choice, runs, in_hbm, *place)
+    other, mlp1, got_t2, got_m2 = tie(other, mlp1, got_t2, got_m2)
+    mlp1 = Reduction(mlp1, same)
+    got_t2, got_m1 = att_2.third(got_t2), mlp1.first()
     gm1, gm_low1, grad_rows1, part, small_b1 = attention_backward(
         grad, part, other, mid1, gains_first, qkv1, att1, logs1, seg_col, seg_row,
         flags, att_w1,
     )
-    part, gm_low1, (att_2.pair, mlp1.pair) = tie(part, gm_low1, sums)
+    part, gm_low1, got_t2, got_m1 = tie(part, gm_low1, got_t2, got_m1)
     other = from_core(part)
-    sums = (att_2.further(), mlp1.second())
-    att_1 = Reduction(weight_grads(gm_low1, att1, normed_a1, grad_rows1), same)
-    other, att_1.pair, (att_2.pair, mlp1.pair) = tie(other, att_1.pair, sums)
-    sums = (mlp1.further(), att_1.first())
+    got_m1, got_t2 = mlp1.second(got_m1), att_2.fourth(got_t2)
+    att_1 = weight_grads(gm_low1, att1, normed_a1, grad_rows1, choice, runs, in_hbm)
+    other, att_1, got_m1, got_t2 = tie(other, att_1, got_m1, got_t2)
+    att_1 = Reduction(att_1, same)
+    got_t1, got_m1 = att_1.first(), mlp1.third(got_m1)
     grad_in, grad_in_low, small_a1 = input_grad(gm1, part, other, tokens_in, gains_first)
-    grad_in_low, (mlp1.pair, att_1.pair) = tie(grad_in_low, sums)
+    grad_in_low, small_a1, got_t1, got_m1 = tie(grad_in_low, small_a1, got_t1, got_m1)
+    got_t1, got_m1 = att_1.second(got_t1), mlp1.fourth(got_m1)
     grad_input = to_mesh_rows(grad_in_low, same).astype(F32)
     grad_input = jnp.where(same, grad_in, grad_input)
-    att_1.second()
-
+
+    small_a1, got_t1, got_m1 = tie(small_a1, got_t1, got_m1)
+    got_t1 = att_1.third(got_t1)
     small = jnp.concatenate([small_a1[:1], small_b1[:1], small_a2[1:3], small_a2[:1], small_b2[:1]])
-    runs = lax.axis_size("dp")
     for bit in range(1, runs.bit_length() - 1):
         small = small + lax.ppermute(small, "dp", [(i, i ^ (1 << bit)) for i in range(runs)])
     small = small + lax.ppermute(small, "mp", [(0, 1), (1, 0)])
     width = small.shape[1] // runs
     small = lax.dynamic_slice_in_dim(small, dp * width, width, 1)
-
-    def placed(mlp, att):
+    small, got_t1 = tie(small, got_t1)
+    got_t1 = att_1.fourth(got_t1)
+
+    def placed(mlp, got_mlp, att, got_att):
         local = att1.shape[1]
-        down, up = mlp.rest()
-        proj_qkv = jnp.concatenate(att.rest(), axis=1)
+        down, up = mlp.done(got_mlp)
+        proj_qkv = jnp.concatenate(att.done(got_att), axis=1)
         return proj_qkv[:, local:].reshape(-1, 3, local), proj_qkv[:, :local].T, up, down.T
 
-    second = placed(mlp2, att_2)
-    first = placed(mlp1, att_1)
+    second = placed(mlp2, got_m2, att_2, got_t2)
+    first = placed(mlp1, got_m1, att_1, got_t1)
     return (
         output,
         grad_input,

time: 462 us -> 420 us (0.909); the launches traced: 453 us -> 416 us
  Pallas kernels: 210 us -> 191 us
  starting transfers between devices: 121 us -> 107 us
  local copies, waits for them, and re-layouts: 46.3 us -> 38.2 us
  other arithmetic: 23.7 us -> 30.3 us
    pallas_call x13, Pallas kernels: 210 us -> 191 us  [call(): pl.pallas_call(body, grid=(steps,), in_specs=[x[1] for x in inputs], out_...]
    unnamed x86 -> x156, local copies, waits for them, and re-layouts: 10.3 us -> 23.4 us
    ppermute x6 -> x14, starting transfers between devices: 6.51 us -> 17.3 us  [across(): lax.ppermute(values, BOTH, moves(lambda dp, mp: (dp ^ 1, 1 - mp) if dp &...]
    ppermute x1, waiting for transfers between devices: 10.9 us -> 2.96 us  [per_device(): small = small + lax.ppermute(small, 'mp', [(0, 1), (1, 0)])]
    dynamic_slice x24 -> x0, local copies, waits for them, and re-layouts: 7.45 us -> none  [shards(): return lax.dynamic_index_in_dim(parts, index, axis, keepdims=False)]
    ppermute x8, starting transfers between devices: 38.5 us -> 31.1 us  [from_core(): return lax.ppermute(values, BOTH, moves(lambda dp, mp: (dp ^ 1, mp)))]
    another operation x0 -> x8, other arithmetic: none -> 6.63 us
    ppermute x32 -> x24, starting transfers between devices: 33.6 us -> 27.5 us  [the longest x8 9.74 us: step(): return [lax.ppermute(goes, 'dp', pairs)]]
  transfers between devices with their start and end apart: 67 -> 62, of which waited for: 12 -> 14; matrix products, arithmetic and copies ran while one was open for 10% -> 8% of each run, Pallas kernels for 41% -> 39%
where the time goes in v3:
time: 420 us; the launch traced here: 416 us
  Pallas kernels  191 us (45%)
  starting transfers between devices  107 us (25%)
  waiting for transfers between devices  47.4 us (11%)
  local copies, waits for them, and re-layouts  38.2 us (9%)
  other arithmetic  30.3 us (7%)
    pallas_call x13, Pallas kernels, call(): pl.pallas_call(body, grid=(steps,), in_specs=[x[1] for x in inputs], out_...  191 us
    ppermute x8, starting transfers between devices, from_core(): return lax.ppermute(values, BOTH, moves(lambda dp, mp: (dp ^ 1, mp)))  31.1 us
    unnamed x156, local copies, waits for them, and re-layouts  23.4 us
    ppermute x3, starting transfers between devices, own_run(): lax.ppermute(values, BOTH, moves(lambda dp, mp: (dp ^ 1, mp) if dp & 1 !=...  21.5 us
    ppermute x8, waiting for transfers between devices, step(): return [lax.ppermute(goes, 'dp', pairs)]  20.4 us
    ppermute x14, starting transfers between devices, across(): lax.ppermute(values, BOTH, moves(lambda dp, mp: (dp ^ 1, 1 - mp) if dp &...  17.3 us
    ppermute x8, starting transfers between devices, step(): return [lax.ppermute(goes, 'dp', pairs)]  9.74 us
    ppermute x8, starting transfers between devices, along_bit(): return [lax.ppermute(goes, 'dp', [(i, i ^ 2) for i in range(self.runs)])]  9.43 us
  transfers between devices with their start and end apart: 62, of which 14 were waited for; matrix products, arithmetic and copies ran while one was open for 8% of the time, Pallas kernels for 39%

profile of v3, /device:TPU:0, one launch (start us, length us, event | category | flops | bytes accessed | tf_op | source)
XLA Modules:
  0.0 415.9 jit_solution(14812925557802391785)
XLA Ops:
  0.6 3.5 collective-permute-start
  4.2 2.7 copy.61
  8.9 1.8 collective-permute-start.2
  10.7 3.0 collective-permute-start.1
  17.3 1.8 collective-permute-start.7
  20.3 1.8 collective-permute-start.5
  24.9 2.3 fusion.49
  30.5 1.8 broadcast_select_fusion.2.refs_0_.res_ref
  32.4 16.1 %shard_map.237 = (bf16[1024,768]{1,0:T(8,128)(2,1)}, bf16[1024,1152]{1,0:T(8,128)(2,1)}, bf16[1024,384]{1,0:T(8,128)(2,1)}, f32[8,1024]{1,0:T(8,128)S(1)}, bf16[1024,768]{1,0:T(8,128)(2,1)S(1)}) custom-call(bf16[1024,768]{1,0:T(8,128)(2,1)S(1)} %broadcast_select_fusion.2.refs_0_.res_ref, s32[1024,1]{1,0:T(8,128)S(1)} %copy.62.refs_1_.refs_4_.seg_col, ...), custom_call_target="tpu_custom_call" | custom-call | flops 4026531840 | bytes 6305800 | tf_op jit(solution)/shard_map/pallas_call | solution.py:543
  49.3 17.8 %collective-permute-start.8 = (bf16[1024,768]{1,0:T(8,128)(2,1)S(1)}, bf16[1024,768]{1,0:T(8,128)(2,1)S(1)}, u32[]{:S(2)}, u32[]{:S(2)}) collective-permute-start(bf16[1024,768]{1,0:T(8,128)(2,1)S(1)} %get-tuple-element.148.own_ref), channel_id=1, source_target_pairs={{2,0},{3,1},{0,2},{1,3},{6,4},{7,5},{4,6},{5,7},{10,8},{11,9},{8,1... | collective-permute-start | bytes 4718600 | tf_op jit(solution)/shard_map/ppermute | solution.py:36
  71.3 15.0 %collective-permute-start.17 = (bf16[1024,768]{1,0:T(8,128)(2,1)S(1)}, bf16[1024,768]{1,0:T(8,128)(2,1)S(1)}, u32[]{:S(2)}, u32[]{:S(2)}) collective-permute-start(bf16[1024,768]{1,0:T(8,128)(2,1)S(1)} %copy-done.52), channel_id=1, source_target_pairs={{3,1},{0,2},{7,5},{4,6},{11,9},{8,10},{15,13},{12,14},{19,17},{16,... | collective-permute-start | bytes 4718600 | tf_op jit(solution)/shard_map/ppermute | solution.py:40
  86.3 14.9 %shard_map.238 = (f32[1024,768]{1,0:T(8,128)}, bf16[1024,3840]{1,0:T(8,128)(2,1)}, bf16[1024,768]{1,0:T(8,128)(2,1)S(1)}) custom-call(bf16[1024,768]{1,0:T(8,128)(2,1)S(1)} %broadcast_select_fusion.2.refs_0_.res_ref, bf16[1024,768]{1,0:T(8,128)(2,1)S(1)} %get-tuple-element.148.own_ref, bf16[1024,768]{1,0:T(8,128)(2,1)S(1)} %collective-permute-done.8.other_ref, ...), custom_call_target="tpu_custom_call" | custom-call | flops 4831838208 | bytes 14161928 | tf_op jit(solution)/shard_map/pallas_call | solution.py:543
  104.8 17.1 %shard_map.239 = (f32[1024,768]{1,0:T(8,128)S(1)}, bf16[1024,768]{1,0:T(8,128)(2,1)}, bf16[1024,1152]{1,0:T(8,128)(2,1)}, bf16[1024,384]{1,0:T(8,128)(2,1)}, f32...) custom-call(f32[1024,768]{1,0:T(8,128)} %get-tuple-element.151.refs_0_.mid_ref, ...), custom_call_target="tpu_custom_call" | custom-call | flops 4026531840 | bytes 11027464 | tf_op jit(solution)/shard_map/pallas_call | solution.py:543
  122.0 2.7 collective-permute-start.18
  124.7 3.0 collective-permute-done.18.other_ref
  127.8 26.8 %shard_map.240 = (f32[1024,768]{1,0:T(8,128)}, bf16[1024,3840]{1,0:T(8,128)(2,1)S(1)}, bf16[1024,768]{1,0:T(8,128)(2,1)S(1)}) custom-call(f32[1024,768]{1,0:T(8,128)S(1)} %get-tuple-element.161.res_ref.refs_3_, bf16[1024,768]{1,0:T(8,128)(2,1)S(1)} %get-tuple-element.162.own_ref, bf16[1024,768]{1,0:T(8,128)(2,1)S(1)} %collective-permute-done.18.other_ref, ...), custom_call_target="tpu_custom_call" | custom-call | flops 4831838208 | bytes 15734792 | tf_op jit(solution)/shard_map/pallas_call | solution.py:543
  155.0 3.0 collective-permute-done.20
  158.0 2.4 add_convert_fusion
  161.2 10.8 %shard_map.241 = (bf16[1024,1536]{1,0:T(8,128)(2,1)}, bf16[1024,768]{1,0:T(8,128)(2,1)S(1)}) custom-call(bf16[1024,768]{1,0:T(8,128)(2,1)S(1)} %broadcast_select_fusion.1.refs_0_.left_a.grad_ref, bf16[1024,3840]{1,0:T(8,128)(2,1)S(1)} %get-tuple-element.167.refs_1_.right_a.left_b, s32[2]{0:T(128)S(1)} %pad_add_fusion.refs_4_.flags.refs_7_.refs_2_.refs_6_, ...), custom_call_target="tpu_custom_call" | custom-call | flops 4831838208 | bytes 18874376 | tf_op jit(solution)/shard_map/pallas_call | solution.py:543
  172.0 5.3 %collective-permute-start.19 = (bf16[1024,768]{1,0:T(8,128)(2,1)S(1)}, bf16[1024,768]{1,0:T(8,128)(2,1)S(1)}, u32[]{:S(2)}, u32[]{:S(2)}) collective-permute-start(bf16[1024,768]{1,0:T(8,128)(2,1)S(1)} %get-tuple-element.168.own_ref), channel_id=1, source_target_pairs={{2,0},{3,1},{0,2},{1,3},{6,4},{7,5},{4,6},{5,7},{10,8},{11,9},{8,1... | collective-permute-start | bytes 4718600 | tf_op jit(solution)/shard_map/ppermute | solution.py:36
  177.4 1.9 copy-done.7
  179.2 12.0 %shard_map.242 = (bf16[384,1536]{1,0:T(8,128)(2,1)}, bf16[384,1536]{1,0:T(8,128)(2,1)}, bf16[384,1536]{1,0:T(8,128)(2,1)S(1)}, bf16[384,1536]{1,0:T(8,128)(2,1)}) custom-call(s32[2]{0:T(128)S(1)} %pad_add_fusion.1.choice, bf16[1024,768]{1,0:T(8,128)(2,1)S(1)} %broadcast_select_fusion.1.refs_0_.left_a.grad_ref, ...), custom_call_target="tpu_custom_call" | custom-call | flops 4831838208 | bytes 20447240 | tf_op jit(solution)/shard_map/pallas_call | solution.py:543
  201.4 23.5 %shard_map.243 = (f32[1024,768]{1,0:T(8,128)}, bf16[1024,768]{1,0:T(8,128)(2,1)}, bf16[1024,1152]{1,0:T(8,128)(2,1)}, bf16[1024,768]{1,0:T(8,128)(2,1)}, f32[8,768]{1,0:T(8,128)S(1)}) custom-call(bf16[1024,768]{1,0:T(8,128)(2,1)S(1)} %broadcast_select_fusion.1.refs_0_.left_a.grad_ref, bf16[1024,768]{1,0:T(8,128)(2,1)S(1)} %copy-done.25, ...), custom_call_target="tpu_custom_call" | custom-call | flops 6442450944 | bytes 15775752 | tf_op jit(solution)/shard_map/pallas_call | solution.py:543
  224.9 1.8 collective-permute-start.25
  226.8 2.5 fusion.4
  233.3 2.0 fusion.2
  238.9 7.6 %shard_map.244 = (bf16[384,768]{1,0:T(8,128)(2,1)S(1)}, bf16[384,768]{1,0:T(8,128)(2,1)S(1)}, bf16[384,768]{1,0:T(8,128)(2,1)S(1)}, bf16[384,768]{1,0:T(8,128)(2,1)S(1)}) custom-call(s32[2]{0:T(128)S(1)} %pad_add_fusion.1.choice, bf16[1024,768]{1,0:T(8,128)(2,1)S(1)} %copy-done.32, bf16[1024,384]{1,0:T(8,128)(2,1)} %get-tuple-element.179.att_ref.right_a, ...), custom_call_target="tpu_custom_call" | custom-call | flops 2415919104 | bytes 6291464 | tf_op jit(solution)/shard_map/pallas_call | solution.py:543
  247.4 2.7 collective-permute-done.26
  250.2 2.2 fusion.1
  256.6 14.1 %shard_map.245 = (f32[1024,768]{1,0:T(8,128)}, bf16[1024,768]{1,0:T(8,128)(2,1)}, f32[8,768]{1,0:T(8,128)S(1)}, bf16[1024,1536]{1,0:T(8,128)(2,1)}, bf16[1024,768]{1,0:T(8,128)(2,1)}) custom-call(f32[1024,768]{1,0:T(8,128)S(1)} %copy-done.5, bf16[1024,768]{1,0:T(8,128)(2,1)} %get-tuple-element.187.refs_1_, ...), custom_call_target="tpu_custom_call" | custom-call | flops 4831838208 | bytes 26744840 | tf_op jit(solution)/shard_map/pallas_call | solution.py:543
  272.5 1.9 collective-permute-start.33
  275.7 2.7 collective-permute-start.37
  282.1 12.4 %shard_map.246 = (bf16[384,1536]{1,0:T(8,128)(2,1)S(1)}, bf16[384,1536]{1,0:T(8,128)(2,1)S(1)}, bf16[384,1536]{1,0:T(8,128)(2,1)S(1)}, bf16[384,1536]{1,0:T(8,128)(2,1)S(1)}) custom-call(s32[2]{0:T(128)S(1)} %pad_add_fusion.1.choice, bf16[1024,768]{1,0:T(8,128)(2,1)S(1)} %copy-done.8, bf16[1024,3840]{1,0:T(8,128)(2,1)} %get-tuple-element.200.refs_5_.right_a.left_b, ...), custom_call_target="tpu_custom_call" | custom-call | flops 4831838208 | bytes 20447240 | tf_op jit(solution)/shard_map/pallas_call | solution.py:543
  295.3 4.1 collective-permute-start.39
  303.1 23.5 %shard_map.247 = (f32[1024,768]{1,0:T(8,128)}, bf16[1024,768]{1,0:T(8,128)(2,1)}, bf16[1024,1152]{1,0:T(8,128)(2,1)}, bf16[1024,768]{1,0:T(8,128)(2,1)S(1)}, f32[8,768]{1,0:T(8,128)S(1)}) custom-call(f32[1024,768]{1,0:T(8,128)S(1)} %copy-done.23, bf16[1024,768]{1,0:T(8,128)(2,1)} %get-tuple-element.210.own_ref, ...), custom_call_target="tpu_custom_call" | custom-call | flops 6442450944 | bytes 17348616 | tf_op jit(solution)/shard_map/pallas_call | solution.py:543
  339.8 7.7 %shard_map.248 = (bf16[384,768]{1,0:T(8,128)(2,1)S(1)}, bf16[384,768]{1,0:T(8,128)(2,1)S(1)}, bf16[384,768]{1,0:T(8,128)(2,1)S(1)}, bf16[384,768]{1,0:T(8,128)(2,1)S(1)}) custom-call(s32[2]{0:T(128)S(1)} %pad_add_fusion.1.choice, bf16[1024,768]{1,0:T(8,128)(2,1)S(1)} %copy-done.31, bf16[1024,384]{1,0:T(8,128)(2,1)} %get-tuple-element.224.att_ref.right_a, ...), custom_call_target="tpu_custom_call" | custom-call | flops 2415919104 | bytes 6291464 | tf_op jit(solution)/shard_map/pallas_call | solution.py:543
  357.9 4.0 shard_map.249
  362.0 5.9 %collective-permute-done.50 = bf16[2,48,3072]{2,1,0:T(8,128)(2,1)S(1)} collective-permute-done((bf16[2,48,3072]{2,1,0:T(8,128)(2,1)S(1)}, bf16[2,48,3072]{2,1,0:T(8,128)(2,1)S(1)}, u32[]{:S(2)}, u32[]{:S(2)}) %collective-permute-start.50) | collective-permute-done | bytes 589856 | tf_op jit(solution)/shard_map/ppermute | solution.py:149
  367.9 2.3 collective-permute-done.49
  376.3 1.8 collective-permute-start.51
  378.1 9.2 %collective-permute-done.55 = bf16[48,3072]{1,0:T(8,128)(2,1)S(1)} collective-permute-done((bf16[48,3072]{1,0:T(8,128)(2,1)S(1)}, bf16[48,3072]{1,0:T(8,128)(2,1)S(1)}, u32[]{:S(2)}, u32[]{:S(2)}) %collective-permute-start.55) | collective-permute-done | bytes 294944 | tf_op jit(solution)/shard_map/ppermute | solution.py:149
  389.5 2.5 collective-permute-done.56
  392.2 3.7 collective-permute-done.57
  396.1 2.1 collective-permute-start.60
  398.1 2.6 collective-permute-done.58
  401.6 3.0 collective-permute-done.59
  406.8 5.3 %collective-permute-done.61 = bf16[48,1536]{1,0:T(8,128)(2,1)S(1)} collective-permute-done((bf16[48,1536]{1,0:T(8,128)(2,1)S(1)}, bf16[48,1536]{1,0:T(8,128)(2,1)S(1)}, u32[]{:S(2)}, u32[]{:S(2)}) %collective-permute-start.61) | collective-permute-done | bytes 147488 | tf_op jit(solution)/shard_map/ppermute | solution.py:149
  413.5 2.2 convert_select_fusion
  (315 shorter events, 92.6 us)
Async XLA Ops:
  0.6 28.0 %collective-permute-start = (bf16[1024,768]{1,0:T(8,128)(2,1)}, bf16[1024,768]{1,0:T(8,128)(2,1)}, u32[]{:S(2)}, u32[]{:S(2)}) collective-permute-start(bf16[1024,768]{1,0:T(8,128)(2,1)} %param.14), channel_id=1, source_target_pairs={{3,1},{0,2},{7,5},{4,6},{11,9},{8,10},{15,13},{12,14},{19,17},{16,... | collective-permute-start | bytes 4718600 | tf_op jit(solution)/shard_map/ppermute | solution.py:40
  8.9 14.3 %collective-permute-start.2 = (bf16[768,768]{1,0:T(8,128)(2,1)}, bf16[768,768]{1,0:T(8,128)(2,1)}, u32[]{:S(2)}, u32[]{:S(2)}) collective-permute-start(bf16[768,768]{1,0:T(8,128)(2,1)} %dynamic-slice_bitcast_fusion.5), channel_id=1, source_target_pairs={{2,1},{1,2},{6,5},{5,6},{10,9},{9,10},{14,13},{13,14},{18,17},{17,... | collective-permute-start | bytes 3538952 | tf_op jit(solution)/shard_map/ppermute | solution.py:55
  10.7 16.5 %collective-permute-start.1 = (s32[1024]{0:T(1024)S(1)}, s32[1024]{0:T(1024)S(1)}, u32[]{:S(2)}, u32[]{:S(2)}) collective-permute-start(s32[1024]{0:T(1024)S(1)} %copy-done.76), channel_id=1, source_target_pairs={{3,1},{0,2},{7,5},{4,6},{11,9},{8,10},{15,13},{12,14},{19,17},{16,... | collective-permute-start | bytes 12296 | tf_op jit(solution)/shard_map/ppermute | solution.py:40
  17.3 31.2 %collective-permute-start.7 = (bf16[768,768]{1,0:T(8,128)(2,1)S(1)}, bf16[768,768]{1,0:T(8,128)(2,1)}, u32[]{:S(2)}, u32[]{:S(2)}) collective-permute-start(bf16[768,768]{1,0:T(8,128)(2,1)S(1)} %dynamic-slice_bitcast_fusion.2), channel_id=1, source_target_pairs={{2,1},{1,2},{6,5},{5,6},{10,9},{9,10},{14,13},{13,14},{18,17},{17,... | collective-permute-start | bytes 3538952 | tf_op jit(solution)/shard_map/ppermute | solution.py:55
  20.3 28.2 %collective-permute-start.5 = (bf16[384,1536]{1,0:T(8,128)(2,1)}, bf16[384,1536]{1,0:T(8,128)(2,1)}, u32[]{:S(2)}, u32[]{:S(2)}) collective-permute-start(bf16[384,1536]{1,0:T(8,128)(2,1)} %dynamic-slice_bitcast_fusion.4), channel_id=1, source_target_pairs={{2,1},{1,2},{6,5},{5,6},{10,9},{9,10},{14,13},{13,14},{18,17},{17,... | collective-permute-start | bytes 3538952 | tf_op jit(solution)/shard_map/ppermute | solution.py:55
  23.2 25.3 %collective-permute-start.6 = (bf16[768,768]{1,0:T(8,128)(2,1)}, bf16[768,768]{1,0:T(8,128)(2,1)}, u32[]{:S(2)}, u32[]{:S(2)}) collective-permute-start(bf16[768,768]{1,0:T(8,128)(2,1)} %dynamic-slice_bitcast_fusion.3), channel_id=1, source_target_pairs={{2,1},{1,2},{6,5},{5,6},{10,9},{9,10},{14,13},{13,14},{18,17},{17,... | collective-permute-start | bytes 3538952 | tf_op jit(solution)/shard_map/ppermute | solution.py:55
  48.5 22.0 %collective-permute-start.10 = (bf16[768,768]{1,0:T(8,128)(2,1)}, bf16[768,768]{1,0:T(8,128)(2,1)S(1)}, u32[]{:S(2)}, u32[]{:S(2)}) collective-permute-start(bf16[768,768]{1,0:T(8,128)(2,1)} %collective-permute-done.6.refs_4_.refs_11_), channel_id=1, source_target_pairs={{9,1},{10,2},{13,5},{14,6},{1,9},{2,10},{5,13},{6,14},{25,17},{26,... | collective-permute-start | bytes 3538952 | tf_op jit(solution)/shard_map/ppermute | solution.py:67
  49.3 37.0 %collective-permute-start.8 = (bf16[1024,768]{1,0:T(8,128)(2,1)S(1)}, bf16[1024,768]{1,0:T(8,128)(2,1)S(1)}, u32[]{:S(2)}, u32[]{:S(2)}) collective-permute-start(bf16[1024,768]{1,0:T(8,128)(2,1)S(1)} %get-tuple-element.148.own_ref), channel_id=1, source_target_pairs={{2,0},{3,1},{0,2},{1,3},{6,4},{7,5},{4,6},{5,7},{10,8},{11,9},{8,1... | collective-permute-start | bytes 4718600 | tf_op jit(solution)/shard_map/ppermute | solution.py:36
  68.0 33.3 %collective-permute-start.12 = (bf16[384,1536]{1,0:T(8,128)(2,1)S(1)}, bf16[384,1536]{1,0:T(8,128)(2,1)S(1)}, u32[]{:S(2)}, u32[]{:S(2)}) collective-permute-start(bf16[384,1536]{1,0:T(8,128)(2,1)S(1)} %dynamic-slice_bitcast_fusion.1), channel_id=1, source_target_pairs={{2,1},{1,2},{6,5},{5,6},{10,9},{9,10},{14,13},{13,14},{18,17},{17,... | collective-permute-start | bytes 3538952 | tf_op jit(solution)/shard_map/ppermute | solution.py:55
  69.6 31.7 %collective-permute-start.13 = (bf16[768,768]{1,0:T(8,128)(2,1)S(1)}, bf16[768,768]{1,0:T(8,128)(2,1)S(1)}, u32[]{:S(2)}, u32[]{:S(2)}) collective-permute-start(bf16[768,768]{1,0:T(8,128)(2,1)S(1)} %dynamic-slice_bitcast_fusion), channel_id=1, source_target_pairs={{2,1},{1,2},{6,5},{5,6},{10,9},{9,10},{14,13},{13,14},{18,17},{17,... | collective-permute-start | bytes 3538952 | tf_op jit(solution)/shard_map/ppermute | solution.py:55
  70.5 30.8 %collective-permute-start.11 = (bf16[768,768]{1,0:T(8,128)(2,1)}, bf16[768,768]{1,0:T(8,128)(2,1)S(1)}, u32[]{:S(2)}, u32[]{:S(2)}) collective-permute-start(bf16[768,768]{1,0:T(8,128)(2,1)} %collective-permute-done.7.refs_9_.refs_1_), channel_id=1, source_target_pairs={{5,1},{6,2},{1,5},{2,6},{13,9},{14,10},{9,13},{10,14},{21,17},{22,... | collective-permute-start | bytes 3538952 | tf_op jit(solution)/shard_map/ppermute | solution.py:67
  71.3 31.8 %collective-permute-start.17 = (bf16[1024,768]{1,0:T(8,128)(2,1)S(1)}, bf16[1024,768]{1,0:T(8,128)(2,1)S(1)}, u32[]{:S(2)}, u32[]{:S(2)}) collective-permute-start(bf16[1024,768]{1,0:T(8,128)(2,1)S(1)} %copy-done.52), channel_id=1, source_target_pairs={{3,1},{0,2},{7,5},{4,6},{11,9},{8,10},{15,13},{12,14},{19,17},{16,... | collective-permute-start | bytes 4718600 | tf_op jit(solution)/shard_map/ppermute | solution.py:40
  101.4 20.5 %collective-permute-start.15 = (bf16[384,1536]{1,0:T(8,128)(2,1)S(1)}, bf16[384,1536]{1,0:T(8,128)(2,1)S(1)}, u32[]{:S(2)}, u32[]{:S(2)}) collective-permute-start(bf16[384,1536]{1,0:T(8,128)(2,1)S(1)} %collective-permute-done.12.refs_1_.refs_4_), channel_id=1, source_target_pairs={{5,1},{6,2},{1,5},{2,6},{13,9},{14,10},{9,13},{10,14},{21,17},{22,... | collective-permute-start | bytes 3538952 | tf_op jit(solution)/shard_map/ppermute | solution.py:67
  102.3 19.7 %collective-permute-start.16 = (bf16[768,768]{1,0:T(8,128)(2,1)S(1)}, bf16[768,768]{1,0:T(8,128)(2,1)S(1)}, u32[]{:S(2)}, u32[]{:S(2)}) collective-permute-start(bf16[768,768]{1,0:T(8,128)(2,1)S(1)} %collective-permute-done.13.refs_4_.refs_7_), channel_id=1, source_target_pairs={{9,1},{10,2},{13,5},{14,6},{1,9},{2,10},{5,13},{6,14},{25,17},{26,... | collective-permute-start | bytes 3538952 | tf_op jit(solution)/shard_map/ppermute | solution.py:67
  160.4 30.9 %collective-permute-start.21 = (bf16[1024,768]{1,0:T(8,128)(2,1)S(1)}, bf16[1024,768]{1,0:T(8,128)(2,1)S(1)}, u32[]{:S(2)}, u32[]{:S(2)}) collective-permute-start(bf16[1024,768]{1,0:T(8,128)(2,1)S(1)} %add_convert_fusion), channel_id=1, source_target_pairs={{2,1},{1,2},{6,5},{5,6},{10,9},{9,10},{14,13},{13,14},{18,17},{17,... | collective-permute-start | bytes 4718600 | tf_op jit(solution)/shard_map/ppermute | solution.py:81
  172.0 20.8 %collective-permute-start.19 = (bf16[1024,768]{1,0:T(8,128)(2,1)S(1)}, bf16[1024,768]{1,0:T(8,128)(2,1)S(1)}, u32[]{:S(2)}, u32[]{:S(2)}) collective-permute-start(bf16[1024,768]{1,0:T(8,128)(2,1)S(1)} %get-tuple-element.168.own_ref), channel_id=1, source_target_pairs={{2,0},{3,1},{0,2},{1,3},{6,4},{7,5},{4,6},{5,7},{10,8},{11,9},{8,1... | collective-permute-start | bytes 4718600 | tf_op jit(solution)/shard_map/ppermute | solution.py:36
  194.0 30.9 %collective-permute-start.22 = (bf16[384,1536]{1,0:T(8,128)(2,1)}, bf16[384,1536]{1,0:T(8,128)(2,1)}, u32[]{:S(2)}, u32[]{:S(2)}) collective-permute-start(bf16[384,1536]{1,0:T(8,128)(2,1)} %get-tuple-element.184), channel_id=1, source_target_pairs={{1,0},{3,1},{0,2},{2,3},{5,4},{7,5},{4,6},{6,7},{9,8},{11,9},{8,10... | collective-permute-start | bytes 3538952 | tf_op jit(solution)/shard_map/ppermute | solution.py:116
  194.4 30.5 %collective-permute-start.23 = (bf16[384,1536]{1,0:T(8,128)(2,1)}, bf16[384,1536]{1,0:T(8,128)(2,1)}, u32[]{:S(2)}, u32[]{:S(2)}) collective-permute-start(bf16[384,1536]{1,0:T(8,128)(2,1)} %get-tuple-element.185), channel_id=1, source_target_pairs={{2,1},{1,2},{6,5},{5,6},{10,9},{9,10},{14,13},{13,14},{18,17},{17,... | collective-permute-start | bytes 3538952 | tf_op jit(solution)/shard_map/ppermute | solution.py:55
  196.1 28.9 %collective-permute-start.24 = (bf16[384,1536]{1,0:T(8,128)(2,1)}, bf16[384,1536]{1,0:T(8,128)(2,1)}, u32[]{:S(2)}, u32[]{:S(2)}) collective-permute-start(bf16[384,1536]{1,0:T(8,128)(2,1)} %get-tuple-element.186), channel_id=1, source_target_pairs={{0,4},{2,6},{4,0},{6,2},{8,12},{10,14},{12,8},{14,10},{16,20},{18,... | collective-permute-start | bytes 3538952 | tf_op jit(solution)/shard_map/ppermute | solution.py:119
  224.9 25.2 %collective-permute-start.25 = (bf16[1024,768]{1,0:T(8,128)(2,1)}, bf16[1024,768]{1,0:T(8,128)(2,1)S(1)}, u32[]{:S(2)}, u32[]{:S(2)}) collective-permute-start(bf16[1024,768]{1,0:T(8,128)(2,1)} %get-tuple-element.187.refs_1_), channel_id=1, source_target_pairs={{2,0},{3,1},{0,2},{1,3},{6,4},{7,5},{4,6},{5,7},{10,8},{11,9},{8,1... | collective-permute-start | bytes 4718600 | tf_op jit(solution)/shard_map/ppermute | solution.py:36
  229.3 18.1 %collective-permute-start.27 = (bf16[2,2,48,1536]{3,2,1,0:T(8,128)(2,1)}, bf16[2,2,48,1536]{3,2,1,0:T(8,128)(2,1)}, u32[]{:S(2)}, u32[]{:S(2)}) collective-permute-start(bf16[2,2,48,1536]{3,2,1,0:T(8,128)(2,1)} %get-tuple-element.293), channel_id=1, source_target_pairs={{1,0},{3,1},{0,2},{2,3},{5,4},{7,5},{4,6},{6,7},{9,8},{11,9},{8,10... | collective-permute-start | bytes 1769480 | tf_op jit(solution)/shard_map/ppermute | solution.py:116
  229.3 18.1 %collective-permute-start.28 = (bf16[2,2,48,1536]{3,2,1,0:T(8,128)(2,1)}, bf16[2,2,48,1536]{3,2,1,0:T(8,128)(2,1)}, u32[]{:S(2)}, u32[]{:S(2)}) collective-permute-start(bf16[2,2,48,1536]{3,2,1,0:T(8,128)(2,1)} %get-tuple-element.292), channel_id=1, source_target_pairs={{2,1},{1,2},{6,5},{5,6},{10,9},{9,10},{14,13},{13,14},{18,17},{17,... | collective-permute-start | bytes 1769480 | tf_op jit(solution)/shard_map/ppermute | solution.py:55
  235.3 14.9 %collective-permute-start.26 = (bf16[2,2,48,1536]{3,2,1,0:T(8,128)(2,1)}, bf16[2,2,48,1536]{3,2,1,0:T(8,128)(2,1)}, u32[]{:S(2)}, u32[]{:S(2)}) collective-permute-start(bf16[2,2,48,1536]{3,2,1,0:T(8,128)(2,1)} %fusion.2), channel_id=1, source_target_pairs={{0,4},{2,6},{4,0},{6,2},{8,12},{10,14},{12,8},{14,10},{16,20},{18,... | collective-permute-start | bytes 1769480 | tf_op jit(solution)/shard_map/ppermute | solution.py:119
  252.5 18.3 %collective-permute-start.32 = (bf16[2,48,3072]{2,1,0:T(8,128)(2,1)S(1)}, bf16[2,48,3072]{2,1,0:T(8,128)(2,1)S(1)}, u32[]{:S(2)}, u32[]{:S(2)}) collective-permute-start(bf16[2,48,3072]{2,1,0:T(8,128)(2,1)S(1)} %fusion.11), channel_id=1, source_target_pairs={{0,8},{2,10},{4,12},{6,14},{8,0},{10,2},{12,4},{14,6},{16,24},{18,... | collective-permute-start | bytes 1769480 | tf_op jit(solution)/shard_map/ppermute | solution.py:149
  253.1 17.7 %collective-permute-start.29 = (bf16[384,768]{1,0:T(8,128)(2,1)S(1)}, bf16[384,768]{1,0:T(8,128)(2,1)S(1)}, u32[]{:S(2)}, u32[]{:S(2)}) collective-permute-start(bf16[384,768]{1,0:T(8,128)(2,1)S(1)} %get-tuple-element.204), channel_id=1, source_target_pairs={{1,0},{3,1},{0,2},{2,3},{5,4},{7,5},{4,6},{6,7},{9,8},{11,9},{8,10... | collective-permute-start | bytes 1769480 | tf_op jit(solution)/shard_map/ppermute | solution.py:116
  254.3 16.5 %collective-permute-start.30 = (bf16[384,768]{1,0:T(8,128)(2,1)S(1)}, bf16[384,768]{1,0:T(8,128)(2,1)S(1)}, u32[]{:S(2)}, u32[]{:S(2)}) collective-permute-start(bf16[384,768]{1,0:T(8,128)(2,1)S(1)} %get-tuple-element.205), channel_id=1, source_target_pairs={{2,1},{1,2},{6,5},{5,6},{10,9},{9,10},{14,13},{13,14},{18,17},{17,... | collective-permute-start | bytes 1769480 | tf_op jit(solution)/shard_map/ppermute | solution.py:55
  255.0 15.9 %collective-permute-start.31 = (bf16[384,768]{1,0:T(8,128)(2,1)S(1)}, bf16[384,768]{1,0:T(8,128)(2,1)S(1)}, u32[]{:S(2)}, u32[]{:S(2)}) collective-permute-start(bf16[384,768]{1,0:T(8,128)(2,1)S(1)} %get-tuple-element.206), channel_id=1, source_target_pairs={{0,4},{2,6},{4,0},{6,2},{8,12},{10,14},{12,8},{14,10},{16,20},{18,... | collective-permute-start | bytes 1769480 | tf_op jit(solution)/shard_map/ppermute | solution.py:119
  272.5 22.1 %collective-permute-start.33 = (bf16[1024,768]{1,0:T(8,128)(2,1)}, bf16[1024,768]{1,0:T(8,128)(2,1)}, u32[]{:S(2)}, u32[]{:S(2)}) collective-permute-start(bf16[1024,768]{1,0:T(8,128)(2,1)} %get-tuple-element.210.own_ref), channel_id=1, source_target_pairs={{2,0},{3,1},{0,2},{1,3},{6,4},{7,5},{4,6},{5,7},{10,8},{11,9},{8,1... | collective-permute-start | bytes 4718600 | tf_op jit(solution)/shard_map/ppermute | solution.py:36
  275.7 18.8 %collective-permute-start.37 = (bf16[48,3072]{1,0:T(8,128)(2,1)S(1)}, bf16[48,3072]{1,0:T(8,128)(2,1)S(1)}, u32[]{:S(2)}, u32[]{:S(2)}) collective-permute-start(bf16[48,3072]{1,0:T(8,128)(2,1)S(1)} %fusion.15), channel_id=1, source_target_pairs={{0,16},{2,18},{4,20},{6,22},{8,24},{10,26},{12,28},{14,30},{16,0},... | collective-permute-start | bytes 884744 | tf_op jit(solution)/shard_map/ppermute | solution.py:149
  279.7 14.8 %collective-permute-start.35 = (bf16[2,2,48,768]{3,2,1,0:T(8,128)(2,1)S(1)}, bf16[2,2,48,768]{3,2,1,0:T(8,128)(2,1)S(1)}, u32[]{:S(2)}, u32[]{:S(2)}) collective-permute-start(bf16[2,2,48,768]{3,2,1,0:T(8,128)(2,1)S(1)} %get-tuple-element.297), channel_id=1, source_target_pairs={{1,0},{3,1},{0,2},{2,3},{5,4},{7,5},{4,6},{6,7},{9,8},{11,9},{8,10... | collective-permute-start | bytes 884744 | tf_op jit(solution)/shard_map/ppermute | solution.py:116
  279.8 14.8 %collective-permute-start.36 = (bf16[2,2,48,768]{3,2,1,0:T(8,128)(2,1)S(1)}, bf16[2,2,48,768]{3,2,1,0:T(8,128)(2,1)S(1)}, u32[]{:S(2)}, u32[]{:S(2)}) collective-permute-start(bf16[2,2,48,768]{3,2,1,0:T(8,128)(2,1)S(1)} %get-tuple-element.296), channel_id=1, source_target_pairs={{2,1},{1,2},{6,5},{5,6},{10,9},{9,10},{14,13},{13,14},{18,17},{17,... | collective-permute-start | bytes 884744 | tf_op jit(solution)/shard_map/ppermute | solution.py:55
  295.3 31.4 %collective-permute-start.39 = (bf16[384,1536]{1,0:T(8,128)(2,1)S(1)}, bf16[384,1536]{1,0:T(8,128)(2,1)S(1)}, u32[]{:S(2)}, u32[]{:S(2)}) collective-permute-start(bf16[384,1536]{1,0:T(8,128)(2,1)S(1)} %get-tuple-element.232), channel_id=1, source_target_pairs={{1,0},{3,1},{0,2},{2,3},{5,4},{7,5},{4,6},{6,7},{9,8},{11,9},{8,10... | collective-permute-start | bytes 3538952 | tf_op jit(solution)/shard_map/ppermute | solution.py:116
  299.4 27.3 %collective-permute-start.40 = (bf16[384,1536]{1,0:T(8,128)(2,1)S(1)}, bf16[384,1536]{1,0:T(8,128)(2,1)S(1)}, u32[]{:S(2)}, u32[]{:S(2)}) collective-permute-start(bf16[384,1536]{1,0:T(8,128)(2,1)S(1)} %get-tuple-element.233), channel_id=1, source_target_pairs={{2,1},{1,2},{6,5},{5,6},{10,9},{9,10},{14,13},{13,14},{18,17},{17,... | collective-permute-start | bytes 3538952 | tf_op jit(solution)/shard_map/ppermute | solution.py:55
  300.1 27.8 %collective-permute-start.41 = (bf16[384,1536]{1,0:T(8,128)(2,1)S(1)}, bf16[384,1536]{1,0:T(8,128)(2,1)S(1)}, u32[]{:S(2)}, u32[]{:S(2)}) collective-permute-start(bf16[384,1536]{1,0:T(8,128)(2,1)S(1)} %get-tuple-element.234), channel_id=1, source_target_pairs={{0,4},{2,6},{4,0},{6,2},{8,12},{10,14},{12,8},{14,10},{16,20},{18,... | collective-permute-start | bytes 3538952 | tf_op jit(solution)/shard_map/ppermute | solution.py:119
  302.0 24.6 %collective-permute-start.38 = (bf16[2,48,1536]{2,1,0:T(8,128)(2,1)S(1)}, bf16[2,48,1536]{2,1,0:T(8,128)(2,1)S(1)}, u32[]{:S(2)}, u32[]{:S(2)}) collective-permute-start(bf16[2,48,1536]{2,1,0:T(8,128)(2,1)S(1)} %fusion.27), channel_id=1, source_target_pairs={{0,8},{2,10},{4,12},{6,14},{8,0},{10,2},{12,4},{14,6},{16,24},{18,... | collective-permute-start | bytes 884744 | tf_op jit(solution)/shard_map/ppermute | solution.py:149
  327.9 21.0 %collective-permute-start.42 = (bf16[1024,768]{1,0:T(8,128)(2,1)S(1)}, bf16[1024,768]{1,0:T(8,128)(2,1)}, u32[]{:S(2)}, u32[]{:S(2)}) collective-permute-start(bf16[1024,768]{1,0:T(8,128)(2,1)S(1)} %get-tuple-element.235.own_ref), channel_id=1, source_target_pairs={{2,0},{3,1},{0,2},{1,3},{6,4},{7,5},{4,6},{5,7},{10,8},{11,9},{8,1... | collective-permute-start | bytes 4718600 | tf_op jit(solution)/shard_map/ppermute | solution.py:36
  330.2 17.4 %collective-permute-start.44 = (bf16[2,2,48,1536]{3,2,1,0:T(8,128)(2,1)}, bf16[2,2,48,1536]{3,2,1,0:T(8,128)(2,1)}, u32[]{:S(2)}, u32[]{:S(2)}) collective-permute-start(bf16[2,2,48,1536]{3,2,1,0:T(8,128)(2,1)} %get-tuple-element.291), channel_id=1, source_target_pairs={{1,0},{3,1},{0,2},{2,3},{5,4},{7,5},{4,6},{6,7},{9,8},{11,9},{8,10... | collective-permute-start | bytes 1769480 | tf_op jit(solution)/shard_map/ppermute | solution.py:116
  330.3 17.3 %collective-permute-start.45 = (bf16[2,2,48,1536]{3,2,1,0:T(8,128)(2,1)}, bf16[2,2,48,1536]{3,2,1,0:T(8,128)(2,1)}, u32[]{:S(2)}, u32[]{:S(2)}) collective-permute-start(bf16[2,2,48,1536]{3,2,1,0:T(8,128)(2,1)} %get-tuple-element.290), channel_id=1, source_target_pairs={{2,1},{1,2},{6,5},{5,6},{10,9},{9,10},{14,13},{13,14},{18,17},{17,... | collective-permute-start | bytes 1769480 | tf_op jit(solution)/shard_map/ppermute | solution.py:55
  333.9 15.0 %collective-permute-start.43 = (bf16[2,2,48,1536]{3,2,1,0:T(8,128)(2,1)}, bf16[2,2,48,1536]{3,2,1,0:T(8,128)(2,1)}, u32[]{:S(2)}, u32[]{:S(2)}) collective-permute-start(bf16[2,2,48,1536]{3,2,1,0:T(8,128)(2,1)} %fusion.5), channel_id=1, source_target_pairs={{0,4},{2,6},{4,0},{6,2},{8,12},{10,14},{12,8},{14,10},{16,20},{18,... | collective-permute-start | bytes 1769480 | tf_op jit(solution)/shard_map/ppermute | solution.py:119
  351.9 16.0 %collective-permute-start.50 = (bf16[2,48,3072]{2,1,0:T(8,128)(2,1)S(1)}, bf16[2,48,3072]{2,1,0:T(8,128)(2,1)S(1)}, u32[]{:S(2)}, u32[]{:S(2)}) collective-permute-start(bf16[2,48,3072]{2,1,0:T(8,128)(2,1)S(1)} %fusion.9), channel_id=1, source_target_pairs={{0,8},{2,10},{4,12},{6,14},{8,0},{10,2},{12,4},{14,6},{16,24},{18,... | collective-permute-start | bytes 1769480 | tf_op jit(solution)/shard_map/ppermute | solution.py:149
  353.2 14.7 %collective-permute-start.47 = (bf16[384,768]{1,0:T(8,128)(2,1)S(1)}, bf16[384,768]{1,0:T(8,128)(2,1)S(1)}, u32[]{:S(2)}, u32[]{:S(2)}) collective-permute-start(bf16[384,768]{1,0:T(8,128)(2,1)S(1)} %get-tuple-element.252), channel_id=1, source_target_pairs={{1,0},{3,1},{0,2},{2,3},{5,4},{7,5},{4,6},{6,7},{9,8},{11,9},{8,10... | collective-permute-start | bytes 1769480 | tf_op jit(solution)/shard_map/ppermute | solution.py:116
  354.4 13.5 %collective-permute-start.48 = (bf16[384,768]{1,0:T(8,128)(2,1)S(1)}, bf16[384,768]{1,0:T(8,128)(2,1)S(1)}, u32[]{:S(2)}, u32[]{:S(2)}) collective-permute-start(bf16[384,768]{1,0:T(8,128)(2,1)S(1)} %get-tuple-element.253), channel_id=1, source_target_pairs={{2,1},{1,2},{6,5},{5,6},{10,9},{9,10},{14,13},{13,14},{18,17},{17,... | collective-permute-start | bytes 1769480 | tf_op jit(solution)/shard_map/ppermute | solution.py:55
  355.1 15.1 %collective-permute-start.49 = (bf16[384,768]{1,0:T(8,128)(2,1)S(1)}, bf16[384,768]{1,0:T(8,128)(2,1)S(1)}, u32[]{:S(2)}, u32[]{:S(2)}) collective-permute-start(bf16[384,768]{1,0:T(8,128)(2,1)S(1)} %get-tuple-element.254), channel_id=1, source_target_pairs={{0,4},{2,6},{4,0},{6,2},{8,12},{10,14},{12,8},{14,10},{16,20},{18,... | collective-permute-start | bytes 1769480 | tf_op jit(solution)/shard_map/ppermute | solution.py:119
  370.3 17.0 %collective-permute-start.55 = (bf16[48,3072]{1,0:T(8,128)(2,1)S(1)}, bf16[48,3072]{1,0:T(8,128)(2,1)S(1)}, u32[]{:S(2)}, u32[]{:S(2)}) collective-permute-start(bf16[48,3072]{1,0:T(8,128)(2,1)S(1)} %fusion.14), channel_id=1, source_target_pairs={{0,16},{2,18},{4,20},{6,22},{8,24},{10,26},{12,28},{14,30},{16,0},... | collective-permute-start | bytes 884744 | tf_op jit(solution)/shard_map/ppermute | solution.py:149
  371.1 16.2 %collective-permute-start.53 = (bf16[2,2,48,768]{3,2,1,0:T(8,128)(2,1)S(1)}, bf16[2,2,48,768]{3,2,1,0:T(8,128)(2,1)S(1)}, u32[]{:S(2)}, u32[]{:S(2)}) collective-permute-start(bf16[2,2,48,768]{3,2,1,0:T(8,128)(2,1)S(1)} %get-tuple-element.295), channel_id=1, source_target_pairs={{1,0},{3,1},{0,2},{2,3},{5,4},{7,5},{4,6},{6,7},{9,8},{11,9},{8,10... | collective-permute-start | bytes 884744 | tf_op jit(solution)/shard_map/ppermute | solution.py:116
  372.3 15.0 %collective-permute-start.54 = (bf16[2,2,48,768]{3,2,1,0:T(8,128)(2,1)S(1)}, bf16[2,2,48,768]{3,2,1,0:T(8,128)(2,1)S(1)}, u32[]{:S(2)}, u32[]{:S(2)}) collective-permute-start(bf16[2,2,48,768]{3,2,1,0:T(8,128)(2,1)S(1)} %get-tuple-element.294), channel_id=1, source_target_pairs={{2,1},{1,2},{6,5},{5,6},{10,9},{9,10},{14,13},{13,14},{18,17},{17,... | collective-permute-start | bytes 884744 | tf_op jit(solution)/shard_map/ppermute | solution.py:55
  373.3 14.0 %collective-permute-start.52 = (bf16[2,2,48,768]{3,2,1,0:T(8,128)(2,1)S(1)}, bf16[2,2,48,768]{3,2,1,0:T(8,128)(2,1)S(1)}, u32[]{:S(2)}, u32[]{:S(2)}) collective-permute-start(bf16[2,2,48,768]{3,2,1,0:T(8,128)(2,1)S(1)} %fusion.21), channel_id=1, source_target_pairs={{0,4},{2,6},{4,0},{6,2},{8,12},{10,14},{12,8},{14,10},{16,20},{18,... | collective-permute-start | bytes 884744 | tf_op jit(solution)/shard_map/ppermute | solution.py:119
  376.3 37.2 %collective-permute-start.51 = (bf16[1024,768]{1,0:T(8,128)(2,1)S(1)}, bf16[1024,768]{1,0:T(8,128)(2,1)}, u32[]{:S(2)}, u32[]{:S(2)}) collective-permute-start(bf16[1024,768]{1,0:T(8,128)(2,1)S(1)} %get-tuple-element.258), channel_id=1, source_target_pairs={{2,1},{1,2},{6,5},{5,6},{10,9},{9,10},{14,13},{13,14},{18,17},{17,... | collective-permute-start | bytes 4718600 | tf_op jit(solution)/shard_map/ppermute | solution.py:81
  (92 other events, 512.8 us)
